TPU v7x, 512 devices: a whole 4x4x16 slice. The times are simulated.
512 devices in a mesh: tm: 32 (over x, z_lo), dp: 16 (over y, z_hi, core).
Axes of the slice: x: 4, y: 4, z: 16 (z_hi: 2, z_lo: 8; z = z_hi * 8 + z_lo), core: 2. Of those that a mesh axis runs over, the one named last changes fastest.
Arguments:
- video_tokens: float32 [16, 32, 256, 512], P('dp', 'tm'), may hold values from -24 to 24
- actions: int32 [16, 32], P('dp', 'tm'), may hold values from 0 to 127
- frame_times: int32 [16, 32], P('dp'), may hold values from 0 to 93, as said below
- act_table: float32 [128, 512], replicated, may hold values from -3 to 3
- norm_gain: float32 [512], replicated, may hold values from 0.5 to 1.5
- w_qkv: float32 [512, 1536], P('dp'), may hold values from -12 to 12
- w_out: float32 [512, 512], P('dp'), may hold values from -0.25 to 0.25
- slopes: float32 [8], replicated, may hold values from 0.02 to 1
- out_grad: float32 [16, 32, 256, 512], P('dp', 'tm'), may hold values from -6 to 6
Outputs:
- grad_tokens: float32 [16, 32, 256, 512], P('dp', 'tm')
- grad_qkv: float32 [512, 1536], P('dp')
- grad_out: float32 [512, 512], P('dp')
- grad_table: float32 [128, 512], replicated
- grad_gain: float32 [512], replicated
Inputs may be any that keep to these rules, and one draw needn't show every extreme that they name: `frame_times`: along each clip's 32 frames the times start at 0 and rise by 1 to 3 from one frame to the next; in some clip every rise is 3.
All inputs are finite; a program needn't handle non-finite values.
Results may differ from a plain program's by a relative error of at most 0.0003.
Values sent between devices are 32-bit elements; how exact they have to be, the bound alone decides.
No kernel may reach another device: no remote copies, remote signals or barrier semaphores. Data moves between devices by JAX's collectives and lax.ppermute only.
A program may use at most 64 MiB of HBM per device.

v0:
```python
import math

import jax
import jax.numpy as jnp
from jax import lax
from jax.sharding import PartitionSpec as P

HEADS = 8


precise = lax.Precision.HIGHEST


def attend(qkv_rows, frame_times, slopes, head_count):
    clip_count, frames, patches, triple = qkv_rows.shape
    features = triple // 3
    head_size = features // head_count
    pieces = qkv_rows.reshape(clip_count, frames, patches, 3, head_count, head_size)
    scores = jnp.einsum(
        "cipnd,cjpnd->cpnij", pieces[:, :, :, 0], pieces[:, :, :, 1], precision=precise
    ) / math.sqrt(head_size)
    spacing = (frame_times[:, :, None] - frame_times[:, None, :]).astype(jnp.float32)
    scores = scores - slopes[None, None, :, None, None] * spacing[:, None, None, :, :]
    causal = lax.broadcasted_iota(jnp.int32, (frames, frames), 0) >= lax.broadcasted_iota(
        jnp.int32, (frames, frames), 1
    )
    scores = jnp.where(causal, scores, -jnp.inf)
    row_peak = lax.stop_gradient(jnp.max(scores, axis=-1, keepdims=True))
    raised = jnp.exp(scores - row_peak)
    weights = raised / jnp.sum(raised, axis=-1, keepdims=True)
    mixed_rows = jnp.einsum("cpnij,cjpnd->cipnd", weights, pieces[:, :, :, 2], precision=precise)
    return mixed_rows.reshape(clip_count, frames, patches, features)


def rms_scale(embedded, norm_gain):
    return (
        embedded
        * norm_gain
        * lax.rsqrt(jnp.mean(embedded * embedded, axis=-1, keepdims=True) + 1e-06)
    )


def project(token_rows, matrix):
    return jnp.einsum("cfpd,de->cfpe", token_rows, matrix, precision=precise)


def shards(
    video_tokens, actions, frame_times, act_table, norm_gain, w_qkv, w_out, slopes, out_grad
):
    full_qkv, full_out = (
        lax.all_gather(w_qkv, "dp", axis=0, tiled=True),
        lax.all_gather(w_out, "dp", axis=0, tiled=True),
    )
    lookup = (actions[..., None] == lax.iota(jnp.int32, act_table.shape[0])).astype(jnp.float32)
    embedded = (
        video_tokens
        + jnp.einsum("cfa,ad->cfd", lookup, act_table, precision=precise)[:, :, None, :]
    )

    def attend_here(qkv_rows):
        return attend(qkv_rows, frame_times, slopes, HEADS)

    def front_part(token_rows, gain, matrix):
        return project(rms_scale(token_rows, gain), matrix)

    qkv_local, front_pull = jax.vjp(front_part, embedded, norm_gain, full_qkv)
    qkv_patch = lax.all_to_all(qkv_local, "tm", split_axis=2, concat_axis=1, tiled=True)
    mixed_patch, attend_pull = jax.vjp(attend_here, qkv_patch)
    mixed_rows = lax.all_to_all(mixed_patch, "tm", split_axis=1, concat_axis=2, tiled=True)
    grad_out = jnp.einsum("cfpd,cfpe->de", mixed_rows, out_grad, precision=precise)
    grad_mixed = jnp.einsum("cfpe,de->cfpd", out_grad, full_out, precision=precise)
    grad_patch = lax.all_to_all(grad_mixed, "tm", split_axis=2, concat_axis=1, tiled=True)
    (grad_rows_patch,) = attend_pull(grad_patch)
    grad_rows = lax.all_to_all(grad_rows_patch, "tm", split_axis=1, concat_axis=2, tiled=True)
    grad_embedded, grad_gain, grad_qkv = front_pull(grad_rows)
    grad_tokens = out_grad + grad_embedded
    grad_table = jnp.einsum("cfa,cfd->ad", lookup, jnp.sum(grad_tokens, axis=2), precision=precise)
    qkv_share, out_share = (
        lax.psum_scatter(grad_qkv, "dp", scatter_dimension=0, tiled=True),
        lax.psum_scatter(grad_out, "dp", scatter_dimension=0, tiled=True),
    )
    qkv_share, out_share = lax.psum((qkv_share, out_share), "tm")
    grad_table, grad_gain = lax.psum((grad_table, grad_gain), ("tm", "dp"))
    return (grad_tokens, qkv_share, out_share, grad_table, grad_gain)


def solution(mesh):
    return jax.shard_map(
        shards,
        mesh=mesh,
        in_specs=(
            P("dp", "tm", None, None),
            P("dp", "tm"),
            P("dp", None),
            P(),
            P(),
            P("dp", None),
            P("dp", None),
            P(),
            P("dp", "tm", None, None),
        ),
        out_specs=(P("dp", "tm", None, None), P("dp", None), P("dp", None), P(), P()),
        check_vma=False,
    )
```

profile of v0, /device:TPU:25, one launch (start us, length us, event | category | flops | bytes accessed | tf_op | source)
XLA Modules:
  0.0 1461.0 jit_solution(4635568051918682978)
XLA Ops:
  10.0 112.3 %all-gather.5.cloned.1.call-done = f32[512,1536]{1,0:T(8,128)} async-done(((f32[32,1536]{1,0:T(8,128)}), f32[512,1536]{1,0:T(8,128)}) %all-gather.5.cloned.1.call-update) | async-done | bytes 3145744 | tf_op jit(solution)/shard_map/all_gather | solution.py:51
  122.3 4.9 convolution_bitcast_fusion
  127.1 2.8 copy.38
  129.9 5.4 all-to-all-start.1
  136.1 96.3 %all-gather.3.cloned.1.call-done = f32[512,512]{1,0:T(8,128)} async-done(((f32[32,512]{1,0:T(8,128)}), f32[512,512]{1,0:T(8,128)}) %all-gather.3.cloned.1.call-update) | async-done | bytes 1048592 | tf_op jit(solution)/shard_map/all_gather | solution.py:52
  232.4 2.3 convolution_bitcast_fusion.5
  236.0 9.9 all-to-all-start
  246.1 5.3 reduce.11
  251.3 2.4 reshape.253
  254.2 3.0 fusion.45
  257.9 2.4 convolution_bitcast_fusion.1
  262.0 13.2 all-to-all-done
  275.3 5.6 all-to-all-start.3
  280.9 3.1 reduce.10
  285.3 3.1 multiply_reduce_fusion
  288.4 1.7 convolution_bitcast_fusion.4
  290.2 2.5 convolution_bitcast_fusion.2
  292.7 1.9 convolution_bitcast_fusion.3
  295.1 2.0 copy.43
  297.2 1.7 reshape.257
  298.9 11.1 all-to-all-done.3
  310.0 5.6 all-to-all-start.2
  315.7 3.1 fusion.14
  318.8 79.5 %all-to-all-done.2 = f32[1,32,8,1536]{3,2,0,1:T(8,128)S(1)} async-done(((f32[1,32,8,1536]{3,2,0,1:T(8,128)}), f32[1,32,8,1536]{3,2,0,1:T(8,128)S(1)}, u32[]{:S(2)}, u32[]{:S(2)}) %all-to-all-start.2) | async-done | bytes 1572896 | tf_op jit(solution)/shard_map/all_to_all | solution.py:74
  398.3 4.5 fusion
  402.8 4.8 fusion.13
  409.6 20.8 %reduce-scatter.5.cloned.1.call-done = f32[32,512]{1,0:T(8,128)} async-done(((f32[512,512]{1,0:T(8,128)}), f32[32,512]{1,0:T(8,128)}) %reduce-scatter.5.cloned.1.call-update) | async-done | bytes 65552 | tf_op jit(solution)/shard_map/reduce_scatter | solution.py:80
  430.4 134.3 %reduce-scatter.3.cloned.1.call-done = f32[32,1536]{1,0:T(8,128)} async-done(((f32[512,1536]{1,0:T(8,128)}), f32[32,1536]{1,0:T(8,128)}) %reduce-scatter.3.cloned.1.call-update) | async-done | bytes 196624 | tf_op jit(solution)/shard_map/reduce_scatter | solution.py:79
  564.6 101.2 %psum.31 = f32[512]{0:T(512)} all-reduce(f32[512]{0:T(512)S(1)} %get-tuple-element.5), channel_id=1, replica_groups=mesh['tm'=32,'dp'=16] {'tm','dp'}, use_global_device_ids=true, to_apply=%region_12.13 | all-reduce | flops 512 | bytes 4096 | tf_op jit(solution)/shard_map/psum | solution.py:83
  665.8 354.8 %all-reduce.7.cloned.1.call-done = f32[128,512]{1,0:T(8,128)} async-done(((f32[128,512]{1,0:T(8,128)}), f32[128,512]{1,0:T(8,128)}) %all-reduce.7.cloned.1.call-update) | async-done | bytes 262160 | tf_op jit(solution)/shard_map/psum | solution.py:83
  1020.6 428.6 %all-reduce.9.cloned.1.call-done = (f32[32,1536]{1,0:T(8,128)}, f32[32,512]{1,0:T(8,128)}) async-done(((f32[32,1536]{1,0:T(8,128)}, f32[32,512]{1,0:T(8,128)}), (f32[32,1536]{1,0:T(8,128)}, f32[32,512]{1,0:T(8,128)})) %all-reduce.9.cloned.1.call-update) | async-done | bytes 262160 | tf_op jit(solution)/shard_map/psum | solution.py:82
  1452.2 1.7 copy.84
  (64 shorter events, 14.1 us)
Async XLA Ops:
  7.2 1.4 copy-start
  7.2 115.1 %all-gather.5.cloned.1.call-start = ((), (), s32[]{:S(2)}) async-start(), calls=%async_computation.7 | async-start | bytes 3342336 | tf_op jit(solution)/shard_map/all_gather | solution.py:51
  127.1 105.2 %copy-start.2 = (f32[1,1,256,512]{3,2,1,0:T(8,128)S(1)}, f32[1,1,256,512]{3,2,1,0:T(8,128)}, u32[]{:S(2)}) copy-start(f32[1,1,256,512]{3,2,1,0:T(8,128)} %param.17) | copy-start | bytes 1572868
  129.9 116.0 %copy-start.13 = (s32[1,32]{1,0:T(1,128)S(1)}, s32[1,32]{1,0:T(1,128)}, u32[]{:S(2)}) copy-start(s32[1,32]{1,0:T(1,128)} %param.11) | copy-start | bytes 388
  129.9 116.1 %copy-start.14 = (f32[8]{0:T(128)S(1)}, f32[8]{0:T(128)}, u32[]{:S(2)}) copy-start(f32[8]{0:T(128)} %param.16) | copy-start | bytes 100
  129.9 106.1 %all-to-all-start.1 = ((f32[1,1,256,1536]{3,1,0,2:T(1,128)}), f32[1,1,256,1536]{3,1,0,2:T(1,128)S(1)}, u32[]{:S(2)}, u32[]{:S(2)}) async-start(f32[1,1,256,1536]{3,1,0,2:T(1,128)} %copy.38), calls=%async_computation.1 | async-start | bytes 3145728 | tf_op jit(solution)/shard_map/all_to_all | solution.py:67
  135.3 97.0 %all-gather.3.cloned.1.call-start = ((), (), s32[]{:S(2)}) async-start(), calls=%async_computation.6 | async-start | bytes 1114112 | tf_op jit(solution)/shard_map/all_gather | solution.py:52
  236.0 39.3 %all-to-all-start = ((f32[1,1,256,512]{3,1,0,2:T(1,128)}), f32[1,1,256,512]{3,1,0,2:T(1,128)}, u32[]{:S(2)}, u32[]{:S(2)}) async-start(f32[1,1,256,512]{3,1,0,2:T(1,128)} %copy.36), calls=%async_computation | async-start | bytes 1048576 | tf_op jit(solution)/shard_map/all_to_all | solution.py:72
  254.2 6.1 copy-start.4
  254.2 6.1 copy-start.6
  254.2 6.1 copy-start.8
  257.3 0.6 copy-start.10
  260.9 24.3 %copy-start.9 = (f32[1,32,8,1,8,64]{5,4,3,2,1,0:T(8,128)S(1)}, f32[1,32,8,1,8,64]{5,4,3,2,1,0:T(8,128)}, u32[]{:S(2)}) copy-start(f32[1,32,8,1,8,64]{5,4,3,2,1,0:T(8,128)} %copy-done.8) | copy-start | bytes 1572868
  261.0 24.3 %copy-start.11 = (f32[8,8,32]{2,1,0:T(8,128)S(1)}, f32[8,8,32]{2,1,0:T(8,128)}, u32[]{:S(2)}) copy-start(f32[8,8,32]{2,1,0:T(8,128)} %copy-done.10) | copy-start | bytes 24580
  275.3 34.8 %all-to-all-start.3 = ((f32[1,32,8,512]{3,2,0,1:T(8,128)}), f32[1,32,8,512]{3,2,0,1:T(8,128)}, u32[]{:S(2)}, u32[]{:S(2)}) async-start(f32[1,32,8,512]{3,2,0,1:T(8,128)} %bitcast.105), calls=%async_computation.4 | async-start | bytes 1048576 | tf_op jit(solution)/shard_map/all_to_all | solution.py:69
  288.4 1.8 copy-start.7
  290.1 2.5 copy-start.5
  298.9 16.8 %copy-start.3 = (f32[1,1,256,512]{3,2,1,0:T(8,128)S(1)}, f32[1,1,256,512]{3,2,1,0:T(8,128)}, u32[]{:S(2)}) copy-start(f32[1,1,256,512]{3,2,1,0:T(8,128)} %param.17) | copy-start | bytes 1572868
  310.0 88.3 %copy-start.1 = (f32[1,1,256,512]{3,2,1,0:T(8,128)S(1)}, f32[1,1,256,512]{3,2,1,0:T(8,128)}, u32[]{:S(2)}) copy-start(f32[1,1,256,512]{3,2,1,0:T(8,128)} %param.9) | copy-start | bytes 1572868
  310.0 88.3 %copy-start.12 = (f32[512]{0:T(512)S(1)}, f32[512]{0:T(512)}, u32[]{:S(2)}) copy-start(f32[512]{0:T(512)} %param.13) | copy-start | bytes 6148
  310.0 88.3 %all-to-all-start.2 = ((f32[1,32,8,1536]{3,2,0,1:T(8,128)}), f32[1,32,8,1536]{3,2,0,1:T(8,128)S(1)}, u32[]{:S(2)}, u32[]{:S(2)}) async-start(f32[1,32,8,1536]{3,2,0,1:T(8,128)} %bitcast.104), calls=%async_computation.2 | async-start | bytes 3145728 | tf_op jit(solution)/shard_map/all_to_all | solution.py:74
  315.6 114.8 %reduce-scatter.5.cloned.1.call-start = ((), (), s32[]{:S(2)}) async-start(), calls=%async_computation.9 | async-start | bytes 1114112 | tf_op jit(solution)/shard_map/reduce_scatter | solution.py:80
  318.7 245.9 %reduce-scatter.3.cloned.1.call-start = ((), (), s32[]{:S(2)}) async-start(), calls=%async_computation.8 | async-start | bytes 3342336 | tf_op jit(solution)/shard_map/reduce_scatter | solution.py:79
  402.8 617.8 %all-reduce.7.cloned.1.call-start = ((), (), s32[]{:S(2)}) async-start(), calls=%async_computation.10 | async-start | bytes 524288 | tf_op jit(solution)/shard_map/psum | solution.py:83
  409.5 1039.6 %all-reduce.9.cloned.1.call-start = ((), (), s32[]{:S(2)}) async-start(), calls=%async_computation.11 | async-start | bytes 524288 | tf_op jit(solution)/shard_map/psum | solution.py:82
Sparse Core Ops, SparseCore 0:
  11.3 110.9 all-gather.4
  139.4 92.8 all-gather.2
  321.1 109.1 reduce-scatter.4
  435.9 128.7 reduce-scatter.2
  571.4 449.1 all-reduce.6
  1023.4 425.7 all-reduce.8
where the time goes:
time: 1490 us; the launch traced here: 1460 us
  waiting for transfers between devices  1250 us (84%)
  blocking collectives  101 us (7%)
  matrix products  34.4 us (2%)
  starting transfers between devices  26.7 us (2%)
  local copies, waits for them, and re-layouts  18.8 us (1%)
  between operations  15.3 us (1%)
    psum x1, waiting for transfers between devices, shards(): qkv_share, out_share = lax.psum((qkv_share, out_share), 'tm')  429 us
    psum x1, waiting for transfers between devices, shards(): grad_table, grad_gain = lax.psum((grad_table, grad_gain), ('tm', 'dp'))  355 us
    reduce_scatter x1, waiting for transfers between devices, shards(): lax.psum_scatter(grad_qkv, 'dp', scatter_dimension=0, tiled=True)  134 us
    all_gather x1, waiting for transfers between devices, shards(): lax.all_gather(w_qkv, 'dp', axis=0, tiled=True)  112 us
    psum x1, blocking collectives, shards(): grad_table, grad_gain = lax.psum((grad_table, grad_gain), ('tm', 'dp'))  101 us
    all_gather x1, waiting for transfers between devices, shards(): lax.all_gather(w_out, 'dp', axis=0, tiled=True)  96.3 us
    all_to_all x1, waiting for transfers between devices, shards(): lax.all_to_all(grad_rows_patch, 'tm', split_axis=1, concat_axis=2, tiled=...  79.5 us
  transfers between devices with their start and end apart: 10, of which 9 were waited for; matrix products, arithmetic and copies ran while one was open for 4% of the time, Pallas kernels for 0%

commit v1 on v0

v1 whole, which is shorter than its diff:
```python
import functools

import jax
import jax.numpy as jnp
from jax import lax
from jax.experimental import pallas as pl
from jax.experimental.pallas import tpu as pltpu
from jax.sharding import PartitionSpec as P

NX, NZL, NY, NZH, NC = 4, 8, 4, 2, 2
D, QKV, HEADS, HEAD, FRAMES, OWN = 512, 1536, 8, 64, 32, 8
ROWS = FRAMES * OWN
HALF = ROWS // 2
PAIR = 2 * HEAD
ACTIONS = 128
TILES = 35
f32, bf16 = jnp.float32, jnp.bfloat16
BOTH = ("tm", "dp")


def tm_of(x, zl):
    return x * NZL + zl


def dp_of(y, zh, c):
    return (y * NZH + zh) * NC + c


def flat_of(x, zl, y, zh, c):
    return tm_of(x, zl) * (NY * NZH * NC) + dp_of(y, zh, c)


XS, ZLS, YS, ZHS, CS = range(NX), range(NZL), range(NY), range(NZH), range(NC)
X_GROUPS = [[tm_of(x, zl) for x in XS] for zl in ZLS]
ZL_GROUPS = [[tm_of(x, zl) for zl in ZLS] for x in XS]
XY_GROUPS = [
    [flat_of(x, zl, y, zh, c) for x in XS for y in YS] for zl in ZLS for zh in ZHS for c in CS
]
Z_GROUPS = [
    [flat_of(x, zl, y, zh, c) for zh in ZHS for zl in ZLS] for x in XS for y in YS for c in CS
]
SWAP_CORE = [(dp_of(y, zh, c), dp_of(y, zh, 1 - c)) for y in YS for zh in ZHS for c in CS]
SWAP_ZH = [(dp_of(y, zh, c), dp_of(y, 1 - zh, c)) for y in YS for zh in ZHS for c in CS]


def turn_y(step):
    return [(dp_of(y, zh, c), dp_of((y + step) % NY, zh, c)) for y in YS for zh in ZHS for c in CS]


def turn_x(step):
    return [(tm_of(x, zl), tm_of((x + step) % NX, zl)) for x in XS for zl in ZLS]


def exchange(value, axis, groups=None):
    return lax.all_to_all(value, axis, 0, 0, axis_index_groups=groups, tiled=True)


def split(value):
    high = value.astype(bf16)
    return high, (value - high.astype(f32)).astype(bf16)


NN = (((1,), (0,)), ((), ()))
NT = (((1,), (1,)), ((), ()))


def dot(a, b, dims=NN):
    return lax.dot_general(a, b, dims, preferred_element_type=f32)


def dot3(a, b, dims=NN):
    return dot(a[0], b[0], dims) + (dot(a[0], b[1], dims) + dot(a[1], b[0], dims))


def weights_kernel(place, own, own_other, far, far_other, high, low, held):
    x, y, zh, c = place[0], place[1], place[2], place[3]
    for step in range(NY):
        base = lax.rem(y - step + NY, NY) * (D // NY)
        part = pl.ds(step * 32, 32)
        near = base + zh * 64
        held[pl.ds(pl.multiple_of(near + c * 32, 32), 32), :] = own[part, :]
        held[pl.ds(pl.multiple_of(near + (1 - c) * 32, 32), 32), :] = own_other[part, :]
        away = base + (1 - zh) * 64
        for turn in range(NX):
            inner = lax.rem(x - turn + NX, NX) * 8
            piece = pl.ds(step * 32 + turn * 8, 8)
            held[pl.ds(pl.multiple_of(away + c * 32 + inner, 8), 8), :] = far[piece, :]
            held[pl.ds(pl.multiple_of(away + (1 - c) * 32 + inner, 8), 8), :] = far_other[piece, :]
    for block in range(16):
        rows = pl.ds(block * 32, 32)
        high[rows, :], low[rows, :] = split(held[rows, :])


def take_rows(tiles, rows, count):
    for p in range(OWN):
        for k in range(4):
            rows[p * FRAMES:(p + 1) * FRAMES, k * 128:(k + 1) * 128] = tiles[
                pl.ds(k * 8 + p, FRAMES, stride=count * 8), :
            ]


def to_tiles(rows):
    return rows.reshape(FRAMES, OWN, D // 128, 128).transpose(0, 2, 1, 3)


def head_masks():
    lane = lax.broadcasted_iota(jnp.int32, (HALF, PAIR), 1)
    return lane < HEAD


def forward_kernel(
    slopes, tokens, gain, high, low, spacing,
    emb_out, normt_h, normt_l, qkv_h, qkv_l, weights_out, wt_h, wt_l, mixt_h, mixt_l, pick,
    mixed,
):
    take_rows(tokens, emb_out, 5)
    tags = tokens[pl.ds(32, FRAMES, stride=40), :]
    ids = lax.broadcasted_iota(jnp.int32, (FRAMES, ACTIONS), 1).astype(f32)
    pick[...] = jnp.transpose((tags == ids).astype(f32)).astype(bf16)
    emb = emb_out[...]
    scale = lax.rsqrt(jnp.mean(emb * emb, axis=1, keepdims=True) + 1e-06)
    normed = emb * gain[...] * scale
    normt_h[...], normt_l[...] = split(jnp.transpose(normed))
    parts = split(normed)
    for block in range(QKV // 256):
        cols = slice(block * 256, block * 256 + 256)
        value = dot3(parts, (high[:, cols], low[:, cols]))
        if block < D // 256:
            value = value * 0.125
        qkv_h[:, cols], qkv_l[:, cols] = split(value)
    first = head_masks()
    zero = jnp.zeros((HALF, PAIR), bf16)
    for g in range(2):
        rows = slice(g * HALF, g * HALF + HALF)
        for pair in range(HEADS // 2):
            at = [slice(kind * D + pair * PAIR, kind * D + (pair + 1) * PAIR) for kind in range(3)]
            q, k, v = [(qkv_h[rows, cols], qkv_l[rows, cols]) for cols in at]
            k_twice = jnp.concatenate([k[0], k[0]], axis=1)
            v_all = jnp.concatenate([v[0], v[0], v[1]], axis=0)
            got = []
            for side in range(2):
                keep = first if side == 0 else ~first
                q_h, q_l = jnp.where(keep, q[0], zero), jnp.where(keep, q[1], zero)
                scores = dot(jnp.concatenate([q_h, q_l], axis=1), k_twice, NT) + dot(q_h, k[1], NT)
                scores = scores - slopes[pair * 2 + side] * spacing[...]
                raised = jnp.exp(scores - jnp.max(scores, axis=1, keepdims=True))
                weights = raised * (1.0 / jnp.sum(raised, axis=1, keepdims=True))
                index = (g * 4 + pair) * 2 + side
                weights_out[index] = weights
                wt_h[index], wt_l[index] = split(jnp.transpose(weights))
                w_h, w_l = split(weights)
                got.append(dot(jnp.concatenate([w_h, w_l, w_h], axis=1), v_all))
            mixed[rows, pair * PAIR:(pair + 1) * PAIR] = jnp.where(first, got[0], got[1])
    mixt_h[...], mixt_l[...] = split(jnp.transpose(mixed[...]))


def put_block(place_c, keep_ref, send_ref, block, tile, zero_rows, one_rows):
    mine = place_c == 0
    keep_ref[block, tile] = jnp.where(mine, zero_rows, one_rows)
    send_ref[block, tile] = jnp.where(mine, one_rows, zero_rows)


def backward_kernel(
    place, og_rows, gain, high, low, emb_in, normt_h, normt_l, qkv_h, qkv_l, weights_in,
    wt_h, wt_l, mixt_h, mixt_l, pick,
    keep_ref, send_ref, tokens_out,
    og, gr_h, gr_l,
):
    c = place[3]
    take_rows(og_rows, og, 4)
    og_parts = split(og[...])

    def place_columns(block, value):
        for y in YS:
            for zh in ZHS:
                for x in XS:
                    r = y * 128 + zh * 64 + x * 8
                    for half in range(2):
                        cols = slice(half * 128, half * 128 + 128)
                        put_block(
                            c, keep_ref, send_ref, x * NY + y, (zh * 8 + block) * 2 + half,
                            value[r:r + 8, cols], value[r + 32:r + 40, cols],
                        )

    gm = dot3(og_parts, (high[:, QKV:], low[:, QKV:]), NT)
    gm_h, gm_l = split(gm)
    mixt = (mixt_h[...], mixt_l[...])
    for block in range(2):
        cols = slice(block * 256, block * 256 + 256)
        place_columns(6 + block, dot3(mixt, (og_parts[0][:, cols], og_parts[1][:, cols])))
    first = head_masks()
    zero = jnp.zeros((HALF, PAIR), bf16)
    for g in range(2):
        rows = slice(g * HALF, g * HALF + HALF)
        for pair in range(HEADS // 2):
            at = [slice(kind * D + pair * PAIR, kind * D + (pair + 1) * PAIR) for kind in range(3)]
            q, k, v = [(qkv_h[rows, cols], qkv_l[rows, cols]) for cols in at]
            gmp = (gm_h[rows, at[0]], gm_l[rows, at[0]])
            v_twice = jnp.concatenate([v[0], v[0]], axis=1)
            k_all = jnp.concatenate([k[0], k[0], k[1]], axis=0)
            q_all = jnp.concatenate([q[0], q[0], q[1]], axis=0)
            gm_all = jnp.concatenate([gmp[0], gmp[0], gmp[1]], axis=0)
            dq, dk, dv = [], [], []
            for side in range(2):
                keep = first if side == 0 else ~first
                index = (g * 4 + pair) * 2 + side
                a_h, a_l = jnp.where(keep, gmp[0], zero), jnp.where(keep, gmp[1], zero)
                d_w = dot(jnp.concatenate([a_h, a_l], axis=1), v_twice, NT) + dot(a_h, v[1], NT)
                weights = weights_in[index]
                ds = weights * (d_w - jnp.sum(d_w * weights, axis=1, keepdims=True))
                s_h, s_l = split(ds)
                t_h, t_l = split(jnp.transpose(ds))
                p_h, p_l = wt_h[index], wt_l[index]
                dq.append(dot(jnp.concatenate([s_h, s_l, s_h], axis=1), k_all))
                dk.append(dot(jnp.concatenate([t_h, t_l, t_h], axis=1), q_all))
                dv.append(dot(jnp.concatenate([p_h, p_l, p_h], axis=1), gm_all))
            for cols, pieces, factor in zip(at, (dq, dk, dv), (0.125, 1.0, 1.0)):
                value = jnp.where(first, pieces[0], pieces[1]) * factor
                gr_h[rows, cols], gr_l[rows, cols] = split(value)
    normt = (normt_h[...], normt_l[...])
    for block in range(QKV // 256):
        cols = slice(block * 256, block * 256 + 256)
        place_columns(block, dot3(normt, (gr_h[:, cols], gr_l[:, cols])))
    gn = dot3((gr_h[...], gr_l[...]), (high[:, :QKV], low[:, :QKV]), NT)
    emb = emb_in[...]
    scale = lax.rsqrt(jnp.mean(emb * emb, axis=1, keepdims=True) + 1e-06)
    gain_sum = jnp.sum(gn * emb * scale, axis=0, keepdims=True)
    u = gn * gain[...]
    along = jnp.sum(u * emb, axis=1, keepdims=True) * (scale * scale * scale) * (1.0 / D)
    tokens = og[...] + (u * scale - emb * along)
    total = jnp.zeros((FRAMES, D), f32)
    for p in range(OWN):
        piece = tokens[p * FRAMES:(p + 1) * FRAMES, :]
        for k in range(4):
            tokens_out[pl.ds(k * 8 + p, FRAMES, stride=32), :] = piece[:, k * 128:(k + 1) * 128]
        total = total + piece
    total_h, total_l = split(total)
    table = dot(pick[...], total_h) + dot(pick[...], total_l)
    for block in range(16):
        r = slice(block * 8, block * 8 + 8)
        for half in range(2):
            left = slice(half * 128, half * 128 + 128)
            right = slice(256 + half * 128, 256 + half * 128 + 128)
            put_block(c, keep_ref, send_ref, block, 32 + half, table[r, left], table[r, right])
    gain_tile = jnp.concatenate(
        [gain_sum[:, i * 128:(i + 1) * 128] for i in range(4)] + [jnp.zeros((4, 128), f32)], axis=0
    )
    for block in range(16):
        keep_ref[block, 34] = gain_tile
        send_ref[block, 34] = gain_tile


def call(kernel, outs, scratch, scalars, *arrays, name):
    vmem = pl.BlockSpec(memory_space=pltpu.VMEM)
    smem = pl.BlockSpec(memory_space=pltpu.SMEM)
    return pl.pallas_call(
        kernel,
        out_shape=outs,
        in_specs=[smem] * len(scalars) + [vmem] * len(arrays),
        out_specs=jax.tree.map(lambda _: vmem, outs),
        scratch_shapes=scratch,
        compiler_params=pltpu.CompilerParams(vmem_limit_bytes=48 * 1024 * 1024),
        name=name,
    )(*scalars, *arrays)


def shape(*dims, kind=f32):
    return jax.ShapeDtypeStruct(dims, kind)


def gathered_weights(w_qkv, w_out, x, place):
    mine = jnp.concatenate([w_qkv, w_out], axis=1)
    quarter = lax.dynamic_slice(mine, (x * 8, 0), (8, mine.shape[1]))
    quarter = lax.ppermute(quarter, "dp", SWAP_ZH)
    far = jnp.concatenate(
        [quarter] + [lax.ppermute(quarter, "tm", turn_x(step)) for step in range(1, NX)], axis=0
    )

    def along_y(rows):
        return jnp.concatenate(
            [rows] + [lax.ppermute(rows, "dp", turn_y(step)) for step in range(1, NY)], axis=0
        )

    own_all, far_all = along_y(mine), along_y(far)
    own_other = lax.ppermute(own_all, "dp", SWAP_CORE)
    far_other = lax.ppermute(far_all, "dp", SWAP_CORE)
    return call(
        weights_kernel,
        (shape(D, QKV + D, kind=bf16),) * 2,
        [pltpu.VMEM((D, QKV + D), f32)],
        (place,),
        own_all, own_other, far_all, far_other,
        name="weights",
    )


def shards(
    video_tokens, actions, frame_times, act_table, norm_gain, w_qkv, w_out, slopes, out_grad
):
    t, d = lax.axis_index("tm"), lax.axis_index("dp")
    x, y, zh, c = t // NZL, d // (NZH * NC), (d // NC) % NZH, d % NC
    place = jnp.stack([x, y, zh, c]).astype(jnp.int32)
    gain = norm_gain.reshape(1, D)

    action = actions[0, 0]
    row = lax.dynamic_slice(act_table, (action, 0), (1, D))
    embedded = to_tiles(video_tokens[0, 0] + row)
    tag = jnp.broadcast_to(action.astype(f32), (FRAMES, 1, OWN, ACTIONS))
    tokens = exchange(jnp.concatenate([embedded, tag], axis=1), "tm")
    og = exchange(to_tiles(out_grad[0, 0]), "tm")
    high, low = gathered_weights(w_qkv, w_out, x, place)

    times = jnp.tile(frame_times[0].astype(f32), HALF // FRAMES)
    i = lax.broadcasted_iota(jnp.int32, (HALF, HALF), 0)
    j = lax.broadcasted_iota(jnp.int32, (HALF, HALF), 1)
    seen = (i // FRAMES == j // FRAMES) & (j <= i)
    spacing = jnp.where(seen, times[:, None] - times[None, :], f32(1e30))

    kept = call(
        forward_kernel,
        (
            shape(ROWS, D), shape(D, ROWS, kind=bf16), shape(D, ROWS, kind=bf16),
            shape(ROWS, QKV, kind=bf16), shape(ROWS, QKV, kind=bf16),
            shape(16, HALF, HALF), shape(16, HALF, HALF, kind=bf16),
            shape(16, HALF, HALF, kind=bf16),
            shape(D, ROWS, kind=bf16), shape(D, ROWS, kind=bf16),
            shape(ACTIONS, FRAMES, kind=bf16),
        ),
        [pltpu.VMEM((ROWS, D), f32)],
        (slopes,),
        tokens.reshape(ROWS * 5, 128), gain, high, low, spacing,
        name="forward",
    )
    keep, send, tokens_back = call(
        backward_kernel,
        (shape(16, TILES, 8, 128), shape(16, TILES, 8, 128), shape(ROWS * 4, 128)),
        [
            pltpu.VMEM((ROWS, D), f32),
            pltpu.VMEM((ROWS, QKV), bf16),
            pltpu.VMEM((ROWS, QKV), bf16),
        ],
        (place,),
        og.reshape(ROWS * 4, 128), gain, high, low, *kept,
        name="backward",
    )
    grad_tokens = exchange(tokens_back.reshape(FRAMES, 4, OWN, 128), "tm")

    both_cores = keep + lax.ppermute(send, "dp", SWAP_CORE)
    plane = jnp.sum(exchange(both_cores, BOTH, XY_GROUPS), axis=0)
    column = jnp.concatenate(
        [plane[:32].reshape(16, 2, 8, 128), jnp.broadcast_to(plane[32:], (16, 3, 8, 128))], axis=1
    )
    total = jnp.sum(exchange(column, BOTH, Z_GROUPS), axis=0)

    line = exchange(jnp.broadcast_to(total[:2], (NZL, 2, 8, 128)), "tm", ZL_GROUPS)
    table = total[2:4]
    turned = jnp.stack(
        [table] + [lax.ppermute(table, "dp", turn_y(step)) for step in range(1, NY)]
    )
    table_y = jnp.take(turned, (y - jnp.arange(NY)) % NY, axis=0)
    block = jnp.concatenate([line.reshape(16, 8, 128), table_y.reshape(8, 8, 128)], axis=0)
    sheet = exchange(jnp.broadcast_to(block, (NX, 24, 8, 128)), "tm", X_GROUPS)
    shares = sheet.reshape(NX, 24, 8, 128)
    main = shares[:, :16].transpose(0, 2, 1, 3).reshape(32, QKV + D)
    half = shares[:, 16:].reshape(16, 2, 8, 128).transpose(0, 2, 1, 3).reshape(ACTIONS, 256)
    other = lax.ppermute(half, "dp", SWAP_CORE)
    grad_table = jnp.where(
        c == 0, jnp.concatenate([half, other], axis=1), jnp.concatenate([other, half], axis=1)
    )
    return (
        grad_tokens.transpose(0, 2, 1, 3).reshape(1, 1, ROWS, D),
        main[:, :QKV],
        main[:, QKV:],
        grad_table,
        total[4, :4].reshape(D),
    )


def solution(mesh):
    return jax.shard_map(
        shards,
        mesh=mesh,
        in_specs=(
            P("dp", "tm", None, None),
            P("dp", "tm"),
            P("dp", None),
            P(),
            P(),
            P("dp", None),
            P("dp", None),
            P(),
            P("dp", "tm", None, None),
        ),
        out_specs=(P("dp", "tm", None, None), P("dp", None), P("dp", None), P(), P()),
        check_vma=False,
    )
```

time: 1490 us -> 289 us (0.19); the launches traced: 1460 us -> 284 us
  waiting for transfers between devices: 1250 us -> 43.8 us
  starting transfers between devices: 26.7 us -> 104 us
  matrix products: 34.4 us -> 0 us
  Pallas kernels: 0 us -> 29.3 us
  blocking collectives: 101 us -> 78.5 us
    psum x2 -> x0, waiting for transfers between devices: 783 us -> none  [the longest x1 429 us: shards(): qkv_share, out_share = lax.psum((qkv_share, out_share), 'tm')]
    all_gather x2 -> x0, waiting for transfers between devices: 209 us -> none  [the longest x1 112 us: shards(): lax.all_gather(w_qkv, 'dp', axis=0, tiled=True)]
    reduce_scatter x2 -> x0, waiting for transfers between devices: 155 us -> none  [the longest x1 134 us: shards(): lax.psum_scatter(grad_qkv, 'dp', scatter_dimension=0, tiled=True)]
    psum x1 -> x0, blocking collectives: 101 us -> none  [shards(): grad_table, grad_gain = lax.psum((grad_table, grad_gain), ('tm', 'dp'))]
    all_to_all x0 -> x3, blocking collectives: none -> 78.5 us  [exchange(): lax.all_to_all(value, axis, 0, 0, axis_index_groups=groups, tiled=True)]
    all_to_all x4, waiting for transfers between devices: 104 us -> 28.5 us  [exchange(): lax.all_to_all(value, axis, 0, 0, axis_index_groups=groups, tiled=True)]
    ppermute x0 -> x17, starting transfers between devices: none -> 61.1 us  [the longest x6 16 us: along_y(): lax.ppermute(rows, 'dp', turn_y(step))]
    dot_general x12 -> x0, matrix products: 34.4 us -> none  [the longest x3 14.2 us: project(): return jnp.einsum('cfpd,de->cfpe', token_rows, matrix, precision=precise)]
  transfers between devices with their start and end apart: 10 -> 21, of which waited for: 9 -> 9; matrix products, arithmetic and copies ran while one was open for 4% -> 2% of each run, Pallas kernels for 0% -> 5%
where the time goes in v1:
time: 289 us; the launch traced here: 284 us
  starting transfers between devices  104 us (36%)
  blocking collectives  78.5 us (27%)
  waiting for transfers between devices  43.8 us (15%)
  Pallas kernels  29.3 us (10%)
  local copies, waits for them, and re-layouts  21.7 us (8%)
  other arithmetic  5.5 us (2%)
    all_to_all x3, blocking collectives, exchange(): lax.all_to_all(value, axis, 0, 0, axis_index_groups=groups, tiled=True)  78.5 us
    all_to_all x4, starting transfers between devices, exchange(): lax.all_to_all(value, axis, 0, 0, axis_index_groups=groups, tiled=True)  42.5 us
    pallas_call x3, Pallas kernels, call(): pl.pallas_call(kernel, out_shape=outs, in_specs=[smem] * len(scalars) + [...  29.3 us
    all_to_all x4, waiting for transfers between devices, exchange(): lax.all_to_all(value, axis, 0, 0, axis_index_groups=groups, tiled=True)  28.5 us
    unnamed x55, local copies, waits for them, and re-layouts  16.5 us
    ppermute x6, starting transfers between devices, along_y(): lax.ppermute(rows, 'dp', turn_y(step))  16 us
    ppermute x3, starting transfers between devices, gathered_weights(): lax.ppermute(quarter, 'tm', turn_x(step))  10.2 us
    ppermute x3, starting transfers between devices, shards(): lax.ppermute(table, 'dp', turn_y(step))  8.64 us
  transfers between devices with their start and end apart: 21, of which 9 were waited for; matrix products, arithmetic and copies ran while one was open for 2% of the time, Pallas kernels for 5%

profile of v1, /device:TPU:25, one launch (start us, length us, event | category | flops | bytes accessed | tf_op | source)
XLA Modules:
  0.0 284.3 jit_solution(7186589195772419713)
XLA Ops:
  3.6 15.1 %all-to-all-start.1 = ((f32[32,5,8,128]{3,2,1,0:T(8,128)}), f32[32,5,8,128]{3,2,1,0:T(8,128)S(1)}, u32[]{:S(2)}, u32[]{:S(2)}) async-start(f32[32,5,8,128]{3,2,1,0:T(8,128)} %concatenate.32), calls=%async_computation.1 | async-start | bytes 1310720 | tf_op jit(solution)/shard_map/all_to_all | solution.py:55
  18.8 7.9 %collective-permute-start.4 = (f32[8,2048]{1,0:T(8,128)S(1)}, f32[8,2048]{1,0:T(8,128)S(1)}, u32[]{:S(2)}, u32[]{:S(2)}) collective-permute-start(f32[8,2048]{1,0:T(8,128)S(1)} %constant_dynamic-slice_fusion.1), channel_id=1, source_target_pairs={{0,2},{1,3},{2,0},{3,1},{4,6},{5,7},{6,4},{7,5},{8,10},{9,11},{10,... | collective-permute-start | bytes 196616 | tf_op jit(solution)/shard_map/ppermute | solution.py:274
  26.8 1.9 collective-permute-start
  28.7 4.1 %collective-permute-start.1 = (f32[32,2048]{1,0:T(8,128)S(1)}, f32[32,2048]{1,0:T(8,128)S(1)}, u32[]{:S(2)}, u32[]{:S(2)}) collective-permute-start(f32[32,2048]{1,0:T(8,128)S(1)} %constant_dynamic-update-slice_fusion), channel_id=1, source_target_pairs={{0,8},{1,9},{2,10},{3,11},{4,12},{5,13},{6,14},{7,15},{8,0},{9,1},... | collective-permute-start | bytes 786440 | tf_op jit(solution)/shard_map/ppermute | solution.py:281
  32.9 1.9 collective-permute-start.2
  34.8 3.7 %collective-permute-done.4 = f32[8,2048]{1,0:T(8,128)S(1)} collective-permute-done((f32[8,2048]{1,0:T(8,128)S(1)}, f32[8,2048]{1,0:T(8,128)S(1)}, u32[]{:S(2)}, u32[]{:S(2)}) %collective-permute-start.4) | collective-permute-done | bytes 65568 | tf_op jit(solution)/shard_map/ppermute | solution.py:274
  38.5 2.8 collective-permute-start.5
  41.9 4.3 %collective-permute-start.6 = (f32[8,2048]{1,0:T(8,128)S(1)}, f32[8,2048]{1,0:T(8,128)S(1)}, u32[]{:S(2)}, u32[]{:S(2)}) collective-permute-start(f32[8,2048]{1,0:T(8,128)S(1)} %collective-permute-done.4), channel_id=1, source_target_pairs={{0,256},{16,272},{32,288},{48,304},{64,320},{80,336},{96,352},{112... | collective-permute-start | bytes 196616 | tf_op jit(solution)/shard_map/ppermute | solution.py:276
  46.3 3.0 %collective-permute-start.7 = (f32[8,2048]{1,0:T(8,128)S(1)}, f32[8,2048]{1,0:T(8,128)S(1)}, u32[]{:S(2)}, u32[]{:S(2)}) collective-permute-start(f32[8,2048]{1,0:T(8,128)S(1)} %collective-permute-done.4), channel_id=1, source_target_pairs={{0,384},{16,400},{32,416},{48,432},{64,448},{80,464},{96,480},{112... | collective-permute-start | bytes 196616 | tf_op jit(solution)/shard_map/ppermute | solution.py:276
  50.6 6.9 %all-to-all-done.1 = f32[32,5,8,128]{3,2,1,0:T(8,128)S(1)} async-done(((f32[32,5,8,128]{3,2,1,0:T(8,128)}), f32[32,5,8,128]{3,2,1,0:T(8,128)S(1)}, u32[]{:S(2)}, u32[]{:S(2)}) %all-to-all-start.1) | async-done | bytes 655392 | tf_op jit(solution)/shard_map/all_to_all | solution.py:55
  57.5 20.1 %all-to-all-start = ((f32[32,4,8,128]{3,2,1,0:T(8,128)}), f32[32,4,8,128]{3,2,1,0:T(8,128)S(1)}, u32[]{:S(2)}, u32[]{:S(2)}) async-start(f32[32,4,8,128]{3,2,1,0:T(8,128)} %bitcast.5), calls=%async_computation | async-start | bytes 1048576 | tf_op jit(solution)/shard_map/all_to_all | solution.py:55
  80.2 4.1 %collective-permute-start.9 = (f32[32,2048]{1,0:T(8,128)}, f32[32,2048]{1,0:T(8,128)S(1)}, u32[]{:S(2)}, u32[]{:S(2)}) collective-permute-start(f32[32,2048]{1,0:T(8,128)} %get-tuple-element.37), channel_id=1, source_target_pairs={{0,8},{1,9},{2,10},{3,11},{4,12},{5,13},{6,14},{7,15},{8,0},{9,1},... | collective-permute-start | bytes 786440 | tf_op jit(solution)/shard_map/ppermute | solution.py:281
  88.3 5.9 %collective-permute-start.3 = (f32[128,2048]{1,0:T(8,128)S(1)}, f32[128,2048]{1,0:T(8,128)}, u32[]{:S(2)}, u32[]{:S(2)}) collective-permute-start(f32[128,2048]{1,0:T(8,128)S(1)} %pad_maximum_fusion.own), channel_id=1, source_target_pairs={{0,1},{1,0},{2,3},{3,2},{4,5},{5,4},{6,7},{7,6},{8,9},{9,8},{10,11... | collective-permute-start | bytes 3145736 | tf_op jit(solution)/shard_map/ppermute | solution.py:285
  94.3 2.1 collective-permute-done.10
  96.4 4.9 %collective-permute-start.11 = (f32[128,2048]{1,0:T(8,128)S(1)}, f32[128,2048]{1,0:T(8,128)}, u32[]{:S(2)}, u32[]{:S(2)}) collective-permute-start(f32[128,2048]{1,0:T(8,128)S(1)} %constant_dynamic-update-slice_fusion.6.far), channel_id=1, source_target_pairs={{0,1},{1,0},{2,3},{3,2},{4,5},{5,4},{6,7},{7,6},{8,9},{9,8},{10,11... | collective-permute-start | bytes 3145736 | tf_op jit(solution)/shard_map/ppermute | solution.py:286
  103.6 4.6 %weights.1 = (bf16[512,2048]{1,0:T(8,128)(2,1)}, bf16[512,2048]{1,0:T(8,128)(2,1)}) custom-call(s32[4]{0:T(128)S(1)} %pad_add_fusion.place, f32[128,2048]{1,0:T(8,128)S(1)} %pad_maximum_fusion.own, f32[128,2048]{1,0:T(8,128)} %collective-permute-done.3.own_other, f32[128,2048]{1,0:T(8,128)S(1)} %constant_dynamic-update-slice_fusion.6.far, ...), custom_call_target="tpu_custom_call" | custom-call | tf_op jit(solution)/shard_map/weights/pallas_call | solution.py:256
  108.2 9.6 %forward.1 = (f32[256,512]{1,0:T(8,128)S(1)}, bf16[512,256]{1,0:T(8,128)(2,1)S(1)}, bf16[512,256]{1,0:T(8,128)(2,1)S(1)}, bf16[256,1536]{1,0:T(8,128)(2,1)S(1)},...) custom-call(f32[8]{0:T(128)S(1)} %copy-done.17, ...), custom_call_target="tpu_custom_call" | custom-call | tf_op jit(solution)/shard_map/forward/pallas_call | solution.py:256
  130.7 15.0 %backward.1 = (f32[16,35,8,128]{3,2,1,0:T(8,128)}, f32[16,35,8,128]{3,2,1,0:T(8,128)}, f32[1024,128]{1,0:T(8,128)}) custom-call(s32[4]{0:T(128)S(1)} %pad_add_fusion.place, f32[1024,128]{1,0:T(8,128)S(1)} %bitcast.51, f32[1,512]{1,0:T(1,128)S(1)} %bitcast.53, bf16[512,2048]{1,0:T(8,128)(2,1)} %get-tuple-element.21.high, ...), custom_call_target="tpu_custom_call" | custom-call | tf_op jit(solution)/shard_map/backward/pallas_call | solution.py:256
  145.7 2.3 collective-permute-start.12
  148.0 4.3 %collective-permute-done.12 = f32[16,35,8,128]{3,2,1,0:T(8,128)S(1)} collective-permute-done((f32[16,35,8,128]{3,2,1,0:T(8,128)}, f32[16,35,8,128]{3,2,1,0:T(8,128)S(1)}, u32[]{:S(2)}, u32[]{:S(2)}) %collective-permute-start.12) | collective-permute-done | bytes 2293792 | tf_op jit(solution)/shard_map/ppermute | solution.py:348
  154.2 33.8 %all_to_all.35 = f32[16,35,8,128]{3,2,1,0:T(8,128)S(1)} all-to-all(f32[16,35,8,128]{3,2,1,0:T(8,128)S(1)} %add.75), channel_id=1, replica_groups={{0,4,8,12,128,132,136,140,256,260,264,268,384,388,392,396},{1,5,9,13,12..., dimensions={0} | all-to-all | bytes 4587520 | tf_op jit(solution)/shard_map/all_to_all | solution.py:55
  188.2 22.8 %all_to_all.36 = f32[16,5,8,128]{3,2,1,0:T(8,128)S(1)} all-to-all(f32[16,5,8,128]{3,2,1,0:T(8,128)S(1)} %pad_maximum_fusion.1), channel_id=1, replica_groups={{0,16,32,48,64,80,96,112,2,18,34,50,66,82,98,114},{1,17,33,49,65,81,97,..., dimensions={0} | all-to-all | bytes 655360 | tf_op jit(solution)/shard_map/all_to_all | solution.py:55
  211.0 21.9 %all_to_all.37 = f32[8,2,8,128]{3,2,1,0:T(8,128)S(1)} all-to-all(f32[8,2,8,128]{3,2,1,0:T(8,128)S(1)} %broadcast_in_dim.30), channel_id=1, replica_groups={{0,16,32,48,64,80,96,112},{128,144,160,176,192,208,224,240},{256,272,28..., dimensions={0} | all-to-all | bytes 131072 | tf_op jit(solution)/shard_map/all_to_all | solution.py:55
  232.9 3.9 %all-to-all-start.2 = ((f32[32,4,8,128]{3,2,1,0:T(8,128)}), f32[32,4,8,128]{3,2,1,0:T(8,128)S(1)}, u32[]{:S(2)}, u32[]{:S(2)}) async-start(f32[32,4,8,128]{3,2,1,0:T(8,128)} %bitcast.14), calls=%async_computation.2 | async-start | bytes 1048576 | tf_op jit(solution)/shard_map/all_to_all | solution.py:55
  236.8 3.7 %collective-permute-start.13 = (f32[2,8,128]{2,1,0:T(8,128)S(1)}, f32[2,8,128]{2,1,0:T(8,128)S(1)}, u32[]{:S(2)}, u32[]{:S(2)}) collective-permute-start(f32[2,8,128]{2,1,0:T(8,128)S(1)} %get-tuple-element.47), channel_id=1, source_target_pairs={{0,4},{1,5},{2,6},{3,7},{4,8},{5,9},{6,10},{7,11},{8,12},{9,13},{1... | collective-permute-start | bytes 24584 | tf_op jit(solution)/shard_map/ppermute | solution.py:358
  240.6 3.0 %collective-permute-start.14 = (f32[2,8,128]{2,1,0:T(8,128)S(1)}, f32[2,8,128]{2,1,0:T(8,128)S(1)}, u32[]{:S(2)}, u32[]{:S(2)}) collective-permute-start(f32[2,8,128]{2,1,0:T(8,128)S(1)} %get-tuple-element.47), channel_id=1, source_target_pairs={{0,8},{1,9},{2,10},{3,11},{4,12},{5,13},{6,14},{7,15},{8,0},{9,1},... | collective-permute-start | bytes 24584 | tf_op jit(solution)/shard_map/ppermute | solution.py:358
  243.6 1.9 collective-permute-start.15
  246.5 2.7 collective-permute-done.15
  249.8 16.0 %all-to-all-done.2 = f32[32,4,8,128]{3,2,1,0:T(8,128)S(1)} async-done(((f32[32,4,8,128]{3,2,1,0:T(8,128)}), f32[32,4,8,128]{3,2,1,0:T(8,128)S(1)}, u32[]{:S(2)}, u32[]{:S(2)}) %all-to-all-start.2) | async-done | bytes 524320 | tf_op jit(solution)/shard_map/all_to_all | solution.py:55
  266.6 3.5 %all-to-all-start.6 = ((f32[4,24,8,128]{3,2,1,0:T(8,128)}), f32[4,24,8,128]{3,2,1,0:T(8,128)S(1)}, u32[]{:S(2)}, u32[]{:S(2)}) async-start(f32[4,24,8,128]{3,2,1,0:T(8,128)} %broadcast_in_dim.35), calls=%async_computation.6 | async-start | bytes 786432 | tf_op jit(solution)/shard_map/all_to_all | solution.py:55
  270.7 5.6 %all-to-all-done.6 = f32[4,24,8,128]{3,2,1,0:T(8,128)S(1)} async-done(((f32[4,24,8,128]{3,2,1,0:T(8,128)}), f32[4,24,8,128]{3,2,1,0:T(8,128)S(1)}, u32[]{:S(2)}, u32[]{:S(2)}) %all-to-all-start.6) | async-done | bytes 393248 | tf_op jit(solution)/shard_map/all_to_all | solution.py:55
  276.3 5.2 %collective-permute-start.16 = (f32[128,256]{1,0:T(8,128)S(1)}, f32[128,256]{1,0:T(8,128)S(1)}, u32[]{:S(2)}, u32[]{:S(2)}) collective-permute-start(f32[128,256]{1,0:T(8,128)S(1)} %bitcast.55), channel_id=1, source_target_pairs={{0,1},{1,0},{2,3},{3,2},{4,5},{5,4},{6,7},{7,6},{8,9},{9,8},{10,11... | collective-permute-start | bytes 393224 | tf_op jit(solution)/shard_map/ppermute | solution.py:366
  (111 shorter events, 33.6 us)
Async XLA Ops:
  0.6 1.0 copy-start
  0.6 18.1 %copy-start.21 = (f32[32,1536]{1,0:T(8,128)S(1)}, f32[32,1536]{1,0:T(8,128)}, u32[]{:S(2)}) copy-start(f32[32,1536]{1,0:T(8,128)} %param.14) | copy-start | bytes 589828
  0.7 18.1 %copy-start.22 = (f32[32,512]{1,0:T(8,128)S(1)}, f32[32,512]{1,0:T(8,128)}, u32[]{:S(2)}) copy-start(f32[32,512]{1,0:T(8,128)} %param.15) | copy-start | bytes 196612
  3.6 53.9 %all-to-all-start.1 = ((f32[32,5,8,128]{3,2,1,0:T(8,128)}), f32[32,5,8,128]{3,2,1,0:T(8,128)S(1)}, u32[]{:S(2)}, u32[]{:S(2)}) async-start(f32[32,5,8,128]{3,2,1,0:T(8,128)} %concatenate.32), calls=%async_computation.1 | async-start | bytes 1310720 | tf_op jit(solution)/shard_map/all_to_all | solution.py:55
  18.8 67.5 %copy-start.18 = (f32[32,2048]{1,0:T(8,128)}, f32[32,2048]{1,0:T(8,128)S(1)}, u32[]{:S(2)}) copy-start(f32[32,2048]{1,0:T(8,128)S(1)} %constant_dynamic-update-slice_fusion) | copy-start | bytes 786436
  18.8 19.6 %collective-permute-start.4 = (f32[8,2048]{1,0:T(8,128)S(1)}, f32[8,2048]{1,0:T(8,128)S(1)}, u32[]{:S(2)}, u32[]{:S(2)}) collective-permute-start(f32[8,2048]{1,0:T(8,128)S(1)} %constant_dynamic-slice_fusion.1), channel_id=1, source_target_pairs={{0,2},{1,3},{2,0},{3,1},{4,6},{5,7},{6,4},{7,5},{8,10},{9,11},{10,... | collective-permute-start | bytes 196616 | tf_op jit(solution)/shard_map/ppermute | solution.py:274
  26.8 57.6 %collective-permute-start = (f32[32,2048]{1,0:T(8,128)S(1)}, f32[32,2048]{1,0:T(8,128)S(1)}, u32[]{:S(2)}, u32[]{:S(2)}) collective-permute-start(f32[32,2048]{1,0:T(8,128)S(1)} %constant_dynamic-update-slice_fusion), channel_id=1, source_target_pairs={{0,4},{1,5},{2,6},{3,7},{4,8},{5,9},{6,10},{7,11},{8,12},{9,13},{1... | collective-permute-start | bytes 786440 | tf_op jit(solution)/shard_map/ppermute | solution.py:281
  28.7 57.6 %collective-permute-start.1 = (f32[32,2048]{1,0:T(8,128)S(1)}, f32[32,2048]{1,0:T(8,128)S(1)}, u32[]{:S(2)}, u32[]{:S(2)}) collective-permute-start(f32[32,2048]{1,0:T(8,128)S(1)} %constant_dynamic-update-slice_fusion), channel_id=1, source_target_pairs={{0,8},{1,9},{2,10},{3,11},{4,12},{5,13},{6,14},{7,15},{8,0},{9,1},... | collective-permute-start | bytes 786440 | tf_op jit(solution)/shard_map/ppermute | solution.py:281
  32.9 54.2 %collective-permute-start.2 = (f32[32,2048]{1,0:T(8,128)S(1)}, f32[32,2048]{1,0:T(8,128)}, u32[]{:S(2)}, u32[]{:S(2)}) collective-permute-start(f32[32,2048]{1,0:T(8,128)S(1)} %constant_dynamic-update-slice_fusion), channel_id=1, source_target_pairs={{0,12},{1,13},{2,14},{3,15},{4,0},{5,1},{6,2},{7,3},{8,4},{9,5},{1... | collective-permute-start | bytes 786440 | tf_op jit(solution)/shard_map/ppermute | solution.py:281
  38.5 7.8 %collective-permute-start.5 = (f32[8,2048]{1,0:T(8,128)S(1)}, f32[8,2048]{1,0:T(8,128)S(1)}, u32[]{:S(2)}, u32[]{:S(2)}) collective-permute-start(f32[8,2048]{1,0:T(8,128)S(1)} %collective-permute-done.4), channel_id=1, source_target_pairs={{0,128},{16,144},{32,160},{48,176},{64,192},{80,208},{96,224},{112... | collective-permute-start | bytes 196616 | tf_op jit(solution)/shard_map/ppermute | solution.py:276
  41.9 8.1 %collective-permute-start.6 = (f32[8,2048]{1,0:T(8,128)S(1)}, f32[8,2048]{1,0:T(8,128)S(1)}, u32[]{:S(2)}, u32[]{:S(2)}) collective-permute-start(f32[8,2048]{1,0:T(8,128)S(1)} %collective-permute-done.4), channel_id=1, source_target_pairs={{0,256},{16,272},{32,288},{48,304},{64,320},{80,336},{96,352},{112... | collective-permute-start | bytes 196616 | tf_op jit(solution)/shard_map/ppermute | solution.py:276
  46.3 31.3 %collective-permute-start.7 = (f32[8,2048]{1,0:T(8,128)S(1)}, f32[8,2048]{1,0:T(8,128)S(1)}, u32[]{:S(2)}, u32[]{:S(2)}) collective-permute-start(f32[8,2048]{1,0:T(8,128)S(1)} %collective-permute-done.4), channel_id=1, source_target_pairs={{0,384},{16,400},{32,416},{48,432},{64,448},{80,464},{96,480},{112... | collective-permute-start | bytes 196616 | tf_op jit(solution)/shard_map/ppermute | solution.py:276
  57.5 43.9 %copy-start.23 = (s32[1,32]{1,0:T(1,128)S(1)}, s32[1,32]{1,0:T(1,128)}, u32[]{:S(2)}) copy-start(s32[1,32]{1,0:T(1,128)} %param.11) | copy-start | bytes 388
  57.5 66.4 %all-to-all-start = ((f32[32,4,8,128]{3,2,1,0:T(8,128)}), f32[32,4,8,128]{3,2,1,0:T(8,128)S(1)}, u32[]{:S(2)}, u32[]{:S(2)}) async-start(f32[32,4,8,128]{3,2,1,0:T(8,128)} %bitcast.5), calls=%async_computation | async-start | bytes 1048576 | tf_op jit(solution)/shard_map/all_to_all | solution.py:55
  78.3 16.0 %collective-permute-start.8 = (f32[32,2048]{1,0:T(8,128)}, f32[32,2048]{1,0:T(8,128)S(1)}, u32[]{:S(2)}, u32[]{:S(2)}) collective-permute-start(f32[32,2048]{1,0:T(8,128)} %get-tuple-element.37), channel_id=1, source_target_pairs={{0,4},{1,5},{2,6},{3,7},{4,8},{5,9},{6,10},{7,11},{8,12},{9,13},{1... | collective-permute-start | bytes 786440 | tf_op jit(solution)/shard_map/ppermute | solution.py:281
  80.2 14.1 %collective-permute-start.9 = (f32[32,2048]{1,0:T(8,128)}, f32[32,2048]{1,0:T(8,128)S(1)}, u32[]{:S(2)}, u32[]{:S(2)}) collective-permute-start(f32[32,2048]{1,0:T(8,128)} %get-tuple-element.37), channel_id=1, source_target_pairs={{0,8},{1,9},{2,10},{3,11},{4,12},{5,13},{6,14},{7,15},{8,0},{9,1},... | collective-permute-start | bytes 786440 | tf_op jit(solution)/shard_map/ppermute | solution.py:281
  84.4 2.0 copy-start.19
  84.4 12.0 %collective-permute-start.10 = (f32[32,2048]{1,0:T(8,128)}, f32[32,2048]{1,0:T(8,128)S(1)}, u32[]{:S(2)}, u32[]{:S(2)}) collective-permute-start(f32[32,2048]{1,0:T(8,128)} %get-tuple-element.37), channel_id=1, source_target_pairs={{0,12},{1,13},{2,14},{3,15},{4,0},{5,1},{6,2},{7,3},{8,4},{9,5},{1... | collective-permute-start | bytes 786440 | tf_op jit(solution)/shard_map/ppermute | solution.py:281
  88.3 13.4 %collective-permute-start.3 = (f32[128,2048]{1,0:T(8,128)S(1)}, f32[128,2048]{1,0:T(8,128)}, u32[]{:S(2)}, u32[]{:S(2)}) collective-permute-start(f32[128,2048]{1,0:T(8,128)S(1)} %pad_maximum_fusion.own), channel_id=1, source_target_pairs={{0,1},{1,0},{2,3},{3,2},{4,5},{5,4},{6,7},{7,6},{8,9},{9,8},{10,11... | collective-permute-start | bytes 3145736 | tf_op jit(solution)/shard_map/ppermute | solution.py:285
  96.4 11.8 %copy-start.16 = (f32[512]{0:T(512)S(1)}, f32[512]{0:T(512)}, u32[]{:S(2)}) copy-start(f32[512]{0:T(512)} %param.13) | copy-start | bytes 6148
  96.4 11.8 %copy-start.17 = (f32[8]{0:T(128)S(1)}, f32[8]{0:T(128)}, u32[]{:S(2)}) copy-start(f32[8]{0:T(128)} %slopes.1) | copy-start | bytes 100
  96.4 7.1 %collective-permute-start.11 = (f32[128,2048]{1,0:T(8,128)S(1)}, f32[128,2048]{1,0:T(8,128)}, u32[]{:S(2)}, u32[]{:S(2)}) collective-permute-start(f32[128,2048]{1,0:T(8,128)S(1)} %constant_dynamic-update-slice_fusion.6.far), channel_id=1, source_target_pairs={{0,1},{1,0},{2,3},{3,2},{4,5},{5,4},{6,7},{7,6},{8,9},{9,8},{10,11... | collective-permute-start | bytes 3145736 | tf_op jit(solution)/shard_map/ppermute | solution.py:286
  123.9 1.0 copy-start.3
  125.0 1.0 copy-start.5
  126.0 1.0 copy-start.7
  145.7 6.5 %collective-permute-start.12 = (f32[16,35,8,128]{3,2,1,0:T(8,128)}, f32[16,35,8,128]{3,2,1,0:T(8,128)S(1)}, u32[]{:S(2)}, u32[]{:S(2)}) collective-permute-start(f32[16,35,8,128]{3,2,1,0:T(8,128)} %get-tuple-element.36), channel_id=1, source_target_pairs={{0,1},{1,0},{2,3},{3,2},{4,5},{5,4},{6,7},{7,6},{8,9},{9,8},{10,11... | collective-permute-start | bytes 6881288 | tf_op jit(solution)/shard_map/ppermute | solution.py:348
  232.9 32.9 %all-to-all-start.2 = ((f32[32,4,8,128]{3,2,1,0:T(8,128)}), f32[32,4,8,128]{3,2,1,0:T(8,128)S(1)}, u32[]{:S(2)}, u32[]{:S(2)}) async-start(f32[32,4,8,128]{3,2,1,0:T(8,128)} %bitcast.14), calls=%async_computation.2 | async-start | bytes 1048576 | tf_op jit(solution)/shard_map/all_to_all | solution.py:55
  236.8 8.8 %collective-permute-start.13 = (f32[2,8,128]{2,1,0:T(8,128)S(1)}, f32[2,8,128]{2,1,0:T(8,128)S(1)}, u32[]{:S(2)}, u32[]{:S(2)}) collective-permute-start(f32[2,8,128]{2,1,0:T(8,128)S(1)} %get-tuple-element.47), channel_id=1, source_target_pairs={{0,4},{1,5},{2,6},{3,7},{4,8},{5,9},{6,10},{7,11},{8,12},{9,13},{1... | collective-permute-start | bytes 24584 | tf_op jit(solution)/shard_map/ppermute | solution.py:358
  240.6 5.9 %collective-permute-start.14 = (f32[2,8,128]{2,1,0:T(8,128)S(1)}, f32[2,8,128]{2,1,0:T(8,128)S(1)}, u32[]{:S(2)}, u32[]{:S(2)}) collective-permute-start(f32[2,8,128]{2,1,0:T(8,128)S(1)} %get-tuple-element.47), channel_id=1, source_target_pairs={{0,8},{1,9},{2,10},{3,11},{4,12},{5,13},{6,14},{7,15},{8,0},{9,1},... | collective-permute-start | bytes 24584 | tf_op jit(solution)/shard_map/ppermute | solution.py:358
  243.6 5.6 %collective-permute-start.15 = (f32[2,8,128]{2,1,0:T(8,128)S(1)}, f32[2,8,128]{2,1,0:T(8,128)S(1)}, u32[]{:S(2)}, u32[]{:S(2)}) collective-permute-start(f32[2,8,128]{2,1,0:T(8,128)S(1)} %get-tuple-element.47), channel_id=1, source_target_pairs={{0,12},{1,13},{2,14},{3,15},{4,0},{5,1},{6,2},{7,3},{8,4},{9,5},{1... | collective-permute-start | bytes 24584 | tf_op jit(solution)/shard_map/ppermute | solution.py:358
  266.6 9.7 %all-to-all-start.6 = ((f32[4,24,8,128]{3,2,1,0:T(8,128)}), f32[4,24,8,128]{3,2,1,0:T(8,128)S(1)}, u32[]{:S(2)}, u32[]{:S(2)}) async-start(f32[4,24,8,128]{3,2,1,0:T(8,128)} %broadcast_in_dim.35), calls=%async_computation.6 | async-start | bytes 786432 | tf_op jit(solution)/shard_map/all_to_all | solution.py:55
  276.3 6.5 %collective-permute-start.16 = (f32[128,256]{1,0:T(8,128)S(1)}, f32[128,256]{1,0:T(8,128)S(1)}, u32[]{:S(2)}, u32[]{:S(2)}) collective-permute-start(f32[128,256]{1,0:T(8,128)S(1)} %bitcast.55), channel_id=1, source_target_pairs={{0,1},{1,0},{2,3},{3,2},{4,5},{5,4},{6,7},{7,6},{8,9},{9,8},{10,11... | collective-permute-start | bytes 393224 | tf_op jit(solution)/shard_map/ppermute | solution.py:366
  (13 other events, 10.4 us)

commit v2 on v0

v2 whole, which is shorter than its diff:
```python
import functools

import jax
import jax.numpy as jnp
from jax import lax
from jax.experimental import pallas as pl
from jax.experimental.pallas import tpu as pltpu
from jax.sharding import PartitionSpec as P

NX, NZL, NY, NZH, NC = 4, 8, 4, 2, 2
D, QKV, HEADS, HEAD, FRAMES, OWN = 512, 1536, 8, 64, 32, 8
ROWS = FRAMES * OWN
HALF = ROWS // 2
PAIR = 2 * HEAD
ACTIONS = 128
TILES = 41
f32, bf16 = jnp.float32, jnp.bfloat16
BOTH = ("tm", "dp")


def tm_of(x, zl):
    return x * NZL + zl


def dp_of(y, zh, c):
    return (y * NZH + zh) * NC + c


def flat_of(x, zl, y, zh, c):
    return tm_of(x, zl) * (NY * NZH * NC) + dp_of(y, zh, c)


XS, ZLS, YS, ZHS, CS = range(NX), range(NZL), range(NY), range(NZH), range(NC)
X_GROUPS = [[tm_of(x, zl) for x in XS] for zl in ZLS]
ZL_GROUPS = [[tm_of(x, zl) for zl in ZLS] for x in XS]
YC_GROUPS = [[dp_of(y, zh, c) for y in YS for c in CS] for zh in ZHS]
Z_GROUPS = [
    [flat_of(x, zl, y, zh, c) for zh in ZHS for zl in ZLS] for x in XS for y in YS for c in CS
]
SWAP_CORE = [(dp_of(y, zh, c), dp_of(y, zh, 1 - c)) for y in YS for zh in ZHS for c in CS]
SWAP_ZH = [(dp_of(y, zh, c), dp_of(y, 1 - zh, c)) for y in YS for zh in ZHS for c in CS]


def turn_y(step):
    return [(dp_of(y, zh, c), dp_of((y + step) % NY, zh, c)) for y in YS for zh in ZHS for c in CS]


def turn_x(step):
    return [(tm_of(x, zl), tm_of((x + step) % NX, zl)) for x in XS for zl in ZLS]


def exchange(value, axis, groups=None):
    return lax.all_to_all(value, axis, 0, 0, axis_index_groups=groups, tiled=True)


def split(value):
    high = value.astype(bf16)
    return high, (value - high.astype(f32)).astype(bf16)


NN = (((1,), (0,)), ((), ()))
NT = (((1,), (1,)), ((), ()))


def dot(a, b, dims=NN):
    return lax.dot_general(a, b, dims, preferred_element_type=f32)


def dot3(a, b, dims=NN):
    return dot(a[0], b[0], dims) + (dot(a[0], b[1], dims) + dot(a[1], b[0], dims))


def take_rows(tiles, rows, start):
    for p in range(OWN):
        for k in range(4):
            rows[p * FRAMES:(p + 1) * FRAMES, k * 128:(k + 1) * 128] = tiles[
                pl.ds((start + k) * 8 + p, FRAMES, stride=72), :
            ]


def to_tiles(rows):
    return rows.reshape(FRAMES, OWN, D // 128, 128).transpose(0, 2, 1, 3)


def head_masks():
    lane = lax.broadcasted_iota(jnp.int32, (HALF, PAIR), 1)
    return lane < HEAD


def gather_weights(place, own, far_mine, far_other, high, low):
    x, y, zh, c = place[0], place[1], place[2], place[3]
    for y_to in YS:
        for side in CS:
            at = pl.ds(pl.multiple_of(y_to * 128 + zh * 64 + side * 32, 32), 32)
            high[at, :], low[at, :] = split(own[y_to * 2 + side])
        turn_y = lax.rem(y - y_to + NY, NY) * NX
        for x_to in range(0, NX, 2):
            turns = [turn_y + lax.rem(x - x_to - i + NX, NX) for i in range(2)]
            for side, ref in ((c, far_mine), (1 - c, far_other)):
                rows = jnp.concatenate([ref[turn] for turn in turns], axis=0)
                at = y_to * 128 + (1 - zh) * 64 + side * 32 + x_to * 8
                at = pl.ds(pl.multiple_of(at, 16), 16)
                high[at, :], low[at, :] = split(rows)


def sublayer_kernel(
    place, slopes, tiles, gain, own, far_mine, far_other, spacing,
    grads, tokens_out,
    high, low, emb_ref, og, qkv_h, qkv_l, gm_h, gm_l, mixed, gr_h, gr_l,
):
    take_rows(tiles, emb_ref, 0)
    take_rows(tiles, og, 4)
    gather_weights(place, own, far_mine, far_other, high, low)

    tags = tiles[pl.ds(64, FRAMES, stride=72), :]
    ids = lax.broadcasted_iota(jnp.int32, (FRAMES, ACTIONS), 1).astype(f32)
    pick = jnp.transpose((tags == ids).astype(f32)).astype(bf16)

    emb = emb_ref[...]
    scale = lax.rsqrt(jnp.mean(emb * emb, axis=1, keepdims=True) + 1e-06)
    normed = emb * gain[...] * scale
    parts = split(normed)
    for block in range(QKV // 256):
        cols = slice(block * 256, block * 256 + 256)
        value = dot3(parts, (high[:, cols], low[:, cols]))
        if block < D // 256:
            value = value * 0.125
        qkv_h[:, cols], qkv_l[:, cols] = split(value)
    og_parts = split(og[...])
    gm_h[...], gm_l[...] = split(dot3(og_parts, (high[:, QKV:], low[:, QKV:]), NT))

    lane = lax.broadcasted_iota(jnp.int32, (ROWS, PAIR), 1) < HEAD
    upper = lax.broadcasted_iota(jnp.int32, (ROWS, PAIR), 0) < HALF
    own_half = lane == upper
    first = lane[:HALF]
    zero = jnp.zeros((ROWS, PAIR), bf16)

    def both_heads(parts):
        twice = [jnp.where(own_half, jnp.concatenate([v, v], axis=0), zero) for v in parts]
        return jnp.concatenate([twice[0], twice[1], twice[0]], axis=1)

    def wide(parts):
        return jnp.concatenate([parts[0], parts[0], parts[1]], axis=1)

    def tall(parts):
        return jnp.concatenate([parts[0], parts[0], parts[1]], axis=0)

    def left(value):
        high_part, low_part = split(value)
        return jnp.concatenate([high_part, low_part, high_part], axis=1)

    def turned(value):
        return jnp.concatenate([jnp.transpose(value[:HALF]), jnp.transpose(value[HALF:])], axis=0)

    def pick_lanes(value):
        return jnp.where(first, value[:HALF], value[HALF:])

    for pair in range(HEADS // 2):
        slope = jnp.concatenate(
            [slopes[pair * 2] * spacing[...], slopes[pair * 2 + 1] * spacing[...]], axis=0
        )
        at = [slice(kind * D + pair * PAIR, kind * D + (pair + 1) * PAIR) for kind in range(3)]
        for g in range(2):
            rows = slice(g * HALF, g * HALF + HALF)
            q, k, v = [(qkv_h[rows, cols], qkv_l[rows, cols]) for cols in at]
            gmp = (gm_h[rows, at[0]], gm_l[rows, at[0]])
            scores = dot(both_heads(q), wide(k), NT) - slope
            raised = jnp.exp(scores - jnp.max(scores, axis=1, keepdims=True))
            weights = raised * (1.0 / jnp.sum(raised, axis=1, keepdims=True))
            d_w = dot(both_heads(gmp), wide(v), NT)
            ds = weights * (d_w - jnp.sum(d_w * weights, axis=1, keepdims=True))
            mixed[rows, at[0]] = pick_lanes(dot(left(weights), tall(v)))
            dq = pick_lanes(dot(left(ds), tall(k))) * 0.125
            dk = pick_lanes(dot(left(turned(ds)), tall(q)))
            dv = pick_lanes(dot(left(turned(weights)), tall(gmp)))
            for cols, value in zip(at, (dq, dk, dv)):
                gr_h[rows, cols], gr_l[rows, cols] = split(value)

    def place_columns(block, value):
        for y in YS:
            for side in CS:
                for x in XS:
                    for zh in ZHS:
                        r = y * 128 + zh * 64 + side * 32 + x * 8
                        for half in range(2):
                            grads[y * 2 + side, x, (zh * 8 + block) * 2 + half] = value[
                                r:r + 8, half * 128:half * 128 + 128
                            ]

    normt = split(jnp.transpose(normed))
    for block in range(QKV // 256):
        cols = slice(block * 256, block * 256 + 256)
        place_columns(block, dot3(normt, (gr_h[:, cols], gr_l[:, cols])))
    mixt = split(jnp.transpose(mixed[...]))
    for block in range(2):
        cols = slice(block * 256, block * 256 + 256)
        place_columns(6 + block, dot3(mixt, (og_parts[0][:, cols], og_parts[1][:, cols])))

    gn = dot3((gr_h[...], gr_l[...]), (high[:, :QKV], low[:, :QKV]), NT)
    gain_sum = jnp.sum(gn * emb * scale, axis=0, keepdims=True)
    u = gn * gain[...]
    along = jnp.sum(u * emb, axis=1, keepdims=True) * (scale * scale * scale) * (1.0 / D)
    tokens = og[...] + (u * scale - emb * along)
    total = jnp.zeros((FRAMES, D), f32)
    for p in range(OWN):
        piece = tokens[p * FRAMES:(p + 1) * FRAMES, :]
        for k in range(4):
            tokens_out[pl.ds(k * 8 + p, FRAMES, stride=32), :] = piece[:, k * 128:(k + 1) * 128]
        total = total + piece
    total_h, total_l = split(total)
    table = dot(pick, total_h) + dot(pick, total_l)
    gain_tile = jnp.concatenate(
        [gain_sum[:, i * 128:(i + 1) * 128] for i in range(4)] + [jnp.zeros((4, 128), f32)], axis=0
    )
    for x in XS:
        for side in CS:
            for k in range(8):
                r, start = x * 32 + (k // 2) * 8, side * 256 + (k % 2) * 128
                for y in YS:
                    grads[y * 2 + side, x, 32 + k] = table[r:r + 8, start:start + 128]
            for y in YS:
                grads[y * 2 + side, x, 40] = gain_tile


def call(kernel, outs, scratch, scalars, *arrays, name):
    vmem = pl.BlockSpec(memory_space=pltpu.VMEM)
    smem = pl.BlockSpec(memory_space=pltpu.SMEM)
    return pl.pallas_call(
        kernel,
        out_shape=outs,
        in_specs=[smem] * len(scalars) + [vmem] * len(arrays),
        out_specs=jax.tree.map(lambda _: vmem, outs),
        scratch_shapes=scratch,
        compiler_params=pltpu.CompilerParams(vmem_limit_bytes=48 * 1024 * 1024),
        name=name,
    )(*scalars, *arrays)


def shape(*dims, kind=f32):
    return jax.ShapeDtypeStruct(dims, kind)


def gathered_weights(w_qkv, w_out, x):
    mine = jnp.concatenate([w_qkv, w_out], axis=1)
    own = lax.all_gather(mine, "dp", axis_index_groups=YC_GROUPS)
    quarter = lax.ppermute(lax.dynamic_slice(mine, (x * 8, 0), (8, QKV + D)), "dp", SWAP_ZH)
    return own, quarter


def far_weights(quarter):
    row = jnp.stack([quarter] + [lax.ppermute(quarter, "tm", turn_x(i)) for i in range(1, NX)])
    far = jnp.concatenate([row] + [lax.ppermute(row, "dp", turn_y(i)) for i in range(1, NY)])
    return far, lax.ppermute(far, "dp", SWAP_CORE)


def shards(
    video_tokens, actions, frame_times, act_table, norm_gain, w_qkv, w_out, slopes, out_grad
):
    t, d = lax.axis_index("tm"), lax.axis_index("dp")
    x, y, zh, c = t // NZL, d // (NZH * NC), (d // NC) % NZH, d % NC
    place = jnp.stack([x, y, zh, c]).astype(jnp.int32)

    own, quarter = gathered_weights(w_qkv, w_out, x)
    action = actions[0, 0]
    row = lax.dynamic_slice(act_table, (action, 0), (1, D))
    tag = jnp.broadcast_to(action.astype(f32), (FRAMES, 1, OWN, ACTIONS))
    payload = jnp.concatenate(
        [to_tiles(video_tokens[0, 0] + row), to_tiles(out_grad[0, 0]), tag], axis=1
    )
    quarter, payload = lax.optimization_barrier((quarter, payload))
    tiles = exchange(payload, "tm")
    weights = (own, *far_weights(quarter))

    times = jnp.tile(frame_times[0].astype(f32), HALF // FRAMES)
    i = lax.broadcasted_iota(jnp.int32, (HALF, HALF), 0)
    j = lax.broadcasted_iota(jnp.int32, (HALF, HALF), 1)
    seen = (i // FRAMES == j // FRAMES) & (j <= i)
    spacing = jnp.where(seen, times[:, None] - times[None, :], f32(1e30))

    grads, tokens_back = call(
        sublayer_kernel,
        (shape(NY * NC, NX, TILES, 8, 128), shape(ROWS * 4, 128)),
        [
            pltpu.VMEM((D, QKV + D), bf16), pltpu.VMEM((D, QKV + D), bf16),
            pltpu.VMEM((ROWS, D), f32), pltpu.VMEM((ROWS, D), f32),
            pltpu.VMEM((ROWS, QKV), bf16), pltpu.VMEM((ROWS, QKV), bf16),
            pltpu.VMEM((ROWS, D), bf16), pltpu.VMEM((ROWS, D), bf16),
            pltpu.VMEM((ROWS, D), f32),
            pltpu.VMEM((ROWS, QKV), bf16), pltpu.VMEM((ROWS, QKV), bf16),
        ],
        (place, slopes),
        tiles.reshape(ROWS * 9, 128), norm_gain.reshape(1, D), *weights, spacing,
        name="sublayer",
    )
    grad_tokens = exchange(tokens_back.reshape(FRAMES, 4, OWN, 128), "tm")

    row = lax.psum_scatter(
        grads, "dp", scatter_dimension=0, axis_index_groups=YC_GROUPS, tiled=True
    ).reshape(NX, TILES, 8, 128)
    row, grad_tokens = lax.optimization_barrier((row, grad_tokens))
    plane = jnp.sum(exchange(row, "tm", X_GROUPS), axis=0)
    column = jnp.concatenate(
        [
            plane[:32].reshape(16, 2, 8, 128),
            jnp.tile(plane[32:40], (2, 1, 1)).reshape(16, 1, 8, 128),
            jnp.broadcast_to(plane[40:], (16, 1, 8, 128)),
        ],
        axis=1,
    )
    total = jnp.sum(exchange(column, BOTH, Z_GROUPS), axis=0)

    line = exchange(jnp.broadcast_to(total[:3], (NZL, 3, 8, 128)), "tm", ZL_GROUPS)
    sheet = exchange(jnp.broadcast_to(line, (NX, NZL, 3, 8, 128)), "tm", X_GROUPS)
    main = sheet[:, :, :2].transpose(0, 3, 1, 2, 4).reshape(32, QKV + D)
    half = sheet[:, :, 2].reshape(NX, 4, 2, 8, 128).transpose(0, 1, 3, 2, 4).reshape(ACTIONS, 256)
    other = lax.ppermute(half, "dp", SWAP_CORE)
    grad_table = jnp.where(
        c == 0, jnp.concatenate([half, other], axis=1), jnp.concatenate([other, half], axis=1)
    )
    return (
        grad_tokens.transpose(0, 2, 1, 3).reshape(1, 1, ROWS, D),
        main[:, :QKV],
        main[:, QKV:],
        grad_table,
        total[3, :4].reshape(D),
    )


def solution(mesh):
    return jax.shard_map(
        shards,
        mesh=mesh,
        in_specs=(
            P("dp", "tm", None, None),
            P("dp", "tm"),
            P("dp", None),
            P(),
            P(),
            P("dp", None),
            P("dp", None),
            P(),
            P("dp", "tm", None, None),
        ),
        out_specs=(P("dp", "tm", None, None), P("dp", None), P("dp", None), P(), P()),
        check_vma=False,
    )
```

time: 1490 us -> 245 us (0.16); the launches traced: 1460 us -> 244 us
  waiting for transfers between devices: 1250 us -> 46.9 us
  matrix products: 34.4 us -> 0 us
  starting transfers between devices: 26.7 us -> 58.7 us
    psum x2 -> x0, waiting for transfers between devices: 783 us -> none  [the longest x1 429 us: shards(): qkv_share, out_share = lax.psum((qkv_share, out_share), 'tm')]
    all_gather x2 -> x1, waiting for transfers between devices: 209 us -> 0.01 us  [gathered_weights(): own = lax.all_gather(mine, 'dp', axis_index_groups=YC_GROUPS)]
    reduce_scatter x2 -> x1, waiting for transfers between devices: 155 us -> 7.82 us  [shards(): lax.psum_scatter(grads, 'dp', scatter_dimension=0, axis_index_groups=YC_G...]
    psum x1 -> x0, blocking collectives: 101 us -> none  [shards(): grad_table, grad_gain = lax.psum((grad_table, grad_gain), ('tm', 'dp'))]
    all_to_all x0 -> x4, blocking collectives: none -> 95.2 us  [exchange(): lax.all_to_all(value, axis, 0, 0, axis_index_groups=groups, tiled=True)]
    all_to_all x4 -> x2, waiting for transfers between devices: 104 us -> 15.5 us  [exchange(): lax.all_to_all(value, axis, 0, 0, axis_index_groups=groups, tiled=True)]
    ppermute x0 -> x9, starting transfers between devices: none -> 42 us  [the longest x1 15.4 us: gathered_weights(): lax.ppermute(lax.dynamic_slice(mine, (x * 8, 0), (8, QKV + D)), 'dp', SWA...]
    dot_general x12 -> x0, matrix products: 34.4 us -> none  [the longest x3 14.2 us: project(): return jnp.einsum('cfpd,de->cfpe', token_rows, matrix, precision=precise)]
  transfers between devices with their start and end apart: 10 -> 13, of which waited for: 9 -> 7; matrix products, arithmetic and copies ran while one was open for 4% -> 2% of each run, Pallas kernels for 0% -> 0%
where the time goes in v2:
time: 245 us; the launch traced here: 244 us
  blocking collectives  95.2 us (39%)
  starting transfers between devices  58.7 us (24%)
  waiting for transfers between devices  46.9 us (19%)
  between operations  15.1 us (6%)
  Pallas kernels  14.1 us (6%)
  local copies, waits for them, and re-layouts  9.92 us (4%)
  other arithmetic  3.95 us (2%)
    all_to_all x4, blocking collectives, exchange(): lax.all_to_all(value, axis, 0, 0, axis_index_groups=groups, tiled=True)  95.2 us
    ppermute x3, waiting for transfers between devices, far_weights(): lax.ppermute(row, 'dp', turn_y(i))  16.7 us
    all_to_all x2, starting transfers between devices, exchange(): lax.all_to_all(value, axis, 0, 0, axis_index_groups=groups, tiled=True)  16.7 us
    all_to_all x2, waiting for transfers between devices, exchange(): lax.all_to_all(value, axis, 0, 0, axis_index_groups=groups, tiled=True)  15.5 us
    ppermute x1, starting transfers between devices, gathered_weights(): lax.ppermute(lax.dynamic_slice(mine, (x * 8, 0), (8, QKV + D)), 'dp', SWA...  15.4 us
    pallas_call x1, Pallas kernels, call(): pl.pallas_call(kernel, out_shape=outs, in_specs=[smem] * len(scalars) + [...  14.1 us
    ppermute x3, starting transfers between devices, far_weights(): lax.ppermute(quarter, 'tm', turn_x(i))  9.33 us
    ppermute x3, starting transfers between devices, far_weights(): lax.ppermute(row, 'dp', turn_y(i))  8.75 us
  transfers between devices with their start and end apart: 13, of which 7 were waited for; matrix products, arithmetic and copies ran while one was open for 2% of the time, Pallas kernels for 0%

profile of v2, /device:TPU:25, one launch (start us, length us, event | category | flops | bytes accessed | tf_op | source)
XLA Modules:
  0.0 243.9 jit_solution(1747961654146279631)
XLA Ops:
  7.2 1.0 constant_dynamic-update-slice_fusion.1
  8.2 0.8 constant_dynamic-update-slice_fusion
  9.1 15.4 %collective-permute-start = (f32[8,2048]{1,0:T(8,128)S(1)}, f32[8,2048]{1,0:T(8,128)S(1)}, u32[]{:S(2)}, u32[]{:S(2)}) collective-permute-start(f32[8,2048]{1,0:T(8,128)S(1)} %constant_dynamic-slice_fusion.1), channel_id=1, source_target_pairs={{0,2},{1,3},{2,0},{3,1},{4,6},{5,7},{6,4},{7,5},{8,10},{9,11},{10,... | collective-permute-start | bytes 196616 | tf_op jit(solution)/shard_map/ppermute | solution.py:246
  25.3 1.1 fusion
  26.4 1.2 maximum_maximum_fusion
  27.6 13.2 %all-to-all-start = ((f32[32,9,8,128]{3,2,1,0:T(8,128)}), f32[32,9,8,128]{3,2,1,0:T(8,128)S(1)}, u32[]{:S(2)}, u32[]{:S(2)}) async-start(f32[32,9,8,128]{3,2,1,0:T(8,128)} %maximum_maximum_fusion), calls=%async_computation | async-start | bytes 2359296 | tf_op jit(solution)/shard_map/all_to_all | solution.py:53
  41.5 4.4 %collective-permute-start.3 = (f32[8,2048]{1,0:T(8,128)S(1)}, f32[8,2048]{1,0:T(8,128)S(1)}, u32[]{:S(2)}, u32[]{:S(2)}) collective-permute-start(f32[8,2048]{1,0:T(8,128)S(1)} %collective-permute-done), channel_id=1, source_target_pairs={{0,384},{16,400},{32,416},{48,432},{64,448},{80,464},{96,480},{112... | collective-permute-start | bytes 196616 | tf_op jit(solution)/shard_map/ppermute | solution.py:251
  46.0 2.4 %collective-permute-start.2 = (f32[8,2048]{1,0:T(8,128)S(1)}, f32[8,2048]{1,0:T(8,128)S(1)}, u32[]{:S(2)}, u32[]{:S(2)}) collective-permute-start(f32[8,2048]{1,0:T(8,128)S(1)} %collective-permute-done), channel_id=1, source_target_pairs={{0,256},{16,272},{32,288},{48,304},{64,320},{80,336},{96,352},{112... | collective-permute-start | bytes 196616 | tf_op jit(solution)/shard_map/ppermute | solution.py:251
  48.4 2.5 %collective-permute-start.1 = (f32[8,2048]{1,0:T(8,128)S(1)}, f32[8,2048]{1,0:T(8,128)S(1)}, u32[]{:S(2)}, u32[]{:S(2)}) collective-permute-start(f32[8,2048]{1,0:T(8,128)S(1)} %collective-permute-done), channel_id=1, source_target_pairs={{0,128},{16,144},{32,160},{48,176},{64,192},{80,208},{96,224},{112... | collective-permute-start | bytes 196616 | tf_op jit(solution)/shard_map/ppermute | solution.py:251
  50.9 1.9 collective-permute-done.2
  52.8 3.1 %collective-permute-done.1 = f32[8,2048]{1,0:T(8,128)S(1)} collective-permute-done((f32[8,2048]{1,0:T(8,128)S(1)}, f32[8,2048]{1,0:T(8,128)S(1)}, u32[]{:S(2)}, u32[]{:S(2)}) %collective-permute-start.1) | collective-permute-done | bytes 65568 | tf_op jit(solution)/shard_map/ppermute | solution.py:251
  55.9 2.4 collective-permute-start.6
  58.3 2.6 %collective-permute-start.5 = (f32[4,8,2048]{2,1,0:T(8,128)S(1)}, f32[4,8,2048]{2,1,0:T(8,128)S(1)}, u32[]{:S(2)}, u32[]{:S(2)}) collective-permute-start(f32[4,8,2048]{2,1,0:T(8,128)S(1)} %pad_maximum_fusion), channel_id=1, source_target_pairs={{0,8},{1,9},{2,10},{3,11},{4,12},{5,13},{6,14},{7,15},{8,0},{9,1},... | collective-permute-start | bytes 786440 | tf_op jit(solution)/shard_map/ppermute | solution.py:252
  60.9 3.8 %collective-permute-start.4 = (f32[4,8,2048]{2,1,0:T(8,128)S(1)}, f32[4,8,2048]{2,1,0:T(8,128)S(1)}, u32[]{:S(2)}, u32[]{:S(2)}) collective-permute-start(f32[4,8,2048]{2,1,0:T(8,128)S(1)} %pad_maximum_fusion), channel_id=1, source_target_pairs={{0,4},{1,5},{2,6},{3,7},{4,8},{5,9},{6,10},{7,11},{8,12},{9,13},{1... | collective-permute-start | bytes 786440 | tf_op jit(solution)/shard_map/ppermute | solution.py:252
  64.7 16.7 %collective-permute-done.4 = f32[4,8,2048]{2,1,0:T(8,128)S(1)} collective-permute-done((f32[4,8,2048]{2,1,0:T(8,128)S(1)}, f32[4,8,2048]{2,1,0:T(8,128)S(1)}, u32[]{:S(2)}, u32[]{:S(2)}) %collective-permute-start.4) | collective-permute-done | bytes 262176 | tf_op jit(solution)/shard_map/ppermute | solution.py:252
  81.6 3.3 %collective-permute-start.7 = (f32[16,8,2048]{2,1,0:T(8,128)S(1)}, f32[16,8,2048]{2,1,0:T(8,128)S(1)}, u32[]{:S(2)}, u32[]{:S(2)}) collective-permute-start(f32[16,8,2048]{2,1,0:T(8,128)S(1)} %constant_dynamic-update-slice_fusion.2.far_mine), channel_id=1, source_target_pairs={{0,1},{1,0},{2,3},{3,2},{4,5},{5,4},{6,7},{7,6},{8,9},{9,8},{10,11... | collective-permute-start | bytes 3145736 | tf_op jit(solution)/shard_map/ppermute | solution.py:253
  85.9 1.2 collective-permute-done.7.far_other
  87.1 9.3 %all-to-all-done = f32[32,9,8,128]{3,2,1,0:T(8,128)S(1)} async-done(((f32[32,9,8,128]{3,2,1,0:T(8,128)}), f32[32,9,8,128]{3,2,1,0:T(8,128)S(1)}, u32[]{:S(2)}, u32[]{:S(2)}) %all-to-all-start) | async-done | bytes 1179680 | tf_op jit(solution)/shard_map/all_to_all | solution.py:53
  96.4 1.6 copy-done.1
  98.0 0.8 copy-done.4
  98.9 14.1 %sublayer.1 = (f32[8,4,41,8,128]{4,3,2,1,0:T(8,128)}, f32[1024,128]{1,0:T(8,128)S(1)}) custom-call(s32[4]{0:T(128)S(1)} %pad_add_fusion.place, f32[8]{0:T(128)S(1)} %copy-done.6, f32[2304,128]{1,0:T(8,128)S(1)} %bitcast.52, f32[1,512]{1,0:T(1,128)S(1)} %bitcast.55, f32[8,32,2048]{2,1,0:T(8,128)S(1)} %bitcast.53, ...), custom_call_target="tpu_custom_call" | custom-call | tf_op jit(solution)/shard_map/sublayer/pallas_call | solution.py:228
  113.0 0.8 copy-done.2
  113.8 1.0 copy-done.3
  114.8 35.9 %all_to_all.30 = f32[32,4,8,128]{3,2,1,0:T(8,128)S(1)} all-to-all(f32[32,4,8,128]{3,2,1,0:T(8,128)S(1)} %bitcast.54), channel_id=1, replica_groups=mesh['tm'=32,'dp'=16] {'tm'}, dimensions={0} | all-to-all | bytes 1048576 | tf_op jit(solution)/shard_map/all_to_all | solution.py:53
  150.8 7.8 %reduce-scatter.2.cloned.1.call-done = f32[1,4,41,8,128]{4,3,2,1,0:T(8,128)} async-done(((f32[8,4,41,8,128]{4,3,2,1,0:T(8,128)}), f32[1,4,41,8,128]{4,3,2,1,0:T(8,128)}) %reduce-scatter.2.cloned.1.call-update) | async-done | bytes 671760 | tf_op jit(solution)/shard_map/reduce_scatter | solution.py:297
  158.6 13.3 %all_to_all.31 = f32[4,41,8,128]{3,2,1,0:T(8,128)S(1)} all-to-all(f32[4,41,8,128]{3,2,1,0:T(8,128)} %bitcast.59), channel_id=1, replica_groups={{0,128,256,384},{16,144,272,400},{32,160,288,416},{48,176,304,432},{64,..., dimensions={0} | all-to-all | bytes 1343488 | tf_op jit(solution)/shard_map/all_to_all | solution.py:53
  172.0 29.0 %all_to_all.32 = f32[16,4,8,128]{3,2,1,0:T(8,128)S(1)} all-to-all(f32[16,4,8,128]{3,2,1,0:T(8,128)S(1)} %pad_maximum_fusion.1), channel_id=1, replica_groups={{0,16,32,48,64,80,96,112,2,18,34,50,66,82,98,114},{1,17,33,49,65,81,97,..., dimensions={0} | all-to-all | bytes 524288 | tf_op jit(solution)/shard_map/all_to_all | solution.py:53
  201.1 17.0 %all_to_all.33 = f32[8,3,8,128]{3,2,1,0:T(8,128)S(1)} all-to-all(f32[8,3,8,128]{3,2,1,0:T(8,128)S(1)} %broadcast_in_dim.19), channel_id=1, replica_groups={{0,16,32,48,64,80,96,112},{128,144,160,176,192,208,224,240},{256,272,28..., dimensions={0} | all-to-all | bytes 196608 | tf_op jit(solution)/shard_map/all_to_all | solution.py:53
  218.8 3.5 %all-to-all-start.5 = ((f32[4,8,3,8,128]{4,3,2,1,0:T(8,128)}), f32[4,8,3,8,128]{4,3,2,1,0:T(8,128)S(1)}, u32[]{:S(2)}, u32[]{:S(2)}) async-start(f32[4,8,3,8,128]{4,3,2,1,0:T(8,128)} %broadcast_in_dim.20), calls=%async_computation.6 | async-start | bytes 786432 | tf_op jit(solution)/shard_map/all_to_all | solution.py:53
  222.3 6.2 %all-to-all-done.5 = f32[4,8,3,8,128]{4,3,2,1,0:T(8,128)S(1)} async-done(((f32[4,8,3,8,128]{4,3,2,1,0:T(8,128)}), f32[4,8,3,8,128]{4,3,2,1,0:T(8,128)S(1)}, u32[]{:S(2)}, u32[]{:S(2)}) %all-to-all-start.5) | async-done | bytes 393248 | tf_op jit(solution)/shard_map/all_to_all | solution.py:53
  228.5 5.1 %collective-permute-start.8 = (f32[128,256]{1,0:T(8,128)S(1)}, f32[128,256]{1,0:T(8,128)S(1)}, u32[]{:S(2)}, u32[]{:S(2)}) collective-permute-start(f32[128,256]{1,0:T(8,128)S(1)} %bitcast.61), channel_id=1, source_target_pairs={{0,1},{1,0},{2,3},{3,2},{4,5},{5,4},{6,7},{7,6},{8,9},{9,8},{10,11... | collective-permute-start | bytes 393224 | tf_op jit(solution)/shard_map/ppermute | solution.py:316
  236.3 0.8 copy.23
  (61 shorter events, 5.5 us)
Async XLA Ops:
  7.2 18.1 %copy-start = (f32[128,512]{1,0:T(8,128)S(1)}, f32[128,512]{1,0:T(8,128)}, u32[]{:S(2)}) copy-start(f32[128,512]{1,0:T(8,128)} %param.12) | copy-start | bytes 786436
  7.2 19.2 %copy-start.8 = (f32[1,1,256,512]{3,2,1,0:T(8,128)S(1)}, f32[1,1,256,512]{3,2,1,0:T(8,128)}, u32[]{:S(2)}) copy-start(f32[1,1,256,512]{3,2,1,0:T(8,128)} %param.17) | copy-start | bytes 1572868
  9.1 18.5 %copy-start.7 = (f32[32,2048]{1,0:T(8,128)}, f32[32,2048]{1,0:T(8,128)S(1)}, u32[]{:S(2)}) copy-start(f32[32,2048]{1,0:T(8,128)S(1)} %constant_dynamic-update-slice_fusion) | copy-start | bytes 786436
  9.1 18.5 %collective-permute-start = (f32[8,2048]{1,0:T(8,128)S(1)}, f32[8,2048]{1,0:T(8,128)S(1)}, u32[]{:S(2)}, u32[]{:S(2)}) collective-permute-start(f32[8,2048]{1,0:T(8,128)S(1)} %constant_dynamic-slice_fusion.1), channel_id=1, source_target_pairs={{0,2},{1,3},{2,0},{3,1},{4,6},{5,7},{6,4},{7,5},{8,10},{9,11},{10,... | collective-permute-start | bytes 196616 | tf_op jit(solution)/shard_map/ppermute | solution.py:246
  27.6 68.9 %all-to-all-start = ((f32[32,9,8,128]{3,2,1,0:T(8,128)}), f32[32,9,8,128]{3,2,1,0:T(8,128)S(1)}, u32[]{:S(2)}, u32[]{:S(2)}) async-start(f32[32,9,8,128]{3,2,1,0:T(8,128)} %maximum_maximum_fusion), calls=%async_computation | async-start | bytes 2359296 | tf_op jit(solution)/shard_map/all_to_all | solution.py:53
  40.8 46.4 %all-gather.3.cloned.1.call-start = ((), (), s32[]{:S(2)}) async-start(), calls=%async_computation.8 | async-start | bytes 2359296 | tf_op jit(solution)/shard_map/all_gather | solution.py:245
  41.5 117.1 %reduce-scatter.2.cloned.1.call-start = ((), (), s32[]{:S(2)}) async-start(), calls=%async_computation.7 | async-start | bytes 6045696 | tf_op jit(solution)/shard_map/reduce_scatter | solution.py:297
  41.5 9.4 %collective-permute-start.3 = (f32[8,2048]{1,0:T(8,128)S(1)}, f32[8,2048]{1,0:T(8,128)S(1)}, u32[]{:S(2)}, u32[]{:S(2)}) collective-permute-start(f32[8,2048]{1,0:T(8,128)S(1)} %collective-permute-done), channel_id=1, source_target_pairs={{0,384},{16,400},{32,416},{48,432},{64,448},{80,464},{96,480},{112... | collective-permute-start | bytes 196616 | tf_op jit(solution)/shard_map/ppermute | solution.py:251
  46.0 6.8 %collective-permute-start.2 = (f32[8,2048]{1,0:T(8,128)S(1)}, f32[8,2048]{1,0:T(8,128)S(1)}, u32[]{:S(2)}, u32[]{:S(2)}) collective-permute-start(f32[8,2048]{1,0:T(8,128)S(1)} %collective-permute-done), channel_id=1, source_target_pairs={{0,256},{16,272},{32,288},{48,304},{64,320},{80,336},{96,352},{112... | collective-permute-start | bytes 196616 | tf_op jit(solution)/shard_map/ppermute | solution.py:251
  48.4 7.5 %collective-permute-start.1 = (f32[8,2048]{1,0:T(8,128)S(1)}, f32[8,2048]{1,0:T(8,128)S(1)}, u32[]{:S(2)}, u32[]{:S(2)}) collective-permute-start(f32[8,2048]{1,0:T(8,128)S(1)} %collective-permute-done), channel_id=1, source_target_pairs={{0,128},{16,144},{32,160},{48,176},{64,192},{80,208},{96,224},{112... | collective-permute-start | bytes 196616 | tf_op jit(solution)/shard_map/ppermute | solution.py:251
  55.9 29.0 %copy-start.9 = (s32[1,32]{1,0:T(1,128)S(1)}, s32[1,32]{1,0:T(1,128)}, u32[]{:S(2)}) copy-start(s32[1,32]{1,0:T(1,128)} %param.11) | copy-start | bytes 388
  55.9 40.5 %copy-start.5 = (f32[512]{0:T(512)S(1)}, f32[512]{0:T(512)}, u32[]{:S(2)}) copy-start(f32[512]{0:T(512)} %param.13) | copy-start | bytes 6148
  55.9 40.5 %copy-start.6 = (f32[8]{0:T(128)S(1)}, f32[8]{0:T(128)}, u32[]{:S(2)}) copy-start(f32[8]{0:T(128)} %slopes.1) | copy-start | bytes 100
  55.9 25.6 %collective-permute-start.6 = (f32[4,8,2048]{2,1,0:T(8,128)S(1)}, f32[4,8,2048]{2,1,0:T(8,128)S(1)}, u32[]{:S(2)}, u32[]{:S(2)}) collective-permute-start(f32[4,8,2048]{2,1,0:T(8,128)S(1)} %pad_maximum_fusion), channel_id=1, source_target_pairs={{0,12},{1,13},{2,14},{3,15},{4,0},{5,1},{6,2},{7,3},{8,4},{9,5},{1... | collective-permute-start | bytes 786440 | tf_op jit(solution)/shard_map/ppermute | solution.py:252
  58.3 23.2 %collective-permute-start.5 = (f32[4,8,2048]{2,1,0:T(8,128)S(1)}, f32[4,8,2048]{2,1,0:T(8,128)S(1)}, u32[]{:S(2)}, u32[]{:S(2)}) collective-permute-start(f32[4,8,2048]{2,1,0:T(8,128)S(1)} %pad_maximum_fusion), channel_id=1, source_target_pairs={{0,8},{1,9},{2,10},{3,11},{4,12},{5,13},{6,14},{7,15},{8,0},{9,1},... | collective-permute-start | bytes 786440 | tf_op jit(solution)/shard_map/ppermute | solution.py:252
  60.9 20.6 %collective-permute-start.4 = (f32[4,8,2048]{2,1,0:T(8,128)S(1)}, f32[4,8,2048]{2,1,0:T(8,128)S(1)}, u32[]{:S(2)}, u32[]{:S(2)}) collective-permute-start(f32[4,8,2048]{2,1,0:T(8,128)S(1)} %pad_maximum_fusion), channel_id=1, source_target_pairs={{0,4},{1,5},{2,6},{3,7},{4,8},{5,9},{6,10},{7,11},{8,12},{9,13},{1... | collective-permute-start | bytes 786440 | tf_op jit(solution)/shard_map/ppermute | solution.py:252
  81.6 5.6 %collective-permute-start.7 = (f32[16,8,2048]{2,1,0:T(8,128)S(1)}, f32[16,8,2048]{2,1,0:T(8,128)S(1)}, u32[]{:S(2)}, u32[]{:S(2)}) collective-permute-start(f32[16,8,2048]{2,1,0:T(8,128)S(1)} %constant_dynamic-update-slice_fusion.2.far_mine), channel_id=1, source_target_pairs={{0,1},{1,0},{2,3},{3,2},{4,5},{5,4},{6,7},{7,6},{8,9},{9,8},{10,11... | collective-permute-start | bytes 3145736 | tf_op jit(solution)/shard_map/ppermute | solution.py:253
  96.4 1.6 copy-start.1
  98.0 0.8 copy-start.4
  113.0 0.8 copy-start.2
  113.8 1.0 copy-start.3
  218.8 9.7 %all-to-all-start.5 = ((f32[4,8,3,8,128]{4,3,2,1,0:T(8,128)}), f32[4,8,3,8,128]{4,3,2,1,0:T(8,128)S(1)}, u32[]{:S(2)}, u32[]{:S(2)}) async-start(f32[4,8,3,8,128]{4,3,2,1,0:T(8,128)} %broadcast_in_dim.20), calls=%async_computation.6 | async-start | bytes 786432 | tf_op jit(solution)/shard_map/all_to_all | solution.py:53
  228.5 7.1 %collective-permute-start.8 = (f32[128,256]{1,0:T(8,128)S(1)}, f32[128,256]{1,0:T(8,128)S(1)}, u32[]{:S(2)}, u32[]{:S(2)}) collective-permute-start(f32[128,256]{1,0:T(8,128)S(1)} %bitcast.61), channel_id=1, source_target_pairs={{0,1},{1,0},{2,3},{3,2},{4,5},{5,4},{6,7},{7,6},{8,9},{9,8},{10,11... | collective-permute-start | bytes 393224 | tf_op jit(solution)/shard_map/ppermute | solution.py:316
Sparse Core Ops, SparseCore 0:
  44.3 38.6 all-gather.2
  114.0 44.5 reduce-scatter.1

commit v3 on v2

--- a/solution.py
+++ b/solution.py
@@ -14,6 +14,7 @@
 PAIR = 2 * HEAD
 ACTIONS = 128
 TILES = 41
+CHUNK = 65
 f32, bf16 = jnp.float32, jnp.bfloat16
 BOTH = ("tm", "dp")
 
@@ -74,20 +75,30 @@
     for p in range(OWN):
         for k in range(4):
             rows[p * FRAMES:(p + 1) * FRAMES, k * 128:(k + 1) * 128] = tiles[
-                pl.ds((start + k) * 8 + p, FRAMES, stride=72), :
+                pl.ds((start + k) * 8 + p, FRAMES, stride=CHUNK), :
             ]
 
 
-def to_tiles(rows):
-    return rows.reshape(FRAMES, OWN, D // 128, 128).transpose(0, 2, 1, 3)
-
-
-def head_masks():
-    lane = lax.broadcasted_iota(jnp.int32, (HALF, PAIR), 1)
-    return lane < HEAD
-
-
-def gather_weights(place, own, far_mine, far_other, high, low):
+def pack_kernel(action, row, video_in, og_in, out, video, og, sems):
+    arrivals = [
+        pltpu.make_async_copy(source, target, sems.at[i])
+        for i, (source, target) in enumerate(((video_in, video), (og_in, og)))
+    ]
+    for copy in arrivals:
+        copy.start()
+    for copy in arrivals:
+        copy.wait()
+    tag = jnp.zeros((1, 128), f32) + action[0].astype(f32)
+    for f in range(FRAMES):
+        rows = slice(f * OWN, f * OWN + OWN)
+        for k in range(D // 128):
+            cols = slice(k * 128, k * 128 + 128)
+            out[f * CHUNK + k * 8:f * CHUNK + k * 8 + 8, :] = video[rows, cols] + row[:, cols]
+            out[f * CHUNK + 32 + k * 8:f * CHUNK + 40 + k * 8, :] = og[rows, cols]
+        out[f * CHUNK + 64:f * CHUNK + 65, :] = tag
+
+
+def weights_kernel(place, own, far_mine, far_other, high, low):
     x, y, zh, c = place[0], place[1], place[2], place[3]
     for y_to in YS:
         for side in CS:
@@ -104,15 +115,20 @@
 
 
 def sublayer_kernel(
-    place, slopes, tiles, gain, own, far_mine, far_other, spacing,
-    grads, tokens_out,
-    high, low, emb_ref, og, qkv_h, qkv_l, gm_h, gm_l, mixed, gr_h, gr_l,
+    slopes, tiles, gain, spacing, high_in, low_in,
+    grads_out, tokens_out,
+    grads, tokens_new, sems, high, low, emb_ref, og, qkv_h, qkv_l, gm_h, gm_l, mixed, gr_h, gr_l,
 ):
+    arrivals = [
+        pltpu.make_async_copy(source, target, sems.at[18 + i])
+        for i, (source, target) in enumerate(((high_in, high), (low_in, low)))
+    ]
+    for copy in arrivals:
+        copy.start()
     take_rows(tiles, emb_ref, 0)
     take_rows(tiles, og, 4)
-    gather_weights(place, own, far_mine, far_other, high, low)
-
-    tags = tiles[pl.ds(64, FRAMES, stride=72), :]
+
+    tags = tiles[pl.ds(64, FRAMES, stride=CHUNK), :]
     ids = lax.broadcasted_iota(jnp.int32, (FRAMES, ACTIONS), 1).astype(f32)
     pick = jnp.transpose((tags == ids).astype(f32)).astype(bf16)
 
@@ -120,6 +136,8 @@
     scale = lax.rsqrt(jnp.mean(emb * emb, axis=1, keepdims=True) + 1e-06)
     normed = emb * gain[...] * scale
     parts = split(normed)
+    for copy in arrivals:
+        copy.wait()
     for block in range(QKV // 256):
         cols = slice(block * 256, block * 256 + 256)
         value = dot3(parts, (high[:, cols], low[:, cols]))
@@ -176,6 +194,16 @@
             for cols, value in zip(at, (dq, dk, dv)):
                 gr_h[rows, cols], gr_l[rows, cols] = split(value)
 
+    def copy_tiles(tile, count, index):
+        part = (slice(None), slice(None), pl.ds(tile, count))
+        return pltpu.make_async_copy(grads.at[part], grads_out.at[part], sems.at[index])
+
+    copies = []
+
+    def send_tiles(tile, count, index):
+        copies.append(copy_tiles(tile, count, index))
+        copies[-1].start()
+
     def place_columns(block, value):
         for y in YS:
             for side in CS:
@@ -186,6 +214,8 @@
                             grads[y * 2 + side, x, (zh * 8 + block) * 2 + half] = value[
                                 r:r + 8, half * 128:half * 128 + 128
                             ]
+        for zh in ZHS:
+            send_tiles((zh * 8 + block) * 2, 2, block * 2 + zh)
 
     normt = split(jnp.transpose(normed))
     for block in range(QKV // 256):
@@ -205,12 +235,16 @@
     for p in range(OWN):
         piece = tokens[p * FRAMES:(p + 1) * FRAMES, :]
         for k in range(4):
-            tokens_out[pl.ds(k * 8 + p, FRAMES, stride=32), :] = piece[:, k * 128:(k + 1) * 128]
+            tokens_new[pl.ds(k * 8 + p, FRAMES, stride=32), :] = piece[:, k * 128:(k + 1) * 128]
         total = total + piece
+    copies.append(pltpu.make_async_copy(tokens_new, tokens_out, sems.at[17]))
+    copies[-1].start()
     total_h, total_l = split(total)
     table = dot(pick, total_h) + dot(pick, total_l)
     gain_tile = jnp.concatenate(
-        [gain_sum[:, i * 128:(i + 1) * 128] for i in range(4)] + [jnp.zeros((4, 128), f32)], axis=0
+        [gain_sum[:, i * 64:(i + 1) * 64] for i in range(8)], axis=0
+    )
+    gain_tile = jnp.concatenate([gain_tile, jnp.zeros((8, 64), f32)], axis=1
     )
     for x in XS:
         for side in CS:
@@ -220,18 +254,22 @@
                     grads[y * 2 + side, x, 32 + k] = table[r:r + 8, start:start + 128]
             for y in YS:
                 grads[y * 2 + side, x, 40] = gain_tile
-
-
-def call(kernel, outs, scratch, scalars, *arrays, name):
+    send_tiles(32, 9, 16)
+    for copy in copies:
+        copy.wait()
+
+
+def call(kernel, outs, scratch, scalars, *arrays, name, far_ins=0, far_outs=0, limit=24):
     vmem = pl.BlockSpec(memory_space=pltpu.VMEM)
     smem = pl.BlockSpec(memory_space=pltpu.SMEM)
+    hbm = pl.BlockSpec(memory_space=pltpu.HBM)
     return pl.pallas_call(
         kernel,
         out_shape=outs,
-        in_specs=[smem] * len(scalars) + [vmem] * len(arrays),
-        out_specs=jax.tree.map(lambda _: vmem, outs),
+        in_specs=[smem] * len(scalars) + [vmem] * (len(arrays) - far_ins) + [hbm] * far_ins,
+        out_specs=[hbm] * far_outs + [vmem] * (len(outs) - far_outs),
         scratch_shapes=scratch,
-        compiler_params=pltpu.CompilerParams(vmem_limit_bytes=48 * 1024 * 1024),
+        compiler_params=pltpu.CompilerParams(vmem_limit_bytes=limit * 1024 * 1024),
         name=name,
     )(*scalars, *arrays)
 
@@ -243,14 +281,18 @@
 def gathered_weights(w_qkv, w_out, x):
     mine = jnp.concatenate([w_qkv, w_out], axis=1)
     own = lax.all_gather(mine, "dp", axis_index_groups=YC_GROUPS)
-    quarter = lax.ppermute(lax.dynamic_slice(mine, (x * 8, 0), (8, QKV + D)), "dp", SWAP_ZH)
+    quarter = jnp.concatenate(
+        [lax.dynamic_slice(w, (x * 8, 0), (8, w.shape[1])) for w in (w_qkv, w_out)], axis=1
+    )
+    quarter = lax.ppermute(quarter, "dp", SWAP_ZH)
     return own, quarter
 
 
-def far_weights(quarter):
+def far_weights(own, quarter):
     row = jnp.stack([quarter] + [lax.ppermute(quarter, "tm", turn_x(i)) for i in range(1, NX)])
+    row, own = lax.optimization_barrier((row, own))
     far = jnp.concatenate([row] + [lax.ppermute(row, "dp", turn_y(i)) for i in range(1, NY)])
-    return far, lax.ppermute(far, "dp", SWAP_CORE)
+    return own, far, lax.ppermute(far, "dp", SWAP_CORE)
 
 
 def shards(
@@ -263,13 +305,24 @@
     own, quarter = gathered_weights(w_qkv, w_out, x)
     action = actions[0, 0]
     row = lax.dynamic_slice(act_table, (action, 0), (1, D))
-    tag = jnp.broadcast_to(action.astype(f32), (FRAMES, 1, OWN, ACTIONS))
-    payload = jnp.concatenate(
-        [to_tiles(video_tokens[0, 0] + row), to_tiles(out_grad[0, 0]), tag], axis=1
-    )
+    payload = call(
+        pack_kernel,
+        [shape(FRAMES * CHUNK, 128)],
+        [pltpu.VMEM((ROWS, D), f32), pltpu.VMEM((ROWS, D), f32), pltpu.SemaphoreType.DMA((2,))],
+        (action.reshape(1),),
+        row, video_tokens[0, 0], out_grad[0, 0],
+        name="pack", far_ins=2,
+    )[0]
     quarter, payload = lax.optimization_barrier((quarter, payload))
-    tiles = exchange(payload, "tm")
-    weights = (own, *far_weights(quarter))
+    high, low = call(
+        weights_kernel,
+        [shape(D, QKV + D, kind=bf16), shape(D, QKV + D, kind=bf16)],
+        [],
+        (place,),
+        *far_weights(own, quarter),
+        name="weights",
+    )
+    tiles = exchange(payload.reshape(FRAMES, CHUNK, 1, 128), "tm")
 
     times = jnp.tile(frame_times[0].astype(f32), HALF // FRAMES)
     i = lax.broadcasted_iota(jnp.int32, (HALF, HALF), 0)
@@ -279,8 +332,10 @@
 
     grads, tokens_back = call(
         sublayer_kernel,
-        (shape(NY * NC, NX, TILES, 8, 128), shape(ROWS * 4, 128)),
+        [shape(NY * NC, NX, TILES, 8, 128), shape(ROWS * 4, 128)],
         [
+            pltpu.VMEM((NY * NC, NX, TILES, 8, 128), f32), pltpu.VMEM((ROWS * 4, 128), f32),
+            pltpu.SemaphoreType.DMA((20,)),
             pltpu.VMEM((D, QKV + D), bf16), pltpu.VMEM((D, QKV + D), bf16),
             pltpu.VMEM((ROWS, D), f32), pltpu.VMEM((ROWS, D), f32),
             pltpu.VMEM((ROWS, QKV), bf16), pltpu.VMEM((ROWS, QKV), bf16),
@@ -288,9 +343,9 @@
             pltpu.VMEM((ROWS, D), f32),
             pltpu.VMEM((ROWS, QKV), bf16), pltpu.VMEM((ROWS, QKV), bf16),
         ],
-        (place, slopes),
-        tiles.reshape(ROWS * 9, 128), norm_gain.reshape(1, D), *weights, spacing,
-        name="sublayer",
+        (slopes,),
+        tiles.reshape(FRAMES * CHUNK, 128), norm_gain.reshape(1, D), spacing, high, low,
+        name="sublayer", far_ins=2, far_outs=2, limit=48,
     )
     grad_tokens = exchange(tokens_back.reshape(FRAMES, 4, OWN, 128), "tm")
 
@@ -301,15 +356,17 @@
     plane = jnp.sum(exchange(row, "tm", X_GROUPS), axis=0)
     column = jnp.concatenate(
         [
-            plane[:32].reshape(16, 2, 8, 128),
-            jnp.tile(plane[32:40], (2, 1, 1)).reshape(16, 1, 8, 128),
-            jnp.broadcast_to(plane[40:], (16, 1, 8, 128)),
+            plane[:32].reshape(16, 16, 1, 128),
+            jnp.tile(plane[32:40], (2, 1, 1)).reshape(16, 8, 1, 128),
+            jnp.tile(plane[40], (2, 1)).reshape(16, 1, 1, 128),
         ],
         axis=1,
     )
     total = jnp.sum(exchange(column, BOTH, Z_GROUPS), axis=0)
 
-    line = exchange(jnp.broadcast_to(total[:3], (NZL, 3, 8, 128)), "tm", ZL_GROUPS)
+    line = exchange(jnp.broadcast_to(total, (NZL, 25, 1, 128)), "tm", ZL_GROUPS)
+    grad_gain = line[:, 24, 0, :64].reshape(D)
+    line = line[:, :24].reshape(NZL, 3, 8, 128)
     sheet = exchange(jnp.broadcast_to(line, (NX, NZL, 3, 8, 128)), "tm", X_GROUPS)
     main = sheet[:, :, :2].transpose(0, 3, 1, 2, 4).reshape(32, QKV + D)
     half = sheet[:, :, 2].reshape(NX, 4, 2, 8, 128).transpose(0, 1, 3, 2, 4).reshape(ACTIONS, 256)
@@ -322,7 +379,7 @@
         main[:, :QKV],
         main[:, QKV:],
         grad_table,
-        total[3, :4].reshape(D),
+        grad_gain,
     )
 
 

time: 245 us -> 236 us (0.963)
  waiting for transfers between devices: 46.9 us -> 27.6 us
  local copies, waits for them, and re-layouts: 9.92 us -> 17.5 us
  blocking collectives: 95.2 us -> 101 us
  starting transfers between devices: 58.7 us -> 55.1 us
    all_to_all x2 -> x1, waiting for transfers between devices: 15.5 us -> 4.98 us  [exchange(): lax.all_to_all(value, axis, 0, 0, axis_index_groups=groups, tiled=True)]
    ppermute x3, waiting for transfers between devices: 16.7 us -> 8.75 us  [far_weights(): lax.ppermute(row, 'dp', turn_y(i))]
    unnamed x28 -> x34, local copies, waits for them, and re-layouts: 6.14 us -> 13.7 us
    all_to_all x4 -> x5, blocking collectives: 95.2 us -> 101 us  [exchange(): lax.all_to_all(value, axis, 0, 0, axis_index_groups=groups, tiled=True)]
    all_to_all x2 -> x1, starting transfers between devices: 16.7 us -> 12.4 us  [exchange(): lax.all_to_all(value, axis, 0, 0, axis_index_groups=groups, tiled=True)]
    pallas_call x1 -> x3, Pallas kernels: 14.1 us -> 15.2 us  [call(): pl.pallas_call(kernel, out_shape=outs, in_specs=[smem] * len(scalars) + [...]
  transfers between devices with their start and end apart: 13 -> 12, of which waited for: 7 -> 6; matrix products, arithmetic and copies ran while one was open for 2% -> 2% of each run, Pallas kernels for 0% -> 1%
where the time goes in v3:
time: 236 us; the launch traced here: 235 us
  blocking collectives  101 us (43%)
  starting transfers between devices  55.1 us (23%)
  waiting for transfers between devices  27.6 us (12%)
  local copies, waits for them, and re-layouts  17.5 us (7%)
  Pallas kernels  15.2 us (6%)
  between operations  15.1 us (6%)
  other arithmetic  3.04 us (1%)
    all_to_all x5, blocking collectives, exchange(): lax.all_to_all(value, axis, 0, 0, axis_index_groups=groups, tiled=True)  101 us
    ppermute x1, starting transfers between devices, gathered_weights(): quarter = lax.ppermute(quarter, 'dp', SWAP_ZH)  15.4 us
    pallas_call x3, Pallas kernels, call(): pl.pallas_call(kernel, out_shape=outs, in_specs=[smem] * len(scalars) + [...  15.2 us
    unnamed x34, local copies, waits for them, and re-layouts  13.7 us
    all_to_all x1, starting transfers between devices, exchange(): lax.all_to_all(value, axis, 0, 0, axis_index_groups=groups, tiled=True)  12.4 us
    ppermute x3, starting transfers between devices, far_weights(): lax.ppermute(quarter, 'tm', turn_x(i))  9.33 us
    ppermute x3, waiting for transfers between devices, far_weights(): lax.ppermute(row, 'dp', turn_y(i))  8.75 us
    ppermute x3, starting transfers between devices, far_weights(): lax.ppermute(row, 'dp', turn_y(i))  8.15 us
  transfers between devices with their start and end apart: 12, of which 6 were waited for; matrix products, arithmetic and copies ran while one was open for 2% of the time, Pallas kernels for 1%

profile of v3, /device:TPU:25, one launch (start us, length us, event | category | flops | bytes accessed | tf_op | source)
XLA Modules:
  0.0 234.5 jit_solution(6446615207981359940)
XLA Ops:
  7.2 1.7 pad_maximum_fusion.1
  10.5 15.4 %collective-permute-start = (f32[8,2048]{1,0:T(8,128)S(1)}, f32[8,2048]{1,0:T(8,128)S(1)}, u32[]{:S(2)}, u32[]{:S(2)}) collective-permute-start(f32[8,2048]{1,0:T(8,128)S(1)} %pad_maximum_fusion.3), channel_id=1, source_target_pairs={{0,2},{1,3},{2,0},{3,1},{4,6},{5,7},{6,4},{7,5},{8,10},{9,11},{10,... | collective-permute-start | bytes 196616 | tf_op jit(solution)/shard_map/ppermute | solution.py:287
  26.7 1.0 copy-done.10
  27.7 1.0 copy-done.11
  28.7 1.2 pack.1
  29.9 12.4 %all-to-all-start = ((f32[32,65,1,128]{3,2,1,0:T(1,128)}), f32[32,65,1,128]{3,2,1,0:T(1,128)S(1)}, u32[]{:S(2)}, u32[]{:S(2)}) async-start(f32[32,65,1,128]{3,2,1,0:T(1,128)} %bitcast.4), calls=%async_computation | async-start | bytes 2129920 | tf_op jit(solution)/shard_map/all_to_all | solution.py:54
  42.4 4.4 %collective-permute-start.3 = (f32[8,2048]{1,0:T(8,128)S(1)}, f32[8,2048]{1,0:T(8,128)S(1)}, u32[]{:S(2)}, u32[]{:S(2)}) collective-permute-start(f32[8,2048]{1,0:T(8,128)S(1)} %collective-permute-done), channel_id=1, source_target_pairs={{0,384},{16,400},{32,416},{48,432},{64,448},{80,464},{96,480},{112... | collective-permute-start | bytes 196616 | tf_op jit(solution)/shard_map/ppermute | solution.py:292
  46.8 2.4 %collective-permute-start.2 = (f32[8,2048]{1,0:T(8,128)S(1)}, f32[8,2048]{1,0:T(8,128)S(1)}, u32[]{:S(2)}, u32[]{:S(2)}) collective-permute-start(f32[8,2048]{1,0:T(8,128)S(1)} %collective-permute-done), channel_id=1, source_target_pairs={{0,256},{16,272},{32,288},{48,304},{64,320},{80,336},{96,352},{112... | collective-permute-start | bytes 196616 | tf_op jit(solution)/shard_map/ppermute | solution.py:292
  49.2 2.5 %collective-permute-start.1 = (f32[8,2048]{1,0:T(8,128)S(1)}, f32[8,2048]{1,0:T(8,128)S(1)}, u32[]{:S(2)}, u32[]{:S(2)}) collective-permute-start(f32[8,2048]{1,0:T(8,128)S(1)} %collective-permute-done), channel_id=1, source_target_pairs={{0,128},{16,144},{32,160},{48,176},{64,192},{80,208},{96,224},{112... | collective-permute-start | bytes 196616 | tf_op jit(solution)/shard_map/ppermute | solution.py:292
  51.7 2.2 collective-permute-done.2
  53.9 2.8 %collective-permute-done.1 = f32[8,2048]{1,0:T(8,128)S(1)} collective-permute-done((f32[8,2048]{1,0:T(8,128)S(1)}, f32[8,2048]{1,0:T(8,128)S(1)}, u32[]{:S(2)}, u32[]{:S(2)}) %collective-permute-start.1) | collective-permute-done | bytes 65568 | tf_op jit(solution)/shard_map/ppermute | solution.py:292
  56.8 1.9 collective-permute-start.4
  58.7 3.4 %collective-permute-start.6 = (f32[4,8,2048]{2,1,0:T(8,128)S(1)}, f32[4,8,2048]{2,1,0:T(8,128)S(1)}, u32[]{:S(2)}, u32[]{:S(2)}) collective-permute-start(f32[4,8,2048]{2,1,0:T(8,128)S(1)} %pad_maximum_fusion), channel_id=1, source_target_pairs={{0,12},{1,13},{2,14},{3,15},{4,0},{5,1},{6,2},{7,3},{8,4},{9,5},{1... | collective-permute-start | bytes 786440 | tf_op jit(solution)/shard_map/ppermute | solution.py:294
  62.1 2.9 %collective-permute-start.5 = (f32[4,8,2048]{2,1,0:T(8,128)S(1)}, f32[4,8,2048]{2,1,0:T(8,128)S(1)}, u32[]{:S(2)}, u32[]{:S(2)}) collective-permute-start(f32[4,8,2048]{2,1,0:T(8,128)S(1)} %pad_maximum_fusion), channel_id=1, source_target_pairs={{0,8},{1,9},{2,10},{3,11},{4,12},{5,13},{6,14},{7,15},{8,0},{9,1},... | collective-permute-start | bytes 786440 | tf_op jit(solution)/shard_map/ppermute | solution.py:294
  65.0 8.7 %collective-permute-done.5 = f32[4,8,2048]{2,1,0:T(8,128)S(1)} collective-permute-done((f32[4,8,2048]{2,1,0:T(8,128)S(1)}, f32[4,8,2048]{2,1,0:T(8,128)S(1)}, u32[]{:S(2)}, u32[]{:S(2)}) %collective-permute-start.5) | collective-permute-done | bytes 262176 | tf_op jit(solution)/shard_map/ppermute | solution.py:294
  73.8 4.6 %collective-permute-start.7 = (f32[16,8,2048]{2,1,0:T(8,128)S(1)}, f32[16,8,2048]{2,1,0:T(8,128)S(1)}, u32[]{:S(2)}, u32[]{:S(2)}) collective-permute-start(f32[16,8,2048]{2,1,0:T(8,128)S(1)} %constant_dynamic-update-slice_fusion.far_mine), channel_id=1, source_target_pairs={{0,1},{1,0},{2,3},{3,2},{4,5},{5,4},{6,7},{7,6},{8,9},{9,8},{10,11... | collective-permute-start | bytes 3145736 | tf_op jit(solution)/shard_map/ppermute | solution.py:295
  81.7 1.6 copy-done.3
  83.3 1.2 copy-done.5
  84.5 1.2 copy-done.7
  85.7 1.4 weights.1
  87.1 1.3 copy-done.1
  88.4 5.0 %all-to-all-done = f32[32,65,1,128]{3,2,1,0:T(1,128)S(1)} async-done(((f32[32,65,1,128]{3,2,1,0:T(1,128)}), f32[32,65,1,128]{3,2,1,0:T(1,128)S(1)}, u32[]{:S(2)}, u32[]{:S(2)}) %all-to-all-start) | async-done | bytes 1064992 | tf_op jit(solution)/shard_map/all_to_all | solution.py:54
  93.4 1.6 copy-done.2
  95.0 12.6 %sublayer.1 = (f32[8,4,41,8,128]{4,3,2,1,0:T(8,128)}, f32[1024,128]{1,0:T(8,128)S(1)}) custom-call(f32[8]{0:T(128)S(1)} %copy-done.13, f32[2080,128]{1,0:T(8,128)S(1)} %bitcast.41, f32[1,512]{1,0:T(1,128)S(1)} %bitcast.46, f32[128,128]{1,0:T(8,128)S(1)} %subtract_select_fusion.spacing, bf16[512,2048]{1,0:T(8,128)(2,1)S(1)} %get-tuple-element.19.high_in, ...), custom_call_target="tpu_custom_call" | custom-call | tf_op jit(solution)/shard_map/sublayer/pallas_call | solution.py:266
  108.4 1.0 copy-done.9
  109.5 35.6 %all_to_all.30 = f32[32,4,8,128]{3,2,1,0:T(8,128)S(1)} all-to-all(f32[32,4,8,128]{3,2,1,0:T(8,128)S(1)} %bitcast.43), channel_id=1, replica_groups=mesh['tm'=32,'dp'=16] {'tm'}, dimensions={0} | all-to-all | bytes 1048576 | tf_op jit(solution)/shard_map/all_to_all | solution.py:54
  145.0 7.8 %reduce-scatter.2.cloned.1.call-done = f32[1,4,41,8,128]{4,3,2,1,0:T(8,128)} async-done(((f32[8,4,41,8,128]{4,3,2,1,0:T(8,128)}), f32[1,4,41,8,128]{4,3,2,1,0:T(8,128)}) %reduce-scatter.2.cloned.1.call-update) | async-done | bytes 671760 | tf_op jit(solution)/shard_map/reduce_scatter | solution.py:352
  152.9 13.3 %all_to_all.31 = f32[4,41,8,128]{3,2,1,0:T(8,128)S(1)} all-to-all(f32[4,41,8,128]{3,2,1,0:T(8,128)} %bitcast.50), channel_id=1, replica_groups={{0,128,256,384},{16,144,272,400},{32,160,288,416},{48,176,304,432},{64,..., dimensions={0} | all-to-all | bytes 1343488 | tf_op jit(solution)/shard_map/all_to_all | solution.py:54
  166.5 27.1 %all_to_all.32 = f32[16,25,1,128]{3,2,1,0:T(1,128)S(1)} all-to-all(f32[16,25,1,128]{3,2,1,0:T(1,128)S(1)} %pad_maximum_fusion.2), channel_id=1, replica_groups={{0,16,32,48,64,80,96,112,2,18,34,50,66,82,98,114},{1,17,33,49,65,81,97,..., dimensions={0} | all-to-all | bytes 409600 | tf_op jit(solution)/shard_map/all_to_all | solution.py:54
  193.8 16.5 %all_to_all.33 = f32[8,25,1,128]{3,2,1,0:T(1,128)S(1)} all-to-all(f32[8,25,1,128]{3,2,1,0:T(1,128)S(1)} %broadcast_in_dim.11), channel_id=1, replica_groups={{0,16,32,48,64,80,96,112},{128,144,160,176,192,208,224,240},{256,272,28..., dimensions={0} | all-to-all | bytes 204800 | tf_op jit(solution)/shard_map/all_to_all | solution.py:54
  210.3 8.6 %all_to_all.34 = f32[4,8,3,8,128]{4,3,2,1,0:T(8,128)S(1)} all-to-all(f32[4,8,3,8,128]{4,3,2,1,0:T(8,128)S(1)} %broadcast_in_dim.12), channel_id=1, replica_groups={{0,128,256,384},{16,144,272,400},{32,160,288,416},{48,176,304,432},{64,..., dimensions={0} | all-to-all | bytes 786432 | tf_op jit(solution)/shard_map/all_to_all | solution.py:54
  218.9 5.2 %collective-permute-start.8 = (f32[128,256]{1,0:T(8,128)S(1)}, f32[128,256]{1,0:T(8,128)S(1)}, u32[]{:S(2)}, u32[]{:S(2)}) collective-permute-start(f32[128,256]{1,0:T(8,128)S(1)} %bitcast.51), channel_id=1, source_target_pairs={{0,1},{1,0},{2,3},{3,2},{4,5},{5,4},{6,7},{7,6},{8,9},{9,8},{10,11... | collective-permute-start | bytes 393224 | tf_op jit(solution)/shard_map/ppermute | solution.py:373
  (68 shorter events, 9.9 us)
Async XLA Ops:
  7.2 19.5 %copy-start = (f32[128,512]{1,0:T(8,128)S(1)}, f32[128,512]{1,0:T(8,128)}, u32[]{:S(2)}) copy-start(f32[128,512]{1,0:T(8,128)} %param.12) | copy-start | bytes 786436
  7.2 49.6 %all-gather.3.cloned.1.call-start = ((), (), s32[]{:S(2)}) async-start(), calls=%async_computation.8 | async-start | bytes 2359296 | tf_op jit(solution)/shard_map/all_gather | solution.py:283
  10.5 19.4 %collective-permute-start = (f32[8,2048]{1,0:T(8,128)S(1)}, f32[8,2048]{1,0:T(8,128)S(1)}, u32[]{:S(2)}, u32[]{:S(2)}) collective-permute-start(f32[8,2048]{1,0:T(8,128)S(1)} %pad_maximum_fusion.3), channel_id=1, source_target_pairs={{0,2},{1,3},{2,0},{3,1},{4,6},{5,7},{6,4},{7,5},{8,10},{9,11},{10,... | collective-permute-start | bytes 196616 | tf_op jit(solution)/shard_map/ppermute | solution.py:287
  26.7 1.0 copy-start.10
  27.7 1.0 copy-start.11
  29.9 49.5 %copy-start.14 = (s32[1,32]{1,0:T(1,128)S(1)}, s32[1,32]{1,0:T(1,128)}, u32[]{:S(2)}) copy-start(s32[1,32]{1,0:T(1,128)} %param.11) | copy-start | bytes 388
  29.9 63.5 %all-to-all-start = ((f32[32,65,1,128]{3,2,1,0:T(1,128)}), f32[32,65,1,128]{3,2,1,0:T(1,128)S(1)}, u32[]{:S(2)}, u32[]{:S(2)}) async-start(f32[32,65,1,128]{3,2,1,0:T(1,128)} %bitcast.4), calls=%async_computation | async-start | bytes 2129920 | tf_op jit(solution)/shard_map/all_to_all | solution.py:54
  42.3 110.5 %reduce-scatter.2.cloned.1.call-start = ((), (), s32[]{:S(2)}) async-start(), calls=%async_computation.7 | async-start | bytes 6045696 | tf_op jit(solution)/shard_map/reduce_scatter | solution.py:352
  42.4 9.4 %collective-permute-start.3 = (f32[8,2048]{1,0:T(8,128)S(1)}, f32[8,2048]{1,0:T(8,128)S(1)}, u32[]{:S(2)}, u32[]{:S(2)}) collective-permute-start(f32[8,2048]{1,0:T(8,128)S(1)} %collective-permute-done), channel_id=1, source_target_pairs={{0,384},{16,400},{32,416},{48,432},{64,448},{80,464},{96,480},{112... | collective-permute-start | bytes 196616 | tf_op jit(solution)/shard_map/ppermute | solution.py:292
  46.8 7.2 %collective-permute-start.2 = (f32[8,2048]{1,0:T(8,128)S(1)}, f32[8,2048]{1,0:T(8,128)S(1)}, u32[]{:S(2)}, u32[]{:S(2)}) collective-permute-start(f32[8,2048]{1,0:T(8,128)S(1)} %collective-permute-done), channel_id=1, source_target_pairs={{0,256},{16,272},{32,288},{48,304},{64,320},{80,336},{96,352},{112... | collective-permute-start | bytes 196616 | tf_op jit(solution)/shard_map/ppermute | solution.py:292
  49.2 7.5 %collective-permute-start.1 = (f32[8,2048]{1,0:T(8,128)S(1)}, f32[8,2048]{1,0:T(8,128)S(1)}, u32[]{:S(2)}, u32[]{:S(2)}) collective-permute-start(f32[8,2048]{1,0:T(8,128)S(1)} %collective-permute-done), channel_id=1, source_target_pairs={{0,128},{16,144},{32,160},{48,176},{64,192},{80,208},{96,224},{112... | collective-permute-start | bytes 196616 | tf_op jit(solution)/shard_map/ppermute | solution.py:292
  56.8 8.2 %collective-permute-start.4 = (f32[4,8,2048]{2,1,0:T(8,128)S(1)}, f32[4,8,2048]{2,1,0:T(8,128)S(1)}, u32[]{:S(2)}, u32[]{:S(2)}) collective-permute-start(f32[4,8,2048]{2,1,0:T(8,128)S(1)} %pad_maximum_fusion), channel_id=1, source_target_pairs={{0,4},{1,5},{2,6},{3,7},{4,8},{5,9},{6,10},{7,11},{8,12},{9,13},{1... | collective-permute-start | bytes 786440 | tf_op jit(solution)/shard_map/ppermute | solution.py:294
  58.7 15.1 %collective-permute-start.6 = (f32[4,8,2048]{2,1,0:T(8,128)S(1)}, f32[4,8,2048]{2,1,0:T(8,128)S(1)}, u32[]{:S(2)}, u32[]{:S(2)}) collective-permute-start(f32[4,8,2048]{2,1,0:T(8,128)S(1)} %pad_maximum_fusion), channel_id=1, source_target_pairs={{0,12},{1,13},{2,14},{3,15},{4,0},{5,1},{6,2},{7,3},{8,4},{9,5},{1... | collective-permute-start | bytes 786440 | tf_op jit(solution)/shard_map/ppermute | solution.py:294
  62.1 11.7 %collective-permute-start.5 = (f32[4,8,2048]{2,1,0:T(8,128)S(1)}, f32[4,8,2048]{2,1,0:T(8,128)S(1)}, u32[]{:S(2)}, u32[]{:S(2)}) collective-permute-start(f32[4,8,2048]{2,1,0:T(8,128)S(1)} %pad_maximum_fusion), channel_id=1, source_target_pairs={{0,8},{1,9},{2,10},{3,11},{4,12},{5,13},{6,14},{7,15},{8,0},{9,1},... | collective-permute-start | bytes 786440 | tf_op jit(solution)/shard_map/ppermute | solution.py:294
  73.8 6.8 %collective-permute-start.7 = (f32[16,8,2048]{2,1,0:T(8,128)S(1)}, f32[16,8,2048]{2,1,0:T(8,128)S(1)}, u32[]{:S(2)}, u32[]{:S(2)}) collective-permute-start(f32[16,8,2048]{2,1,0:T(8,128)S(1)} %constant_dynamic-update-slice_fusion.far_mine), channel_id=1, source_target_pairs={{0,1},{1,0},{2,3},{3,2},{4,5},{5,4},{6,7},{7,6},{8,9},{9,8},{10,11... | collective-permute-start | bytes 3145736 | tf_op jit(solution)/shard_map/ppermute | solution.py:295
  78.4 1.0 copy-start.4
  80.7 1.0 copy-start.6
  81.7 1.6 copy-start.3
  83.3 1.2 copy-start.5
  84.5 1.2 copy-start.7
  85.7 7.7 %copy-start.12 = (f32[512]{0:T(512)S(1)}, f32[512]{0:T(512)}, u32[]{:S(2)}) copy-start(f32[512]{0:T(512)} %param.13) | copy-start | bytes 6148
  85.7 7.7 %copy-start.13 = (f32[8]{0:T(128)S(1)}, f32[8]{0:T(128)}, u32[]{:S(2)}) copy-start(f32[8]{0:T(128)} %slopes.1) | copy-start | bytes 100
  87.1 1.3 copy-start.1
  93.4 1.6 copy-start.2
  107.6 0.8 copy-start.8
  108.4 1.0 copy-start.9
  218.9 7.2 %collective-permute-start.8 = (f32[128,256]{1,0:T(8,128)S(1)}, f32[128,256]{1,0:T(8,128)S(1)}, u32[]{:S(2)}, u32[]{:S(2)}) collective-permute-start(f32[128,256]{1,0:T(8,128)S(1)} %bitcast.51), channel_id=1, source_target_pairs={{0,1},{1,0},{2,3},{3,2},{4,5},{5,4},{6,7},{7,6},{8,9},{9,8},{10,11... | collective-permute-start | bytes 393224 | tf_op jit(solution)/shard_map/ppermute | solution.py:373
Sparse Core Ops, SparseCore 0:
  10.7 36.4 all-gather.2
  108.6 44.2 reduce-scatter.1

commit v4 on v3

--- a/solution.py
+++ b/solution.py
@@ -79,15 +79,20 @@
             ]
 
 
-def pack_kernel(action, row, video_in, og_in, out, video, og, sems):
-    arrivals = [
-        pltpu.make_async_copy(source, target, sems.at[i])
-        for i, (source, target) in enumerate(((video_in, video), (og_in, og)))
-    ]
-    for copy in arrivals:
-        copy.start()
-    for copy in arrivals:
-        copy.wait()
+def shares_kernel(place, w_qkv, w_out, mine, quarter):
+    mine[:, :QKV] = w_qkv[...]
+    mine[:, QKV:] = w_out[...]
+    x = pl.multiple_of(place[0] * 8, 8)
+    quarter[:, :QKV] = w_qkv[pl.ds(x, 8), :]
+    quarter[:, QKV:] = w_out[pl.ds(x, 8), :]
+
+
+def pass_kernel(value, out):
+    out[...] = value[...]
+
+
+def pack_kernel(action, act_table, video, og, out):
+    row = act_table[pl.ds(action[0], 1), :]
     tag = jnp.zeros((1, 128), f32) + action[0].astype(f32)
     for f in range(FRAMES):
         rows = slice(f * OWN, f * OWN + OWN)
@@ -259,7 +264,7 @@
         copy.wait()
 
 
-def call(kernel, outs, scratch, scalars, *arrays, name, far_ins=0, far_outs=0, limit=24):
+def call(kernel, outs, scratch, scalars, *arrays, name, far_ins=0, far_outs=0, limit=60, work=None):
     vmem = pl.BlockSpec(memory_space=pltpu.VMEM)
     smem = pl.BlockSpec(memory_space=pltpu.SMEM)
     hbm = pl.BlockSpec(memory_space=pltpu.HBM)
@@ -270,22 +275,14 @@
         out_specs=[hbm] * far_outs + [vmem] * (len(outs) - far_outs),
         scratch_shapes=scratch,
         compiler_params=pltpu.CompilerParams(vmem_limit_bytes=limit * 1024 * 1024),
+        cost_estimate=work
+        and pl.CostEstimate(flops=work, bytes_accessed=0, transcendentals=0),
         name=name,
     )(*scalars, *arrays)
 
 
 def shape(*dims, kind=f32):
     return jax.ShapeDtypeStruct(dims, kind)
-
-
-def gathered_weights(w_qkv, w_out, x):
-    mine = jnp.concatenate([w_qkv, w_out], axis=1)
-    own = lax.all_gather(mine, "dp", axis_index_groups=YC_GROUPS)
-    quarter = jnp.concatenate(
-        [lax.dynamic_slice(w, (x * 8, 0), (8, w.shape[1])) for w in (w_qkv, w_out)], axis=1
-    )
-    quarter = lax.ppermute(quarter, "dp", SWAP_ZH)
-    return own, quarter
 
 
 def far_weights(own, quarter):
@@ -302,18 +299,27 @@
     x, y, zh, c = t // NZL, d // (NZH * NC), (d // NC) % NZH, d % NC
     place = jnp.stack([x, y, zh, c]).astype(jnp.int32)
 
-    own, quarter = gathered_weights(w_qkv, w_out, x)
-    action = actions[0, 0]
-    row = lax.dynamic_slice(act_table, (action, 0), (1, D))
+    mine, quarter = call(
+        shares_kernel,
+        [shape(32, QKV + D), shape(8, QKV + D)],
+        [],
+        (place,),
+        w_qkv, w_out,
+        name="shares",
+    )
+    own = lax.all_gather(mine, "dp", axis_index_groups=YC_GROUPS)
+    quarter = lax.ppermute(quarter, "dp", SWAP_ZH)
+    quarter = call(
+        pass_kernel, [shape(8, QKV + D)], [], (), quarter, name="swapped", work=20000000000
+    )[0]
     payload = call(
         pack_kernel,
         [shape(FRAMES * CHUNK, 128)],
-        [pltpu.VMEM((ROWS, D), f32), pltpu.VMEM((ROWS, D), f32), pltpu.SemaphoreType.DMA((2,))],
-        (action.reshape(1),),
-        row, video_tokens[0, 0], out_grad[0, 0],
-        name="pack", far_ins=2,
+        [],
+        (actions.reshape(1),),
+        act_table, video_tokens[0, 0], out_grad[0, 0],
+        name="pack",
     )[0]
-    quarter, payload = lax.optimization_barrier((quarter, payload))
     high, low = call(
         weights_kernel,
         [shape(D, QKV + D, kind=bf16), shape(D, QKV + D, kind=bf16)],
@@ -345,7 +351,7 @@
         ],
         (slopes,),
         tiles.reshape(FRAMES * CHUNK, 128), norm_gain.reshape(1, D), spacing, high, low,
-        name="sublayer", far_ins=2, far_outs=2, limit=48,
+        name="sublayer", far_ins=2, far_outs=2, limit=52,
     )
     grad_tokens = exchange(tokens_back.reshape(FRAMES, 4, OWN, 128), "tm")
 

time: 236 us -> 227 us (0.962)
  local copies, waits for them, and re-layouts: 17.5 us -> 3.74 us
  Pallas kernels: 15.2 us -> 24.9 us
  starting transfers between devices: 55.1 us -> 50 us
    unnamed x34 -> x14, local copies, waits for them, and re-layouts: 13.7 us -> 1.49 us
    pallas_call x3 -> x5, Pallas kernels: 15.2 us -> 24.9 us  [call(): pl.pallas_call(kernel, out_shape=outs, in_specs=[smem] * len(scalars) + [...]
    all_to_all x1, starting transfers between devices: 12.4 us -> 7.6 us  [exchange(): lax.all_to_all(value, axis, 0, 0, axis_index_groups=groups, tiled=True)]
  transfers between devices with their start and end apart: 12 -> 12, of which waited for: 6 -> 7; matrix products, arithmetic and copies ran while one was open for 2% -> 1% of each run, Pallas kernels for 1% -> 4%
where the time goes in v4:
time: 227 us; the launch traced here: 226 us
  blocking collectives  101 us (44%)
  starting transfers between devices  50 us (22%)
  waiting for transfers between devices  28.7 us (13%)
  Pallas kernels  24.9 us (11%)
  between operations  15.1 us (7%)
  local copies, waits for them, and re-layouts  3.74 us (2%)
  other arithmetic  2.64 us (1%)
    all_to_all x5, blocking collectives, exchange(): lax.all_to_all(value, axis, 0, 0, axis_index_groups=groups, tiled=True)  101 us
    pallas_call x5, Pallas kernels, call(): pl.pallas_call(kernel, out_shape=outs, in_specs=[smem] * len(scalars) + [...  24.9 us
    ppermute x1, starting transfers between devices, shards(): quarter = lax.ppermute(quarter, 'dp', SWAP_ZH)  15.4 us
    ppermute x3, starting transfers between devices, far_weights(): lax.ppermute(quarter, 'tm', turn_x(i))  9.44 us
    ppermute x3, waiting for transfers between devices, far_weights(): lax.ppermute(row, 'dp', turn_y(i))  8.92 us
    ppermute x3, starting transfers between devices, far_weights(): lax.ppermute(row, 'dp', turn_y(i))  8.15 us
    reduce_scatter x1, waiting for transfers between devices, shards(): lax.psum_scatter(grads, 'dp', scatter_dimension=0, axis_index_groups=YC_G...  7.79 us
    all_to_all x1, starting transfers between devices, exchange(): lax.all_to_all(value, axis, 0, 0, axis_index_groups=groups, tiled=True)  7.6 us
  transfers between devices with their start and end apart: 12, of which 7 were waited for; matrix products, arithmetic and copies ran while one was open for 1% of the time, Pallas kernels for 4%

profile of v4, /device:TPU:25, one launch (start us, length us, event | category | flops | bytes accessed | tf_op | source)
XLA Modules:
  0.0 226.0 jit_solution(17837806962134876467)
XLA Ops:
  7.8 1.7 shares.1
  9.5 15.4 %collective-permute-start = (f32[8,2048]{1,0:T(8,128)}, f32[8,2048]{1,0:T(8,128)S(1)}, u32[]{:S(2)}, u32[]{:S(2)}) collective-permute-start(f32[8,2048]{1,0:T(8,128)} %get-tuple-element.15), channel_id=1, source_target_pairs={{0,2},{1,3},{2,0},{3,1},{4,6},{5,7},{6,4},{7,5},{8,10},{9,11},{10,... | collective-permute-start | bytes 196616 | tf_op jit(solution)/shard_map/ppermute | solution.py:311
  25.6 2.3 %pack.1 = f32[2080,128]{1,0:T(8,128)} custom-call(s32[1]{0:T(128)} %bitcast.36.action, f32[128,512]{1,0:T(8,128)} %act_table.1, f32[256,512]{1,0:T(8,128)} %bitcast.49, f32[256,512]{1,0:T(8,128)} %bitcast.50), custom_call_target="tpu_custom_call" | custom-call | tf_op jit(solution)/shard_map/pack/pallas_call | solution.py:271
  28.0 7.6 %all-to-all-start = ((f32[32,65,1,128]{3,2,1,0:T(1,128)}), f32[32,65,1,128]{3,2,1,0:T(1,128)S(1)}, u32[]{:S(2)}, u32[]{:S(2)}) async-start(f32[32,65,1,128]{3,2,1,0:T(1,128)} %bitcast.40), calls=%async_computation | async-start | bytes 2129920 | tf_op jit(solution)/shard_map/all_to_all | solution.py:54
  36.2 1.5 swapped.1
  37.7 4.5 %collective-permute-start.3 = (f32[8,2048]{1,0:T(8,128)}, f32[8,2048]{1,0:T(8,128)S(1)}, u32[]{:S(2)}, u32[]{:S(2)}) collective-permute-start(f32[8,2048]{1,0:T(8,128)} %swapped.1), channel_id=1, source_target_pairs={{0,384},{16,400},{32,416},{48,432},{64,448},{80,464},{96,480},{112... | collective-permute-start | bytes 196616 | tf_op jit(solution)/shard_map/ppermute | solution.py:289
  42.2 2.4 %collective-permute-start.2 = (f32[8,2048]{1,0:T(8,128)}, f32[8,2048]{1,0:T(8,128)S(1)}, u32[]{:S(2)}, u32[]{:S(2)}) collective-permute-start(f32[8,2048]{1,0:T(8,128)} %swapped.1), channel_id=1, source_target_pairs={{0,256},{16,272},{32,288},{48,304},{64,320},{80,336},{96,352},{112... | collective-permute-start | bytes 196616 | tf_op jit(solution)/shard_map/ppermute | solution.py:289
  44.7 2.5 %collective-permute-start.1 = (f32[8,2048]{1,0:T(8,128)}, f32[8,2048]{1,0:T(8,128)S(1)}, u32[]{:S(2)}, u32[]{:S(2)}) collective-permute-start(f32[8,2048]{1,0:T(8,128)} %swapped.1), channel_id=1, source_target_pairs={{0,128},{16,144},{32,160},{48,176},{64,192},{80,208},{96,224},{112... | collective-permute-start | bytes 196616 | tf_op jit(solution)/shard_map/ppermute | solution.py:289
  47.2 2.5 %collective-permute-done.2 = f32[8,2048]{1,0:T(8,128)S(1)} collective-permute-done((f32[8,2048]{1,0:T(8,128)}, f32[8,2048]{1,0:T(8,128)S(1)}, u32[]{:S(2)}, u32[]{:S(2)}) %collective-permute-start.2) | collective-permute-done | bytes 65568 | tf_op jit(solution)/shard_map/ppermute | solution.py:289
  49.7 3.5 %collective-permute-done.1 = f32[8,2048]{1,0:T(8,128)S(1)} collective-permute-done((f32[8,2048]{1,0:T(8,128)}, f32[8,2048]{1,0:T(8,128)S(1)}, u32[]{:S(2)}, u32[]{:S(2)}) %collective-permute-start.1) | collective-permute-done | bytes 65568 | tf_op jit(solution)/shard_map/ppermute | solution.py:289
  53.2 0.9 pad_maximum_fusion
  54.1 1.9 collective-permute-start.4
  56.0 3.4 %collective-permute-start.6 = (f32[4,8,2048]{2,1,0:T(8,128)S(1)}, f32[4,8,2048]{2,1,0:T(8,128)S(1)}, u32[]{:S(2)}, u32[]{:S(2)}) collective-permute-start(f32[4,8,2048]{2,1,0:T(8,128)S(1)} %pad_maximum_fusion), channel_id=1, source_target_pairs={{0,12},{1,13},{2,14},{3,15},{4,0},{5,1},{6,2},{7,3},{8,4},{9,5},{1... | collective-permute-start | bytes 786440 | tf_op jit(solution)/shard_map/ppermute | solution.py:291
  59.4 2.9 %collective-permute-start.5 = (f32[4,8,2048]{2,1,0:T(8,128)S(1)}, f32[4,8,2048]{2,1,0:T(8,128)S(1)}, u32[]{:S(2)}, u32[]{:S(2)}) collective-permute-start(f32[4,8,2048]{2,1,0:T(8,128)S(1)} %pad_maximum_fusion), channel_id=1, source_target_pairs={{0,8},{1,9},{2,10},{3,11},{4,12},{5,13},{6,14},{7,15},{8,0},{9,1},... | collective-permute-start | bytes 786440 | tf_op jit(solution)/shard_map/ppermute | solution.py:291
  62.6 8.6 %collective-permute-done.5 = f32[4,8,2048]{2,1,0:T(8,128)S(1)} collective-permute-done((f32[4,8,2048]{2,1,0:T(8,128)S(1)}, f32[4,8,2048]{2,1,0:T(8,128)S(1)}, u32[]{:S(2)}, u32[]{:S(2)}) %collective-permute-start.5) | collective-permute-done | bytes 262176 | tf_op jit(solution)/shard_map/ppermute | solution.py:291
  71.3 4.1 %collective-permute-start.7 = (f32[16,8,2048]{2,1,0:T(8,128)S(1)}, f32[16,8,2048]{2,1,0:T(8,128)}, u32[]{:S(2)}, u32[]{:S(2)}) collective-permute-start(f32[16,8,2048]{2,1,0:T(8,128)S(1)} %constant_dynamic-update-slice_fusion.far_mine), channel_id=1, source_target_pairs={{0,1},{1,0},{2,3},{3,2},{4,5},{5,4},{6,7},{7,6},{8,9},{9,8},{10,11... | collective-permute-start | bytes 3145736 | tf_op jit(solution)/shard_map/ppermute | solution.py:292
  75.7 2.1 collective-permute-done.7.far_other
  77.8 5.0 %weights.1 = (bf16[512,2048]{1,0:T(8,128)(2,1)}, bf16[512,2048]{1,0:T(8,128)(2,1)}) custom-call(s32[4]{0:T(128)} %pad_add_fusion.place, f32[8,32,2048]{2,1,0:T(8,128)} %bitcast.41, f32[16,8,2048]{2,1,0:T(8,128)} %copy-done.2, f32[16,8,2048]{2,1,0:T(8,128)} %collective-permute-done.7.far_other), custom_call_target="tpu_custom_call" | custom-call | tf_op jit(solution)/shard_map/weights/pallas_call | solution.py:271
  82.8 3.8 %all-to-all-done = f32[32,65,1,128]{3,2,1,0:T(1,128)S(1)} async-done(((f32[32,65,1,128]{3,2,1,0:T(1,128)}), f32[32,65,1,128]{3,2,1,0:T(1,128)S(1)}, u32[]{:S(2)}, u32[]{:S(2)}) %all-to-all-start) | async-done | bytes 1064992 | tf_op jit(solution)/shard_map/all_to_all | solution.py:54
  86.6 14.4 %sublayer.1 = (f32[8,4,41,8,128]{4,3,2,1,0:T(8,128)}, f32[1024,128]{1,0:T(8,128)S(1)}) custom-call(f32[8]{0:T(128)S(1)} %copy-done.1, f32[2080,128]{1,0:T(8,128)S(1)} %bitcast.37, f32[1,512]{1,0:T(1,128)S(1)} %bitcast.39, f32[128,128]{1,0:T(8,128)S(1)} %subtract_select_fusion.spacing, bf16[512,2048]{1,0:T(8,128)(2,1)} %get-tuple-element.19.high_in, ...), custom_call_target="tpu_custom_call" | custom-call | tf_op jit(solution)/shard_map/sublayer/pallas_call | solution.py:271
  101.1 35.6 %all_to_all.30 = f32[32,4,8,128]{3,2,1,0:T(8,128)S(1)} all-to-all(f32[32,4,8,128]{3,2,1,0:T(8,128)S(1)} %bitcast.38), channel_id=1, replica_groups=mesh['tm'=32,'dp'=16] {'tm'}, dimensions={0} | all-to-all | bytes 1048576 | tf_op jit(solution)/shard_map/all_to_all | solution.py:54
  136.6 7.8 %reduce-scatter.2.cloned.1.call-done = f32[1,4,41,8,128]{4,3,2,1,0:T(8,128)} async-done(((f32[8,4,41,8,128]{4,3,2,1,0:T(8,128)}), f32[1,4,41,8,128]{4,3,2,1,0:T(8,128)}) %reduce-scatter.2.cloned.1.call-update) | async-done | bytes 671760 | tf_op jit(solution)/shard_map/reduce_scatter | solution.py:358
  144.4 13.3 %all_to_all.31 = f32[4,41,8,128]{3,2,1,0:T(8,128)S(1)} all-to-all(f32[4,41,8,128]{3,2,1,0:T(8,128)} %bitcast.45), channel_id=1, replica_groups={{0,128,256,384},{16,144,272,400},{32,160,288,416},{48,176,304,432},{64,..., dimensions={0} | all-to-all | bytes 1343488 | tf_op jit(solution)/shard_map/all_to_all | solution.py:54
  158.0 27.3 %all_to_all.32 = f32[16,25,1,128]{3,2,1,0:T(1,128)S(1)} all-to-all(f32[16,25,1,128]{3,2,1,0:T(1,128)S(1)} %pad_maximum_fusion.1), channel_id=1, replica_groups={{0,16,32,48,64,80,96,112,2,18,34,50,66,82,98,114},{1,17,33,49,65,81,97,..., dimensions={0} | all-to-all | bytes 409600 | tf_op jit(solution)/shard_map/all_to_all | solution.py:54
  185.5 16.2 %all_to_all.33 = f32[8,25,1,128]{3,2,1,0:T(1,128)S(1)} all-to-all(f32[8,25,1,128]{3,2,1,0:T(1,128)S(1)} %broadcast_in_dim.11), channel_id=1, replica_groups={{0,16,32,48,64,80,96,112},{128,144,160,176,192,208,224,240},{256,272,28..., dimensions={0} | all-to-all | bytes 204800 | tf_op jit(solution)/shard_map/all_to_all | solution.py:54
  201.7 8.6 %all_to_all.34 = f32[4,8,3,8,128]{4,3,2,1,0:T(8,128)S(1)} all-to-all(f32[4,8,3,8,128]{4,3,2,1,0:T(8,128)S(1)} %broadcast_in_dim.12), channel_id=1, replica_groups={{0,128,256,384},{16,144,272,400},{32,160,288,416},{48,176,304,432},{64,..., dimensions={0} | all-to-all | bytes 786432 | tf_op jit(solution)/shard_map/all_to_all | solution.py:54
  210.4 5.2 %collective-permute-start.8 = (f32[128,256]{1,0:T(8,128)S(1)}, f32[128,256]{1,0:T(8,128)S(1)}, u32[]{:S(2)}, u32[]{:S(2)}) collective-permute-start(f32[128,256]{1,0:T(8,128)S(1)} %bitcast.46), channel_id=1, source_target_pairs={{0,1},{1,0},{2,3},{3,2},{4,5},{5,4},{6,7},{7,6},{8,9},{9,8},{10,11... | collective-permute-start | bytes 393224 | tf_op jit(solution)/shard_map/ppermute | solution.py:379
  215.6 0.7 reshape_squeeze.7
  216.3 0.6 slice.42
  216.9 0.7 slice.41
  217.6 0.7 maximum_select_fusion
  218.3 0.8 copy.20
  (45 shorter events, 2.5 us)
Async XLA Ops:
  7.2 46.9 %all-gather.3.cloned.1.call-start = ((), (), s32[]{:S(2)}) async-start(), calls=%async_computation.8 | async-start | bytes 2359296 | tf_op jit(solution)/shard_map/all_gather | solution.py:310
  9.5 26.1 %collective-permute-start = (f32[8,2048]{1,0:T(8,128)}, f32[8,2048]{1,0:T(8,128)S(1)}, u32[]{:S(2)}, u32[]{:S(2)}) collective-permute-start(f32[8,2048]{1,0:T(8,128)} %get-tuple-element.15), channel_id=1, source_target_pairs={{0,2},{1,3},{2,0},{3,1},{4,6},{5,7},{6,4},{7,5},{8,10},{9,11},{10,... | collective-permute-start | bytes 196616 | tf_op jit(solution)/shard_map/ppermute | solution.py:311
  28.0 58.6 %all-to-all-start = ((f32[32,65,1,128]{3,2,1,0:T(1,128)}), f32[32,65,1,128]{3,2,1,0:T(1,128)S(1)}, u32[]{:S(2)}, u32[]{:S(2)}) async-start(f32[32,65,1,128]{3,2,1,0:T(1,128)} %bitcast.40), calls=%async_computation | async-start | bytes 2129920 | tf_op jit(solution)/shard_map/all_to_all | solution.py:54
  35.6 108.9 %reduce-scatter.2.cloned.1.call-start = ((), (), s32[]{:S(2)}) async-start(), calls=%async_computation.7 | async-start | bytes 6045696 | tf_op jit(solution)/shard_map/reduce_scatter | solution.py:358
  35.6 0.6 copy-start.3
  37.7 37.7 %copy-start.4 = (s32[1,32]{1,0:T(1,128)S(1)}, s32[1,32]{1,0:T(1,128)}, u32[]{:S(2)}) copy-start(s32[1,32]{1,0:T(1,128)} %param.11) | copy-start | bytes 388
  37.7 9.5 %collective-permute-start.3 = (f32[8,2048]{1,0:T(8,128)}, f32[8,2048]{1,0:T(8,128)S(1)}, u32[]{:S(2)}, u32[]{:S(2)}) collective-permute-start(f32[8,2048]{1,0:T(8,128)} %swapped.1), channel_id=1, source_target_pairs={{0,384},{16,400},{32,416},{48,432},{64,448},{80,464},{96,480},{112... | collective-permute-start | bytes 196616 | tf_op jit(solution)/shard_map/ppermute | solution.py:289
  42.2 7.5 %collective-permute-start.2 = (f32[8,2048]{1,0:T(8,128)}, f32[8,2048]{1,0:T(8,128)S(1)}, u32[]{:S(2)}, u32[]{:S(2)}) collective-permute-start(f32[8,2048]{1,0:T(8,128)} %swapped.1), channel_id=1, source_target_pairs={{0,256},{16,272},{32,288},{48,304},{64,320},{80,336},{96,352},{112... | collective-permute-start | bytes 196616 | tf_op jit(solution)/shard_map/ppermute | solution.py:289
  44.7 8.5 %collective-permute-start.1 = (f32[8,2048]{1,0:T(8,128)}, f32[8,2048]{1,0:T(8,128)S(1)}, u32[]{:S(2)}, u32[]{:S(2)}) collective-permute-start(f32[8,2048]{1,0:T(8,128)} %swapped.1), channel_id=1, source_target_pairs={{0,128},{16,144},{32,160},{48,176},{64,192},{80,208},{96,224},{112... | collective-permute-start | bytes 196616 | tf_op jit(solution)/shard_map/ppermute | solution.py:289
  54.1 8.5 %collective-permute-start.4 = (f32[4,8,2048]{2,1,0:T(8,128)S(1)}, f32[4,8,2048]{2,1,0:T(8,128)S(1)}, u32[]{:S(2)}, u32[]{:S(2)}) collective-permute-start(f32[4,8,2048]{2,1,0:T(8,128)S(1)} %pad_maximum_fusion), channel_id=1, source_target_pairs={{0,4},{1,5},{2,6},{3,7},{4,8},{5,9},{6,10},{7,11},{8,12},{9,13},{1... | collective-permute-start | bytes 786440 | tf_op jit(solution)/shard_map/ppermute | solution.py:291
  56.0 15.2 %collective-permute-start.6 = (f32[4,8,2048]{2,1,0:T(8,128)S(1)}, f32[4,8,2048]{2,1,0:T(8,128)S(1)}, u32[]{:S(2)}, u32[]{:S(2)}) collective-permute-start(f32[4,8,2048]{2,1,0:T(8,128)S(1)} %pad_maximum_fusion), channel_id=1, source_target_pairs={{0,12},{1,13},{2,14},{3,15},{4,0},{5,1},{6,2},{7,3},{8,4},{9,5},{1... | collective-permute-start | bytes 786440 | tf_op jit(solution)/shard_map/ppermute | solution.py:291
  59.4 11.8 %collective-permute-start.5 = (f32[4,8,2048]{2,1,0:T(8,128)S(1)}, f32[4,8,2048]{2,1,0:T(8,128)S(1)}, u32[]{:S(2)}, u32[]{:S(2)}) collective-permute-start(f32[4,8,2048]{2,1,0:T(8,128)S(1)} %pad_maximum_fusion), channel_id=1, source_target_pairs={{0,8},{1,9},{2,10},{3,11},{4,12},{5,13},{6,14},{7,15},{8,0},{9,1},... | collective-permute-start | bytes 786440 | tf_op jit(solution)/shard_map/ppermute | solution.py:291
  71.3 6.5 %copy-start.2 = (f32[16,8,2048]{2,1,0:T(8,128)}, f32[16,8,2048]{2,1,0:T(8,128)S(1)}, u32[]{:S(2)}) copy-start(f32[16,8,2048]{2,1,0:T(8,128)S(1)} %constant_dynamic-update-slice_fusion.far_mine) | copy-start | bytes 3145732
  71.3 6.5 %collective-permute-start.7 = (f32[16,8,2048]{2,1,0:T(8,128)S(1)}, f32[16,8,2048]{2,1,0:T(8,128)}, u32[]{:S(2)}, u32[]{:S(2)}) collective-permute-start(f32[16,8,2048]{2,1,0:T(8,128)S(1)} %constant_dynamic-update-slice_fusion.far_mine), channel_id=1, source_target_pairs={{0,1},{1,0},{2,3},{3,2},{4,5},{5,4},{6,7},{7,6},{8,9},{9,8},{10,11... | collective-permute-start | bytes 3145736 | tf_op jit(solution)/shard_map/ppermute | solution.py:292
  75.7 10.9 %copy-start = (f32[512]{0:T(512)S(1)}, f32[512]{0:T(512)}, u32[]{:S(2)}) copy-start(f32[512]{0:T(512)} %param.13) | copy-start | bytes 6148
  75.7 10.9 %copy-start.1 = (f32[8]{0:T(128)S(1)}, f32[8]{0:T(128)}, u32[]{:S(2)}) copy-start(f32[8]{0:T(128)} %slopes.1) | copy-start | bytes 100
  210.4 7.2 %collective-permute-start.8 = (f32[128,256]{1,0:T(8,128)S(1)}, f32[128,256]{1,0:T(8,128)S(1)}, u32[]{:S(2)}, u32[]{:S(2)}) collective-permute-start(f32[128,256]{1,0:T(8,128)S(1)} %bitcast.46), channel_id=1, source_target_pairs={{0,1},{1,0},{2,3},{3,2},{4,5},{5,4},{6,7},{7,6},{8,9},{9,8},{10,11... | collective-permute-start | bytes 393224 | tf_op jit(solution)/shard_map/ppermute | solution.py:379
Sparse Core Ops, SparseCore 0:
  10.7 36.4 all-gather.2
  101.2 43.1 reduce-scatter.1

commit v5 on v4

--- a/solution.py
+++ b/solution.py
@@ -13,7 +13,7 @@
 HALF = ROWS // 2
 PAIR = 2 * HEAD
 ACTIONS = 128
-TILES = 41
+TILES = 32
 CHUNK = 65
 f32, bf16 = jnp.float32, jnp.bfloat16
 BOTH = ("tm", "dp")
@@ -44,6 +44,10 @@
 
 def turn_y(step):
     return [(dp_of(y, zh, c), dp_of((y + step) % NY, zh, c)) for y in YS for zh in ZHS for c in CS]
+
+
+def swap_y(bit):
+    return [(dp_of(y, zh, c), dp_of(y ^ bit, zh, c)) for y in YS for zh in ZHS for c in CS]
 
 
 def turn_x(step):
@@ -101,6 +105,12 @@
             out[f * CHUNK + k * 8:f * CHUNK + k * 8 + 8, :] = video[rows, cols] + row[:, cols]
             out[f * CHUNK + 32 + k * 8:f * CHUNK + 40 + k * 8, :] = og[rows, cols]
         out[f * CHUNK + 64:f * CHUNK + 65, :] = tag
+
+
+def unpack_kernel(tiles, out):
+    for f in range(FRAMES):
+        for k in range(D // 128):
+            out[f * OWN:f * OWN + OWN, k * 128:k * 128 + 128] = tiles[f, k]
 
 
 def weights_kernel(place, own, far_mine, far_other, high, low):
@@ -120,13 +130,15 @@
 
 
 def sublayer_kernel(
-    slopes, tiles, gain, spacing, high_in, low_in,
-    grads_out, tokens_out,
-    grads, tokens_new, sems, high, low, emb_ref, og, qkv_h, qkv_l, gm_h, gm_l, mixed, gr_h, gr_l,
+    tiles, extras_in, high_in, low_in,
+    grads_out, tokens_out, tables,
+    grads, tokens_new, sems, extras, high, low, emb_ref, og, qkv_h, qkv_l, gm_h, gm_l, mixed, gr_h, gr_l,
 ):
     arrivals = [
-        pltpu.make_async_copy(source, target, sems.at[18 + i])
-        for i, (source, target) in enumerate(((high_in, high), (low_in, low)))
+        pltpu.make_async_copy(source, target, sems.at[17 + i])
+        for i, (source, target) in enumerate(
+            ((extras_in, extras), (high_in, high), (low_in, low))
+        )
     ]
     for copy in arrivals:
         copy.start()
@@ -139,9 +151,12 @@
 
     emb = emb_ref[...]
     scale = lax.rsqrt(jnp.mean(emb * emb, axis=1, keepdims=True) + 1e-06)
-    normed = emb * gain[...] * scale
+    arrivals[0].wait()
+    spacing = extras[:HALF, :]
+    gain = jnp.concatenate([extras[HALF + HEADS + i:HALF + HEADS + i + 1, :] for i in range(4)], axis=1)
+    normed = emb * gain * scale
     parts = split(normed)
-    for copy in arrivals:
+    for copy in arrivals[1:]:
         copy.wait()
     for block in range(QKV // 256):
         cols = slice(block * 256, block * 256 + 256)
@@ -180,7 +195,7 @@
 
     for pair in range(HEADS // 2):
         slope = jnp.concatenate(
-            [slopes[pair * 2] * spacing[...], slopes[pair * 2 + 1] * spacing[...]], axis=0
+            [extras[HALF + pair * 2 + i:HALF + pair * 2 + i + 1, :] * spacing for i in range(2)], axis=0
         )
         at = [slice(kind * D + pair * PAIR, kind * D + (pair + 1) * PAIR) for kind in range(3)]
         for g in range(2):
@@ -222,6 +237,32 @@
         for zh in ZHS:
             send_tiles((zh * 8 + block) * 2, 2, block * 2 + zh)
 
+    gn = dot3((gr_h[...], gr_l[...]), (high[:, :QKV], low[:, :QKV]), NT)
+    gain_sum = jnp.sum(gn * emb * scale, axis=0, keepdims=True)
+    u = gn * gain
+    along = jnp.sum(u * emb, axis=1, keepdims=True) * (scale * scale * scale) * (1.0 / D)
+    tokens = og[...] + (u * scale - emb * along)
+    total = jnp.zeros((FRAMES, D), f32)
+    for p in range(OWN):
+        piece = tokens[p * FRAMES:(p + 1) * FRAMES, :]
+        for k in range(4):
+            tokens_new[pl.ds(k * 8 + p, FRAMES, stride=32), :] = piece[:, k * 128:(k + 1) * 128]
+        total = total + piece
+    copies.append(pltpu.make_async_copy(tokens_new, tokens_out, sems.at[16]))
+    copies[-1].start()
+    total_h, total_l = split(total)
+    table = dot(pick, total_h) + dot(pick, total_l)
+    gain_tile = jnp.concatenate(
+        [gain_sum[:, i * 64:(i + 1) * 64] for i in range(8)], axis=0
+    )
+    gain_tile = jnp.concatenate([gain_tile, jnp.zeros((8, 64), f32)], axis=1
+    )
+    for x in XS:
+        for side in CS:
+            for k in range(8):
+                r, start = x * 32 + (k // 2) * 8, side * 256 + (k % 2) * 128
+                tables[side, x, k] = table[r:r + 8, start:start + 128]
+            tables[side, x, 8] = gain_tile
     normt = split(jnp.transpose(normed))
     for block in range(QKV // 256):
         cols = slice(block * 256, block * 256 + 256)
@@ -230,36 +271,6 @@
     for block in range(2):
         cols = slice(block * 256, block * 256 + 256)
         place_columns(6 + block, dot3(mixt, (og_parts[0][:, cols], og_parts[1][:, cols])))
-
-    gn = dot3((gr_h[...], gr_l[...]), (high[:, :QKV], low[:, :QKV]), NT)
-    gain_sum = jnp.sum(gn * emb * scale, axis=0, keepdims=True)
-    u = gn * gain[...]
-    along = jnp.sum(u * emb, axis=1, keepdims=True) * (scale * scale * scale) * (1.0 / D)
-    tokens = og[...] + (u * scale - emb * along)
-    total = jnp.zeros((FRAMES, D), f32)
-    for p in range(OWN):
-        piece = tokens[p * FRAMES:(p + 1) * FRAMES, :]
-        for k in range(4):
-            tokens_new[pl.ds(k * 8 + p, FRAMES, stride=32), :] = piece[:, k * 128:(k + 1) * 128]
-        total = total + piece
-    copies.append(pltpu.make_async_copy(tokens_new, tokens_out, sems.at[17]))
-    copies[-1].start()
-    total_h, total_l = split(total)
-    table = dot(pick, total_h) + dot(pick, total_l)
-    gain_tile = jnp.concatenate(
-        [gain_sum[:, i * 64:(i + 1) * 64] for i in range(8)], axis=0
-    )
-    gain_tile = jnp.concatenate([gain_tile, jnp.zeros((8, 64), f32)], axis=1
-    )
-    for x in XS:
-        for side in CS:
-            for k in range(8):
-                r, start = x * 32 + (k // 2) * 8, side * 256 + (k % 2) * 128
-                for y in YS:
-                    grads[y * 2 + side, x, 32 + k] = table[r:r + 8, start:start + 128]
-            for y in YS:
-                grads[y * 2 + side, x, 40] = gain_tile
-    send_tiles(32, 9, 16)
     for copy in copies:
         copy.wait()
 
@@ -335,13 +346,22 @@
     j = lax.broadcasted_iota(jnp.int32, (HALF, HALF), 1)
     seen = (i // FRAMES == j // FRAMES) & (j <= i)
     spacing = jnp.where(seen, times[:, None] - times[None, :], f32(1e30))
-
-    grads, tokens_back = call(
+    extras = jnp.concatenate(
+        [
+            spacing, jnp.broadcast_to(slopes[:, None], (HEADS, 128)),
+            norm_gain.reshape(4, 128), jnp.zeros((4, 128), f32),
+        ]
+    )
+
+    grads, tokens_back, tables = call(
         sublayer_kernel,
-        [shape(NY * NC, NX, TILES, 8, 128), shape(ROWS * 4, 128)],
+        [
+            shape(NY * NC, NX, TILES, 8, 128), shape(ROWS * 4, 128),
+            shape(NC, NX, 9, 8, 128),
+        ],
         [
             pltpu.VMEM((NY * NC, NX, TILES, 8, 128), f32), pltpu.VMEM((ROWS * 4, 128), f32),
-            pltpu.SemaphoreType.DMA((20,)),
+            pltpu.SemaphoreType.DMA((20,)), pltpu.VMEM((HALF + 16, 128), f32),
             pltpu.VMEM((D, QKV + D), bf16), pltpu.VMEM((D, QKV + D), bf16),
             pltpu.VMEM((ROWS, D), f32), pltpu.VMEM((ROWS, D), f32),
             pltpu.VMEM((ROWS, QKV), bf16), pltpu.VMEM((ROWS, QKV), bf16),
@@ -349,22 +369,32 @@
             pltpu.VMEM((ROWS, D), f32),
             pltpu.VMEM((ROWS, QKV), bf16), pltpu.VMEM((ROWS, QKV), bf16),
         ],
-        (slopes,),
-        tiles.reshape(FRAMES * CHUNK, 128), norm_gain.reshape(1, D), spacing, high, low,
-        name="sublayer", far_ins=2, far_outs=2, limit=52,
-    )
-    grad_tokens = exchange(tokens_back.reshape(FRAMES, 4, OWN, 128), "tm")
+        (),
+        tiles.reshape(FRAMES * CHUNK, 128), extras, high, low,
+        name="sublayer", far_ins=3, far_outs=2, limit=52,
+    )
+    tokens_there = exchange(tokens_back.reshape(FRAMES, 4, OWN, 128), "tm")
 
     row = lax.psum_scatter(
         grads, "dp", scatter_dimension=0, axis_index_groups=YC_GROUPS, tiled=True
     ).reshape(NX, TILES, 8, 128)
-    row, grad_tokens = lax.optimization_barrier((row, grad_tokens))
+    part = lax.dynamic_index_in_dim(tables, c, 0, False) + lax.ppermute(
+        lax.dynamic_index_in_dim(tables, 1 - c, 0, False), "dp", SWAP_CORE
+    )
+    for bit in (1, 2):
+        part = part + lax.ppermute(part, "dp", swap_y(bit))
+    part, tokens_there = lax.optimization_barrier((part, tokens_there))
+    part = jnp.sum(exchange(part, "tm", X_GROUPS), axis=0)
+    grad_tokens = call(
+        unpack_kernel, [shape(ROWS, D)], [], (), tokens_there, name="unpack"
+    )[0]
+    row, part, grad_tokens = lax.optimization_barrier((row, part, grad_tokens))
     plane = jnp.sum(exchange(row, "tm", X_GROUPS), axis=0)
     column = jnp.concatenate(
         [
-            plane[:32].reshape(16, 16, 1, 128),
-            jnp.tile(plane[32:40], (2, 1, 1)).reshape(16, 8, 1, 128),
-            jnp.tile(plane[40], (2, 1)).reshape(16, 1, 1, 128),
+            plane.reshape(16, 16, 1, 128),
+            jnp.tile(part[:8], (2, 1, 1)).reshape(16, 8, 1, 128),
+            jnp.tile(part[8], (2, 1)).reshape(16, 1, 1, 128),
         ],
         axis=1,
     )
@@ -381,7 +411,7 @@
         c == 0, jnp.concatenate([half, other], axis=1), jnp.concatenate([other, half], axis=1)
     )
     return (
-        grad_tokens.transpose(0, 2, 1, 3).reshape(1, 1, ROWS, D),
+        grad_tokens.reshape(1, 1, ROWS, D),
         main[:, :QKV],
         main[:, QKV:],
         grad_table,

time: 227 us -> 225 us (level)
  blocking collectives: 101 us -> 51.7 us
  starting transfers between devices: 50 us -> 73.6 us
  waiting for transfers between devices: 28.7 us -> 49.3 us
    all_to_all x5 -> x3, blocking collectives: 101 us -> 51.7 us  [exchange(): lax.all_to_all(value, axis, 0, 0, axis_index_groups=groups, tiled=True)]
    all_to_all x1 -> x4, waiting for transfers between devices: 3.82 us -> 20.5 us  [exchange(): lax.all_to_all(value, axis, 0, 0, axis_index_groups=groups, tiled=True)]
    all_to_all x1 -> x4, starting transfers between devices: 7.6 us -> 22.5 us  [exchange(): lax.all_to_all(value, axis, 0, 0, axis_index_groups=groups, tiled=True)]
    ppermute x0 -> x3, waiting for transfers between devices: none -> 14.2 us  [the longest x2 13.3 us: shards(): part = part + lax.ppermute(part, 'dp', swap_y(bit))]
    reduce_scatter x1, waiting for transfers between devices: 7.79 us -> 0.02 us  [shards(): lax.psum_scatter(grads, 'dp', scatter_dimension=0, axis_index_groups=YC_G...]
    ppermute x0 -> x3, starting transfers between devices: none -> 7.47 us  [the longest x2 4.91 us: shards(): part = part + lax.ppermute(part, 'dp', swap_y(bit))]
    ppermute x3, waiting for transfers between devices: 5.98 us -> 2.55 us  [far_weights(): lax.ppermute(quarter, 'tm', turn_x(i))]
    pallas_call x5 -> x6, Pallas kernels: 24.9 us -> 26.3 us  [call(): pl.pallas_call(kernel, out_shape=outs, in_specs=[smem] * len(scalars) + [...]
  transfers between devices with their start and end apart: 12 -> 18, of which waited for: 7 -> 11; matrix products, arithmetic and copies ran while one was open for 1% -> 2% of each run, Pallas kernels for 4% -> 5%
where the time goes in v5:
time: 225 us; the launch traced here: 224 us
  starting transfers between devices  73.6 us (33%)
  blocking collectives  51.7 us (23%)
  waiting for transfers between devices  49.3 us (22%)
  Pallas kernels  26.3 us (12%)
  between operations  15.2 us (7%)
  local copies, waits for them, and re-layouts  4.08 us (2%)
  other arithmetic  3.49 us (2%)
    all_to_all x3, blocking collectives, exchange(): lax.all_to_all(value, axis, 0, 0, axis_index_groups=groups, tiled=True)  51.7 us
    pallas_call x6, Pallas kernels, call(): pl.pallas_call(kernel, out_shape=outs, in_specs=[smem] * len(scalars) + [...  26.3 us
    all_to_all x4, starting transfers between devices, exchange(): lax.all_to_all(value, axis, 0, 0, axis_index_groups=groups, tiled=True)  22.5 us
    all_to_all x4, waiting for transfers between devices, exchange(): lax.all_to_all(value, axis, 0, 0, axis_index_groups=groups, tiled=True)  20.5 us
    ppermute x1, starting transfers between devices, shards(): quarter = lax.ppermute(quarter, 'dp', SWAP_ZH)  15.4 us
    ppermute x2, waiting for transfers between devices, shards(): part = part + lax.ppermute(part, 'dp', swap_y(bit))  13.3 us
    ppermute x3, starting transfers between devices, far_weights(): lax.ppermute(quarter, 'tm', turn_x(i))  10.7 us
    ppermute x3, waiting for transfers between devices, far_weights(): lax.ppermute(row, 'dp', turn_y(i))  10.1 us
  transfers between devices with their start and end apart: 18, of which 11 were waited for; matrix products, arithmetic and copies ran while one was open for 2% of the time, Pallas kernels for 5%

profile of v5, /device:TPU:25, one launch (start us, length us, event | category | flops | bytes accessed | tf_op | source)
XLA Modules:
  0.0 223.6 jit_solution(7702291665607684599)
XLA Ops:
  9.6 15.4 %collective-permute-start = (f32[8,2048]{1,0:T(8,128)}, f32[8,2048]{1,0:T(8,128)S(1)}, u32[]{:S(2)}, u32[]{:S(2)}) collective-permute-start(f32[8,2048]{1,0:T(8,128)} %get-tuple-element.19), channel_id=1, source_target_pairs={{0,2},{1,3},{2,0},{3,1},{4,6},{5,7},{6,4},{7,5},{8,10},{9,11},{10,... | collective-permute-start | bytes 196616 | tf_op jit(solution)/shard_map/ppermute | solution.py:322
  25.7 2.4 %pack.1 = f32[2080,128]{1,0:T(8,128)} custom-call(s32[1]{0:T(128)} %bitcast.38.action, f32[128,512]{1,0:T(8,128)} %act_table.1, f32[256,512]{1,0:T(8,128)} %bitcast.49, f32[256,512]{1,0:T(8,128)} %bitcast.50), custom_call_target="tpu_custom_call" | custom-call | tf_op jit(solution)/shard_map/pack/pallas_call | solution.py:282
  28.0 7.6 %all-to-all-start = ((f32[32,65,1,128]{3,2,1,0:T(1,128)}), f32[32,65,1,128]{3,2,1,0:T(1,128)S(1)}, u32[]{:S(2)}, u32[]{:S(2)}) async-start(f32[32,65,1,128]{3,2,1,0:T(1,128)} %bitcast.40), calls=%async_computation | async-start | bytes 2129920 | tf_op jit(solution)/shard_map/all_to_all | solution.py:58
  37.8 3.3 %collective-permute-start.1 = (f32[8,2048]{1,0:T(8,128)}, f32[8,2048]{1,0:T(8,128)S(1)}, u32[]{:S(2)}, u32[]{:S(2)}) collective-permute-start(f32[8,2048]{1,0:T(8,128)} %swapped.1), channel_id=1, source_target_pairs={{0,128},{16,144},{32,160},{48,176},{64,192},{80,208},{96,224},{112... | collective-permute-start | bytes 196616 | tf_op jit(solution)/shard_map/ppermute | solution.py:300
  41.0 4.3 %collective-permute-start.2 = (f32[8,2048]{1,0:T(8,128)}, f32[8,2048]{1,0:T(8,128)S(1)}, u32[]{:S(2)}, u32[]{:S(2)}) collective-permute-start(f32[8,2048]{1,0:T(8,128)} %swapped.1), channel_id=1, source_target_pairs={{0,256},{16,272},{32,288},{48,304},{64,320},{80,336},{96,352},{112... | collective-permute-start | bytes 196616 | tf_op jit(solution)/shard_map/ppermute | solution.py:300
  45.4 3.1 %collective-permute-start.3 = (f32[8,2048]{1,0:T(8,128)}, f32[8,2048]{1,0:T(8,128)S(1)}, u32[]{:S(2)}, u32[]{:S(2)}) collective-permute-start(f32[8,2048]{1,0:T(8,128)} %swapped.1), channel_id=1, source_target_pairs={{0,384},{16,400},{32,416},{48,432},{64,448},{80,464},{96,480},{112... | collective-permute-start | bytes 196616 | tf_op jit(solution)/shard_map/ppermute | solution.py:300
  48.5 2.5 %collective-permute-done.3 = f32[8,2048]{1,0:T(8,128)S(1)} collective-permute-done((f32[8,2048]{1,0:T(8,128)}, f32[8,2048]{1,0:T(8,128)S(1)}, u32[]{:S(2)}, u32[]{:S(2)}) %collective-permute-start.3) | collective-permute-done | bytes 65568 | tf_op jit(solution)/shard_map/ppermute | solution.py:300
  51.9 1.9 collective-permute-start.4
  53.8 4.1 %collective-permute-start.5 = (f32[4,8,2048]{2,1,0:T(8,128)S(1)}, f32[4,8,2048]{2,1,0:T(8,128)S(1)}, u32[]{:S(2)}, u32[]{:S(2)}) collective-permute-start(f32[4,8,2048]{2,1,0:T(8,128)S(1)} %pad_maximum_fusion), channel_id=1, source_target_pairs={{0,8},{1,9},{2,10},{3,11},{4,12},{5,13},{6,14},{7,15},{8,0},{9,1},... | collective-permute-start | bytes 786440 | tf_op jit(solution)/shard_map/ppermute | solution.py:302
  58.0 1.9 collective-permute-start.6
  60.0 2.8 %collective-permute-done.5 = f32[4,8,2048]{2,1,0:T(8,128)S(1)} collective-permute-done((f32[4,8,2048]{2,1,0:T(8,128)S(1)}, f32[4,8,2048]{2,1,0:T(8,128)S(1)}, u32[]{:S(2)}, u32[]{:S(2)}) %collective-permute-start.5) | collective-permute-done | bytes 262176 | tf_op jit(solution)/shard_map/ppermute | solution.py:302
  62.8 7.3 %collective-permute-done.6 = f32[4,8,2048]{2,1,0:T(8,128)S(1)} collective-permute-done((f32[4,8,2048]{2,1,0:T(8,128)S(1)}, f32[4,8,2048]{2,1,0:T(8,128)S(1)}, u32[]{:S(2)}, u32[]{:S(2)}) %collective-permute-start.6) | collective-permute-done | bytes 262176 | tf_op jit(solution)/shard_map/ppermute | solution.py:302
  70.1 4.4 %collective-permute-start.7 = (f32[16,8,2048]{2,1,0:T(8,128)S(1)}, f32[16,8,2048]{2,1,0:T(8,128)S(1)}, u32[]{:S(2)}, u32[]{:S(2)}) collective-permute-start(f32[16,8,2048]{2,1,0:T(8,128)S(1)} %constant_dynamic-update-slice_fusion.far_mine), channel_id=1, source_target_pairs={{0,1},{1,0},{2,3},{3,2},{4,5},{5,4},{6,7},{7,6},{8,9},{9,8},{10,11... | collective-permute-start | bytes 3145736 | tf_op jit(solution)/shard_map/ppermute | solution.py:303
  77.8 5.0 %weights.1 = (bf16[512,2048]{1,0:T(8,128)(2,1)}, bf16[512,2048]{1,0:T(8,128)(2,1)}) custom-call(s32[4]{0:T(128)} %pad_add_fusion.place, f32[8,32,2048]{2,1,0:T(8,128)} %bitcast.41, f32[16,8,2048]{2,1,0:T(8,128)} %copy-done.1, f32[16,8,2048]{2,1,0:T(8,128)} %copy-done.2), custom_call_target="tpu_custom_call" | custom-call | tf_op jit(solution)/shard_map/weights/pallas_call | solution.py:282
  82.8 3.8 %all-to-all-done = f32[32,65,1,128]{3,2,1,0:T(1,128)S(1)} async-done(((f32[32,65,1,128]{3,2,1,0:T(1,128)}), f32[32,65,1,128]{3,2,1,0:T(1,128)S(1)}, u32[]{:S(2)}, u32[]{:S(2)}) %all-to-all-start) | async-done | bytes 1064992 | tf_op jit(solution)/shard_map/all_to_all | solution.py:58
  86.6 13.9 %sublayer.1 = (f32[8,4,32,8,128]{4,3,2,1,0:T(8,128)}, f32[1024,128]{1,0:T(8,128)}, f32[2,4,9,8,128]{4,3,2,1,0:T(8,128)S(1)}) custom-call(f32[2080,128]{1,0:T(8,128)S(1)} %bitcast.39, f32[144,128]{1,0:T(8,128)S(1)} %maximum_maximum_fusion.extras_in, bf16[512,2048]{1,0:T(8,128)(2,1)} %get-tuple-element.23.high_in, bf16[512,2048]{1,0:T(8,128)(2,1)} %get-tuple-element.24.low_in), custom_call_target="tpu_custom_call" | custom-call | tf_op jit(solution)/shard_map/sublayer/pallas_call | solution.py:282
  100.6 8.1 %all-to-all-start.1 = ((f32[32,4,8,128]{3,2,1,0:T(8,128)}), f32[32,4,8,128]{3,2,1,0:T(8,128)S(1)}, u32[]{:S(2)}, u32[]{:S(2)}) async-start(f32[32,4,8,128]{3,2,1,0:T(8,128)} %bitcast.19), calls=%async_computation.2 | async-start | bytes 1048576 | tf_op jit(solution)/shard_map/all_to_all | solution.py:58
  108.7 2.6 %collective-permute-start.8 = (f32[4,9,8,128]{3,2,1,0:T(8,128)S(1)}, f32[4,9,8,128]{3,2,1,0:T(8,128)S(1)}, u32[]{:S(2)}, u32[]{:S(2)}) collective-permute-start(f32[4,9,8,128]{3,2,1,0:T(8,128)S(1)} %dynamic-slice_bitcast_fusion), channel_id=1, source_target_pairs={{0,1},{1,0},{2,3},{3,2},{4,5},{5,4},{6,7},{7,6},{8,9},{9,8},{10,11... | collective-permute-start | bytes 442376 | tf_op jit(solution)/shard_map/ppermute | solution.py:381
  112.3 1.9 collective-permute-start.9
  114.2 6.6 %collective-permute-done.9 = f32[4,9,8,128]{3,2,1,0:T(8,128)S(1)} collective-permute-done((f32[4,9,8,128]{3,2,1,0:T(8,128)S(1)}, f32[4,9,8,128]{3,2,1,0:T(8,128)S(1)}, u32[]{:S(2)}, u32[]{:S(2)}) %collective-permute-start.9) | collective-permute-done | bytes 147488 | tf_op jit(solution)/shard_map/ppermute | solution.py:385
  120.8 3.0 %collective-permute-start.10 = (f32[4,9,8,128]{3,2,1,0:T(8,128)S(1)}, f32[4,9,8,128]{3,2,1,0:T(8,128)S(1)}, u32[]{:S(2)}, u32[]{:S(2)}) collective-permute-start(f32[4,9,8,128]{3,2,1,0:T(8,128)S(1)} %add.38), channel_id=1, source_target_pairs={{0,8},{1,9},{2,10},{3,11},{4,12},{5,13},{6,14},{7,15},{8,0},{9,1},... | collective-permute-start | bytes 442376 | tf_op jit(solution)/shard_map/ppermute | solution.py:385
  123.8 6.7 %collective-permute-done.10 = f32[4,9,8,128]{3,2,1,0:T(8,128)S(1)} collective-permute-done((f32[4,9,8,128]{3,2,1,0:T(8,128)S(1)}, f32[4,9,8,128]{3,2,1,0:T(8,128)S(1)}, u32[]{:S(2)}, u32[]{:S(2)}) %collective-permute-start.10) | collective-permute-done | bytes 147488 | tf_op jit(solution)/shard_map/ppermute | solution.py:385
  131.1 6.9 %all-to-all-done.1.tiles = f32[32,4,8,128]{3,2,1,0:T(8,128)S(1)} async-done(((f32[32,4,8,128]{3,2,1,0:T(8,128)}), f32[32,4,8,128]{3,2,1,0:T(8,128)S(1)}, u32[]{:S(2)}, u32[]{:S(2)}) %all-to-all-start.1) | async-done | bytes 524320 | tf_op jit(solution)/shard_map/all_to_all | solution.py:58
  138.0 3.3 %all-to-all-start.2 = ((f32[4,9,8,128]{3,2,1,0:T(8,128)}), f32[4,9,8,128]{3,2,1,0:T(8,128)S(1)}, u32[]{:S(2)}, u32[]{:S(2)}) async-start(f32[4,9,8,128]{3,2,1,0:T(8,128)} %add.39), calls=%async_computation.3 | async-start | bytes 294912 | tf_op jit(solution)/shard_map/all_to_all | solution.py:58
  141.4 1.9 unpack.1
  143.2 3.0 %all-to-all-done.2 = f32[4,9,8,128]{3,2,1,0:T(8,128)S(1)} async-done(((f32[4,9,8,128]{3,2,1,0:T(8,128)}), f32[4,9,8,128]{3,2,1,0:T(8,128)S(1)}, u32[]{:S(2)}, u32[]{:S(2)}) %all-to-all-start.2) | async-done | bytes 147488 | tf_op jit(solution)/shard_map/all_to_all | solution.py:58
  146.3 3.5 %all-to-all-start.3 = ((f32[4,32,8,128]{3,2,1,0:T(8,128)}), f32[4,32,8,128]{3,2,1,0:T(8,128)S(1)}, u32[]{:S(2)}, u32[]{:S(2)}) async-start(f32[4,32,8,128]{3,2,1,0:T(8,128)} %bitcast.46), calls=%async_computation.4 | async-start | bytes 1048576 | tf_op jit(solution)/shard_map/all_to_all | solution.py:58
  149.8 6.9 %all-to-all-done.3 = f32[4,32,8,128]{3,2,1,0:T(8,128)S(1)} async-done(((f32[4,32,8,128]{3,2,1,0:T(8,128)}), f32[4,32,8,128]{3,2,1,0:T(8,128)S(1)}, u32[]{:S(2)}, u32[]{:S(2)}) %all-to-all-start.3) | async-done | bytes 524320 | tf_op jit(solution)/shard_map/all_to_all | solution.py:58
  156.9 24.8 %all_to_all.35 = f32[16,25,1,128]{3,2,1,0:T(1,128)S(1)} all-to-all(f32[16,25,1,128]{3,2,1,0:T(1,128)S(1)} %pad_maximum_fusion.1), channel_id=1, replica_groups={{0,16,32,48,64,80,96,112,2,18,34,50,66,82,98,114},{1,17,33,49,65,81,97,..., dimensions={0} | all-to-all | bytes 409600 | tf_op jit(solution)/shard_map/all_to_all | solution.py:58
  181.9 18.2 %all_to_all.36 = f32[8,25,1,128]{3,2,1,0:T(1,128)S(1)} all-to-all(f32[8,25,1,128]{3,2,1,0:T(1,128)S(1)} %broadcast_in_dim.22), channel_id=1, replica_groups={{0,16,32,48,64,80,96,112},{128,144,160,176,192,208,224,240},{256,272,28..., dimensions={0} | all-to-all | bytes 204800 | tf_op jit(solution)/shard_map/all_to_all | solution.py:58
  200.2 8.6 %all_to_all.37 = f32[4,8,3,8,128]{4,3,2,1,0:T(8,128)S(1)} all-to-all(f32[4,8,3,8,128]{4,3,2,1,0:T(8,128)S(1)} %broadcast_in_dim.23), channel_id=1, replica_groups={{0,128,256,384},{16,144,272,400},{32,160,288,416},{48,176,304,432},{64,..., dimensions={0} | all-to-all | bytes 786432 | tf_op jit(solution)/shard_map/all_to_all | solution.py:58
  208.9 5.1 %collective-permute-start.11 = (f32[128,256]{1,0:T(8,128)S(1)}, f32[128,256]{1,0:T(8,128)S(1)}, u32[]{:S(2)}, u32[]{:S(2)}) collective-permute-start(f32[128,256]{1,0:T(8,128)S(1)} %bitcast.44), channel_id=1, source_target_pairs={{0,1},{1,0},{2,3},{3,2},{4,5},{5,4},{6,7},{7,6},{8,9},{9,8},{10,11... | collective-permute-start | bytes 393224 | tf_op jit(solution)/shard_map/ppermute | solution.py:409
  (67 shorter events, 13.6 us)
Async XLA Ops:
  7.2 44.7 %all-gather.3.cloned.1.call-start = ((), (), s32[]{:S(2)}) async-start(), calls=%async_computation.9 | async-start | bytes 2359296 | tf_op jit(solution)/shard_map/all_gather | solution.py:321
  9.6 26.1 %collective-permute-start = (f32[8,2048]{1,0:T(8,128)}, f32[8,2048]{1,0:T(8,128)S(1)}, u32[]{:S(2)}, u32[]{:S(2)}) collective-permute-start(f32[8,2048]{1,0:T(8,128)} %get-tuple-element.19), channel_id=1, source_target_pairs={{0,2},{1,3},{2,0},{3,1},{4,6},{5,7},{6,4},{7,5},{8,10},{9,11},{10,... | collective-permute-start | bytes 196616 | tf_op jit(solution)/shard_map/ppermute | solution.py:322
  28.0 58.6 %all-to-all-start = ((f32[32,65,1,128]{3,2,1,0:T(1,128)}), f32[32,65,1,128]{3,2,1,0:T(1,128)S(1)}, u32[]{:S(2)}, u32[]{:S(2)}) async-start(f32[32,65,1,128]{3,2,1,0:T(1,128)} %bitcast.40), calls=%async_computation | async-start | bytes 2129920 | tf_op jit(solution)/shard_map/all_to_all | solution.py:58
  35.6 110.6 %reduce-scatter.2.cloned.1.call-start = ((), (), s32[]{:S(2)}) async-start(), calls=%async_computation.8 | async-start | bytes 4718592 | tf_op jit(solution)/shard_map/reduce_scatter | solution.py:378
  35.7 0.6 copy-start.5
  37.8 36.7 %copy-start.6 = (s32[1,32]{1,0:T(1,128)S(1)}, s32[1,32]{1,0:T(1,128)}, u32[]{:S(2)}) copy-start(s32[1,32]{1,0:T(1,128)} %param.11) | copy-start | bytes 388
  37.8 36.9 %copy-start.4 = (f32[8]{0:T(128)S(1)}, f32[8]{0:T(128)}, u32[]{:S(2)}) copy-start(f32[8]{0:T(128)} %param.16) | copy-start | bytes 100
  37.8 37.1 %copy-start.3 = (f32[512]{0:T(512)S(1)}, f32[512]{0:T(512)}, u32[]{:S(2)}) copy-start(f32[512]{0:T(512)} %param.13) | copy-start | bytes 6148
  37.8 10.7 %collective-permute-start.1 = (f32[8,2048]{1,0:T(8,128)}, f32[8,2048]{1,0:T(8,128)S(1)}, u32[]{:S(2)}, u32[]{:S(2)}) collective-permute-start(f32[8,2048]{1,0:T(8,128)} %swapped.1), channel_id=1, source_target_pairs={{0,128},{16,144},{32,160},{48,176},{64,192},{80,208},{96,224},{112... | collective-permute-start | bytes 196616 | tf_op jit(solution)/shard_map/ppermute | solution.py:300
  41.0 7.4 %collective-permute-start.2 = (f32[8,2048]{1,0:T(8,128)}, f32[8,2048]{1,0:T(8,128)S(1)}, u32[]{:S(2)}, u32[]{:S(2)}) collective-permute-start(f32[8,2048]{1,0:T(8,128)} %swapped.1), channel_id=1, source_target_pairs={{0,256},{16,272},{32,288},{48,304},{64,320},{80,336},{96,352},{112... | collective-permute-start | bytes 196616 | tf_op jit(solution)/shard_map/ppermute | solution.py:300
  45.4 5.6 %collective-permute-start.3 = (f32[8,2048]{1,0:T(8,128)}, f32[8,2048]{1,0:T(8,128)S(1)}, u32[]{:S(2)}, u32[]{:S(2)}) collective-permute-start(f32[8,2048]{1,0:T(8,128)} %swapped.1), channel_id=1, source_target_pairs={{0,384},{16,400},{32,416},{48,432},{64,448},{80,464},{96,480},{112... | collective-permute-start | bytes 196616 | tf_op jit(solution)/shard_map/ppermute | solution.py:300
  51.9 8.0 %collective-permute-start.4 = (f32[4,8,2048]{2,1,0:T(8,128)S(1)}, f32[4,8,2048]{2,1,0:T(8,128)S(1)}, u32[]{:S(2)}, u32[]{:S(2)}) collective-permute-start(f32[4,8,2048]{2,1,0:T(8,128)S(1)} %pad_maximum_fusion), channel_id=1, source_target_pairs={{0,4},{1,5},{2,6},{3,7},{4,8},{5,9},{6,10},{7,11},{8,12},{9,13},{1... | collective-permute-start | bytes 786440 | tf_op jit(solution)/shard_map/ppermute | solution.py:302
  53.8 8.9 %collective-permute-start.5 = (f32[4,8,2048]{2,1,0:T(8,128)S(1)}, f32[4,8,2048]{2,1,0:T(8,128)S(1)}, u32[]{:S(2)}, u32[]{:S(2)}) collective-permute-start(f32[4,8,2048]{2,1,0:T(8,128)S(1)} %pad_maximum_fusion), channel_id=1, source_target_pairs={{0,8},{1,9},{2,10},{3,11},{4,12},{5,13},{6,14},{7,15},{8,0},{9,1},... | collective-permute-start | bytes 786440 | tf_op jit(solution)/shard_map/ppermute | solution.py:302
  58.0 12.1 %collective-permute-start.6 = (f32[4,8,2048]{2,1,0:T(8,128)S(1)}, f32[4,8,2048]{2,1,0:T(8,128)S(1)}, u32[]{:S(2)}, u32[]{:S(2)}) collective-permute-start(f32[4,8,2048]{2,1,0:T(8,128)S(1)} %pad_maximum_fusion), channel_id=1, source_target_pairs={{0,12},{1,13},{2,14},{3,15},{4,0},{5,1},{6,2},{7,3},{8,4},{9,5},{1... | collective-permute-start | bytes 786440 | tf_op jit(solution)/shard_map/ppermute | solution.py:302
  70.1 6.7 %copy-start.1 = (f32[16,8,2048]{2,1,0:T(8,128)}, f32[16,8,2048]{2,1,0:T(8,128)S(1)}, u32[]{:S(2)}) copy-start(f32[16,8,2048]{2,1,0:T(8,128)S(1)} %constant_dynamic-update-slice_fusion.far_mine) | copy-start | bytes 3145732
  70.1 6.7 %collective-permute-start.7 = (f32[16,8,2048]{2,1,0:T(8,128)S(1)}, f32[16,8,2048]{2,1,0:T(8,128)S(1)}, u32[]{:S(2)}, u32[]{:S(2)}) collective-permute-start(f32[16,8,2048]{2,1,0:T(8,128)S(1)} %constant_dynamic-update-slice_fusion.far_mine), channel_id=1, source_target_pairs={{0,1},{1,0},{2,3},{3,2},{4,5},{5,4},{6,7},{7,6},{8,9},{9,8},{10,11... | collective-permute-start | bytes 3145736 | tf_op jit(solution)/shard_map/ppermute | solution.py:303
  76.8 1.0 copy-start.2
  100.6 37.4 %all-to-all-start.1 = ((f32[32,4,8,128]{3,2,1,0:T(8,128)}), f32[32,4,8,128]{3,2,1,0:T(8,128)S(1)}, u32[]{:S(2)}, u32[]{:S(2)}) async-start(f32[32,4,8,128]{3,2,1,0:T(8,128)} %bitcast.19), calls=%async_computation.2 | async-start | bytes 1048576 | tf_op jit(solution)/shard_map/all_to_all | solution.py:58
  108.7 3.6 %collective-permute-start.8 = (f32[4,9,8,128]{3,2,1,0:T(8,128)S(1)}, f32[4,9,8,128]{3,2,1,0:T(8,128)S(1)}, u32[]{:S(2)}, u32[]{:S(2)}) collective-permute-start(f32[4,9,8,128]{3,2,1,0:T(8,128)S(1)} %dynamic-slice_bitcast_fusion), channel_id=1, source_target_pairs={{0,1},{1,0},{2,3},{3,2},{4,5},{5,4},{6,7},{7,6},{8,9},{9,8},{10,11... | collective-permute-start | bytes 442376 | tf_op jit(solution)/shard_map/ppermute | solution.py:381
  112.3 8.5 %collective-permute-start.9 = (f32[4,9,8,128]{3,2,1,0:T(8,128)S(1)}, f32[4,9,8,128]{3,2,1,0:T(8,128)S(1)}, u32[]{:S(2)}, u32[]{:S(2)}) collective-permute-start(f32[4,9,8,128]{3,2,1,0:T(8,128)S(1)} %bitcast_add_fusion), channel_id=1, source_target_pairs={{0,4},{1,5},{2,6},{3,7},{4,0},{5,1},{6,2},{7,3},{8,12},{9,13},{10,... | collective-permute-start | bytes 442376 | tf_op jit(solution)/shard_map/ppermute | solution.py:385
  120.8 9.7 %collective-permute-start.10 = (f32[4,9,8,128]{3,2,1,0:T(8,128)S(1)}, f32[4,9,8,128]{3,2,1,0:T(8,128)S(1)}, u32[]{:S(2)}, u32[]{:S(2)}) collective-permute-start(f32[4,9,8,128]{3,2,1,0:T(8,128)S(1)} %add.38), channel_id=1, source_target_pairs={{0,8},{1,9},{2,10},{3,11},{4,12},{5,13},{6,14},{7,15},{8,0},{9,1},... | collective-permute-start | bytes 442376 | tf_op jit(solution)/shard_map/ppermute | solution.py:385
  138.0 3.3 %copy-start = (f32[32,4,8,128]{3,2,1,0:T(8,128)}, f32[32,4,8,128]{3,2,1,0:T(8,128)S(1)}, u32[]{:S(2)}) copy-start(f32[32,4,8,128]{3,2,1,0:T(8,128)S(1)} %all-to-all-done.1.tiles) | copy-start | bytes 1572868
  138.0 8.2 %all-to-all-start.2 = ((f32[4,9,8,128]{3,2,1,0:T(8,128)}), f32[4,9,8,128]{3,2,1,0:T(8,128)S(1)}, u32[]{:S(2)}, u32[]{:S(2)}) async-start(f32[4,9,8,128]{3,2,1,0:T(8,128)} %add.39), calls=%async_computation.3 | async-start | bytes 294912 | tf_op jit(solution)/shard_map/all_to_all | solution.py:58
  146.3 10.4 %all-to-all-start.3 = ((f32[4,32,8,128]{3,2,1,0:T(8,128)}), f32[4,32,8,128]{3,2,1,0:T(8,128)S(1)}, u32[]{:S(2)}, u32[]{:S(2)}) async-start(f32[4,32,8,128]{3,2,1,0:T(8,128)} %bitcast.46), calls=%async_computation.4 | async-start | bytes 1048576 | tf_op jit(solution)/shard_map/all_to_all | solution.py:58
  208.9 7.2 %collective-permute-start.11 = (f32[128,256]{1,0:T(8,128)S(1)}, f32[128,256]{1,0:T(8,128)S(1)}, u32[]{:S(2)}, u32[]{:S(2)}) collective-permute-start(f32[128,256]{1,0:T(8,128)S(1)} %bitcast.44), channel_id=1, source_target_pairs={{0,1},{1,0},{2,3},{3,2},{4,5},{5,4},{6,7},{7,6},{8,9},{9,8},{10,11... | collective-permute-start | bytes 393224 | tf_op jit(solution)/shard_map/ppermute | solution.py:409
Sparse Core Ops, SparseCore 0:
  10.7 36.4 all-gather.2
  100.7 43.3 reduce-scatter.1

commit v6 on v5

--- a/solution.py
+++ b/solution.py
@@ -83,19 +83,16 @@
             ]
 
 
-def shares_kernel(place, w_qkv, w_out, mine, quarter):
+def pass_kernel(value, out):
+    out[...] = value[...]
+
+
+def front_kernel(place, action, act_table, video, og, w_qkv, w_out, out, mine, quarter):
     mine[:, :QKV] = w_qkv[...]
     mine[:, QKV:] = w_out[...]
     x = pl.multiple_of(place[0] * 8, 8)
     quarter[:, :QKV] = w_qkv[pl.ds(x, 8), :]
     quarter[:, QKV:] = w_out[pl.ds(x, 8), :]
-
-
-def pass_kernel(value, out):
-    out[...] = value[...]
-
-
-def pack_kernel(action, act_table, video, og, out):
     row = act_table[pl.ds(action[0], 1), :]
     tag = jnp.zeros((1, 128), f32) + action[0].astype(f32)
     for f in range(FRAMES):
@@ -310,26 +307,18 @@
     x, y, zh, c = t // NZL, d // (NZH * NC), (d // NC) % NZH, d % NC
     place = jnp.stack([x, y, zh, c]).astype(jnp.int32)
 
-    mine, quarter = call(
-        shares_kernel,
-        [shape(32, QKV + D), shape(8, QKV + D)],
+    payload, mine, quarter = call(
+        front_kernel,
+        [shape(FRAMES * CHUNK, 128), shape(32, QKV + D), shape(8, QKV + D)],
         [],
-        (place,),
-        w_qkv, w_out,
-        name="shares",
+        (place, actions.reshape(1)),
+        act_table, video_tokens[0, 0], out_grad[0, 0], w_qkv, w_out,
+        name="front",
     )
     own = lax.all_gather(mine, "dp", axis_index_groups=YC_GROUPS)
     quarter = lax.ppermute(quarter, "dp", SWAP_ZH)
     quarter = call(
         pass_kernel, [shape(8, QKV + D)], [], (), quarter, name="swapped", work=20000000000
-    )[0]
-    payload = call(
-        pack_kernel,
-        [shape(FRAMES * CHUNK, 128)],
-        [],
-        (actions.reshape(1),),
-        act_table, video_tokens[0, 0], out_grad[0, 0],
-        name="pack",
     )[0]
     high, low = call(
         weights_kernel,

time: 225 us -> 223 us (level)
    pallas_call x6 -> x5, Pallas kernels: 26.3 us -> 24.7 us  [call(): pl.pallas_call(kernel, out_shape=outs, in_specs=[smem] * len(scalars) + [...]
  transfers between devices with their start and end apart: 18 -> 18, of which waited for: 11 -> 11; matrix products, arithmetic and copies ran while one was open for 2% -> 2% of each run, Pallas kernels for 5% -> 4%
where the time goes in v6:
time: 223 us; the launch traced here: 222 us
  starting transfers between devices  73.6 us (33%)
  blocking collectives  51.8 us (23%)
  waiting for transfers between devices  49.4 us (22%)
  Pallas kernels  24.7 us (11%)
  between operations  15.2 us (7%)
  local copies, waits for them, and re-layouts  4.08 us (2%)
  other arithmetic  3.49 us (2%)
    all_to_all x3, blocking collectives, exchange(): lax.all_to_all(value, axis, 0, 0, axis_index_groups=groups, tiled=True)  51.8 us
    pallas_call x5, Pallas kernels, call(): pl.pallas_call(kernel, out_shape=outs, in_specs=[smem] * len(scalars) + [...  24.7 us
    all_to_all x4, starting transfers between devices, exchange(): lax.all_to_all(value, axis, 0, 0, axis_index_groups=groups, tiled=True)  22.5 us
    all_to_all x4, waiting for transfers between devices, exchange(): lax.all_to_all(value, axis, 0, 0, axis_index_groups=groups, tiled=True)  20.6 us
    ppermute x1, starting transfers between devices, shards(): quarter = lax.ppermute(quarter, 'dp', SWAP_ZH)  15.4 us
    ppermute x2, waiting for transfers between devices, shards(): part = part + lax.ppermute(part, 'dp', swap_y(bit))  13.3 us
    ppermute x3, starting transfers between devices, far_weights(): lax.ppermute(quarter, 'tm', turn_x(i))  10.7 us
    ppermute x3, waiting for transfers between devices, far_weights(): lax.ppermute(row, 'dp', turn_y(i))  10.1 us
  transfers between devices with their start and end apart: 18, of which 11 were waited for; matrix products, arithmetic and copies ran while one was open for 2% of the time, Pallas kernels for 4%

profile of v6, /device:TPU:25, one launch (start us, length us, event | category | flops | bytes accessed | tf_op | source)
XLA Modules:
  0.0 222.3 jit_solution(15168102056940836386)
XLA Ops:
  8.5 2.5 %front.1 = (f32[2080,128]{1,0:T(8,128)}, f32[32,2048]{1,0:T(8,128)}, f32[8,2048]{1,0:T(8,128)}) custom-call(s32[4]{0:T(128)} %pad_add_fusion.place, s32[1]{0:T(128)} %bitcast.38.action, f32[128,512]{1,0:T(8,128)} %act_table.1, f32[256,512]{1,0:T(8,128)} %bitcast.49, f32[256,512]{1,0:T(8,128)} %bitcast.50, f32[32,1536]{1,0:T(8,128)} %w_qkv.1, f32[32,512]{1,0:T(8,128)} %w_out.1), custom_call_target="tpu_custom_call" | custom-call | tf_op jit(solution)/shard_map/front/pallas_call | solution.py:279
  11.0 15.4 %collective-permute-start = (f32[8,2048]{1,0:T(8,128)}, f32[8,2048]{1,0:T(8,128)S(1)}, u32[]{:S(2)}, u32[]{:S(2)}) collective-permute-start(f32[8,2048]{1,0:T(8,128)} %get-tuple-element.21), channel_id=1, source_target_pairs={{0,2},{1,3},{2,0},{3,1},{4,6},{5,7},{6,4},{7,5},{8,10},{9,11},{10,... | collective-permute-start | bytes 196616 | tf_op jit(solution)/shard_map/ppermute | solution.py:319
  26.5 7.6 %all-to-all-start = ((f32[32,65,1,128]{3,2,1,0:T(1,128)}), f32[32,65,1,128]{3,2,1,0:T(1,128)S(1)}, u32[]{:S(2)}, u32[]{:S(2)}) async-start(f32[32,65,1,128]{3,2,1,0:T(1,128)} %bitcast.41), calls=%async_computation | async-start | bytes 2129920 | tf_op jit(solution)/shard_map/all_to_all | solution.py:58
  36.2 3.3 %collective-permute-start.1 = (f32[8,2048]{1,0:T(8,128)}, f32[8,2048]{1,0:T(8,128)S(1)}, u32[]{:S(2)}, u32[]{:S(2)}) collective-permute-start(f32[8,2048]{1,0:T(8,128)} %swapped.1), channel_id=1, source_target_pairs={{0,128},{16,144},{32,160},{48,176},{64,192},{80,208},{96,224},{112... | collective-permute-start | bytes 196616 | tf_op jit(solution)/shard_map/ppermute | solution.py:297
  39.5 4.3 %collective-permute-start.2 = (f32[8,2048]{1,0:T(8,128)}, f32[8,2048]{1,0:T(8,128)S(1)}, u32[]{:S(2)}, u32[]{:S(2)}) collective-permute-start(f32[8,2048]{1,0:T(8,128)} %swapped.1), channel_id=1, source_target_pairs={{0,256},{16,272},{32,288},{48,304},{64,320},{80,336},{96,352},{112... | collective-permute-start | bytes 196616 | tf_op jit(solution)/shard_map/ppermute | solution.py:297
  43.9 3.1 %collective-permute-start.3 = (f32[8,2048]{1,0:T(8,128)}, f32[8,2048]{1,0:T(8,128)S(1)}, u32[]{:S(2)}, u32[]{:S(2)}) collective-permute-start(f32[8,2048]{1,0:T(8,128)} %swapped.1), channel_id=1, source_target_pairs={{0,384},{16,400},{32,416},{48,432},{64,448},{80,464},{96,480},{112... | collective-permute-start | bytes 196616 | tf_op jit(solution)/shard_map/ppermute | solution.py:297
  46.9 2.5 %collective-permute-done.3 = f32[8,2048]{1,0:T(8,128)S(1)} collective-permute-done((f32[8,2048]{1,0:T(8,128)}, f32[8,2048]{1,0:T(8,128)S(1)}, u32[]{:S(2)}, u32[]{:S(2)}) %collective-permute-start.3) | collective-permute-done | bytes 65568 | tf_op jit(solution)/shard_map/ppermute | solution.py:297
  50.4 1.9 collective-permute-start.4
  52.3 4.1 %collective-permute-start.5 = (f32[4,8,2048]{2,1,0:T(8,128)S(1)}, f32[4,8,2048]{2,1,0:T(8,128)S(1)}, u32[]{:S(2)}, u32[]{:S(2)}) collective-permute-start(f32[4,8,2048]{2,1,0:T(8,128)S(1)} %pad_maximum_fusion), channel_id=1, source_target_pairs={{0,8},{1,9},{2,10},{3,11},{4,12},{5,13},{6,14},{7,15},{8,0},{9,1},... | collective-permute-start | bytes 786440 | tf_op jit(solution)/shard_map/ppermute | solution.py:299
  56.5 1.9 collective-permute-start.6
  58.5 2.8 %collective-permute-done.5 = f32[4,8,2048]{2,1,0:T(8,128)S(1)} collective-permute-done((f32[4,8,2048]{2,1,0:T(8,128)S(1)}, f32[4,8,2048]{2,1,0:T(8,128)S(1)}, u32[]{:S(2)}, u32[]{:S(2)}) %collective-permute-start.5) | collective-permute-done | bytes 262176 | tf_op jit(solution)/shard_map/ppermute | solution.py:299
  61.2 7.3 %collective-permute-done.6 = f32[4,8,2048]{2,1,0:T(8,128)S(1)} collective-permute-done((f32[4,8,2048]{2,1,0:T(8,128)S(1)}, f32[4,8,2048]{2,1,0:T(8,128)S(1)}, u32[]{:S(2)}, u32[]{:S(2)}) %collective-permute-start.6) | collective-permute-done | bytes 262176 | tf_op jit(solution)/shard_map/ppermute | solution.py:299
  68.6 4.4 %collective-permute-start.7 = (f32[16,8,2048]{2,1,0:T(8,128)S(1)}, f32[16,8,2048]{2,1,0:T(8,128)S(1)}, u32[]{:S(2)}, u32[]{:S(2)}) collective-permute-start(f32[16,8,2048]{2,1,0:T(8,128)S(1)} %constant_dynamic-update-slice_fusion.far_mine), channel_id=1, source_target_pairs={{0,1},{1,0},{2,3},{3,2},{4,5},{5,4},{6,7},{7,6},{8,9},{9,8},{10,11... | collective-permute-start | bytes 3145736 | tf_op jit(solution)/shard_map/ppermute | solution.py:300
  76.3 5.0 %weights.1 = (bf16[512,2048]{1,0:T(8,128)(2,1)}, bf16[512,2048]{1,0:T(8,128)(2,1)}) custom-call(s32[4]{0:T(128)} %pad_add_fusion.place, f32[8,32,2048]{2,1,0:T(8,128)} %bitcast.40, f32[16,8,2048]{2,1,0:T(8,128)} %copy-done.1, f32[16,8,2048]{2,1,0:T(8,128)} %copy-done.2), custom_call_target="tpu_custom_call" | custom-call | tf_op jit(solution)/shard_map/weights/pallas_call | solution.py:279
  81.3 3.8 %all-to-all-done = f32[32,65,1,128]{3,2,1,0:T(1,128)S(1)} async-done(((f32[32,65,1,128]{3,2,1,0:T(1,128)}), f32[32,65,1,128]{3,2,1,0:T(1,128)S(1)}, u32[]{:S(2)}, u32[]{:S(2)}) %all-to-all-start) | async-done | bytes 1064992 | tf_op jit(solution)/shard_map/all_to_all | solution.py:58
  85.1 13.9 %sublayer.1 = (f32[8,4,32,8,128]{4,3,2,1,0:T(8,128)}, f32[1024,128]{1,0:T(8,128)}, f32[2,4,9,8,128]{4,3,2,1,0:T(8,128)S(1)}) custom-call(f32[2080,128]{1,0:T(8,128)S(1)} %bitcast.39, f32[144,128]{1,0:T(8,128)S(1)} %maximum_maximum_fusion.extras_in, bf16[512,2048]{1,0:T(8,128)(2,1)} %get-tuple-element.25.high_in, bf16[512,2048]{1,0:T(8,128)(2,1)} %get-tuple-element.26.low_in), custom_call_target="tpu_custom_call" | custom-call | tf_op jit(solution)/shard_map/sublayer/pallas_call | solution.py:279
  99.1 8.0 %all-to-all-start.1 = ((f32[32,4,8,128]{3,2,1,0:T(8,128)}), f32[32,4,8,128]{3,2,1,0:T(8,128)S(1)}, u32[]{:S(2)}, u32[]{:S(2)}) async-start(f32[32,4,8,128]{3,2,1,0:T(8,128)} %bitcast.19), calls=%async_computation.2 | async-start | bytes 1048576 | tf_op jit(solution)/shard_map/all_to_all | solution.py:58
  107.1 2.6 %collective-permute-start.8 = (f32[4,9,8,128]{3,2,1,0:T(8,128)S(1)}, f32[4,9,8,128]{3,2,1,0:T(8,128)S(1)}, u32[]{:S(2)}, u32[]{:S(2)}) collective-permute-start(f32[4,9,8,128]{3,2,1,0:T(8,128)S(1)} %dynamic-slice_bitcast_fusion), channel_id=1, source_target_pairs={{0,1},{1,0},{2,3},{3,2},{4,5},{5,4},{6,7},{7,6},{8,9},{9,8},{10,11... | collective-permute-start | bytes 442376 | tf_op jit(solution)/shard_map/ppermute | solution.py:370
  110.7 1.9 collective-permute-start.9
  112.6 6.5 %collective-permute-done.9 = f32[4,9,8,128]{3,2,1,0:T(8,128)S(1)} collective-permute-done((f32[4,9,8,128]{3,2,1,0:T(8,128)S(1)}, f32[4,9,8,128]{3,2,1,0:T(8,128)S(1)}, u32[]{:S(2)}, u32[]{:S(2)}) %collective-permute-start.9) | collective-permute-done | bytes 147488 | tf_op jit(solution)/shard_map/ppermute | solution.py:374
  119.2 2.9 %collective-permute-start.10 = (f32[4,9,8,128]{3,2,1,0:T(8,128)S(1)}, f32[4,9,8,128]{3,2,1,0:T(8,128)S(1)}, u32[]{:S(2)}, u32[]{:S(2)}) collective-permute-start(f32[4,9,8,128]{3,2,1,0:T(8,128)S(1)} %add.38), channel_id=1, source_target_pairs={{0,8},{1,9},{2,10},{3,11},{4,12},{5,13},{6,14},{7,15},{8,0},{9,1},... | collective-permute-start | bytes 442376 | tf_op jit(solution)/shard_map/ppermute | solution.py:374
  122.1 6.7 %collective-permute-done.10 = f32[4,9,8,128]{3,2,1,0:T(8,128)S(1)} collective-permute-done((f32[4,9,8,128]{3,2,1,0:T(8,128)S(1)}, f32[4,9,8,128]{3,2,1,0:T(8,128)S(1)}, u32[]{:S(2)}, u32[]{:S(2)}) %collective-permute-start.10) | collective-permute-done | bytes 147488 | tf_op jit(solution)/shard_map/ppermute | solution.py:374
  129.5 6.9 %all-to-all-done.1.tiles = f32[32,4,8,128]{3,2,1,0:T(8,128)S(1)} async-done(((f32[32,4,8,128]{3,2,1,0:T(8,128)}), f32[32,4,8,128]{3,2,1,0:T(8,128)S(1)}, u32[]{:S(2)}, u32[]{:S(2)}) %all-to-all-start.1) | async-done | bytes 524320 | tf_op jit(solution)/shard_map/all_to_all | solution.py:58
  136.5 3.3 %all-to-all-start.2 = ((f32[4,9,8,128]{3,2,1,0:T(8,128)}), f32[4,9,8,128]{3,2,1,0:T(8,128)S(1)}, u32[]{:S(2)}, u32[]{:S(2)}) async-start(f32[4,9,8,128]{3,2,1,0:T(8,128)} %add.39), calls=%async_computation.3 | async-start | bytes 294912 | tf_op jit(solution)/shard_map/all_to_all | solution.py:58
  139.8 1.9 unpack.1
  141.7 3.0 %all-to-all-done.2 = f32[4,9,8,128]{3,2,1,0:T(8,128)S(1)} async-done(((f32[4,9,8,128]{3,2,1,0:T(8,128)}), f32[4,9,8,128]{3,2,1,0:T(8,128)S(1)}, u32[]{:S(2)}, u32[]{:S(2)}) %all-to-all-start.2) | async-done | bytes 147488 | tf_op jit(solution)/shard_map/all_to_all | solution.py:58
  144.7 3.5 %all-to-all-start.3 = ((f32[4,32,8,128]{3,2,1,0:T(8,128)}), f32[4,32,8,128]{3,2,1,0:T(8,128)S(1)}, u32[]{:S(2)}, u32[]{:S(2)}) async-start(f32[4,32,8,128]{3,2,1,0:T(8,128)} %bitcast.46), calls=%async_computation.4 | async-start | bytes 1048576 | tf_op jit(solution)/shard_map/all_to_all | solution.py:58
  148.2 6.9 %all-to-all-done.3 = f32[4,32,8,128]{3,2,1,0:T(8,128)S(1)} async-done(((f32[4,32,8,128]{3,2,1,0:T(8,128)}), f32[4,32,8,128]{3,2,1,0:T(8,128)S(1)}, u32[]{:S(2)}, u32[]{:S(2)}) %all-to-all-start.3) | async-done | bytes 524320 | tf_op jit(solution)/shard_map/all_to_all | solution.py:58
  155.4 25.0 %all_to_all.35 = f32[16,25,1,128]{3,2,1,0:T(1,128)S(1)} all-to-all(f32[16,25,1,128]{3,2,1,0:T(1,128)S(1)} %pad_maximum_fusion.1), channel_id=1, replica_groups={{0,16,32,48,64,80,96,112,2,18,34,50,66,82,98,114},{1,17,33,49,65,81,97,..., dimensions={0} | all-to-all | bytes 409600 | tf_op jit(solution)/shard_map/all_to_all | solution.py:58
  180.5 18.3 %all_to_all.36 = f32[8,25,1,128]{3,2,1,0:T(1,128)S(1)} all-to-all(f32[8,25,1,128]{3,2,1,0:T(1,128)S(1)} %broadcast_in_dim.22), channel_id=1, replica_groups={{0,16,32,48,64,80,96,112},{128,144,160,176,192,208,224,240},{256,272,28..., dimensions={0} | all-to-all | bytes 204800 | tf_op jit(solution)/shard_map/all_to_all | solution.py:58
  198.8 8.6 %all_to_all.37 = f32[4,8,3,8,128]{4,3,2,1,0:T(8,128)S(1)} all-to-all(f32[4,8,3,8,128]{4,3,2,1,0:T(8,128)S(1)} %broadcast_in_dim.23), channel_id=1, replica_groups={{0,128,256,384},{16,144,272,400},{32,160,288,416},{48,176,304,432},{64,..., dimensions={0} | all-to-all | bytes 786432 | tf_op jit(solution)/shard_map/all_to_all | solution.py:58
  207.5 5.2 %collective-permute-start.11 = (f32[128,256]{1,0:T(8,128)S(1)}, f32[128,256]{1,0:T(8,128)S(1)}, u32[]{:S(2)}, u32[]{:S(2)}) collective-permute-start(f32[128,256]{1,0:T(8,128)S(1)} %bitcast.44), channel_id=1, source_target_pairs={{0,1},{1,0},{2,3},{3,2},{4,5},{5,4},{6,7},{7,6},{8,9},{9,8},{10,11... | collective-permute-start | bytes 393224 | tf_op jit(solution)/shard_map/ppermute | solution.py:398
  (66 shorter events, 12.0 us)
Async XLA Ops:
  7.2 43.2 %all-gather.3.cloned.1.call-start = ((), (), s32[]{:S(2)}) async-start(), calls=%async_computation.9 | async-start | bytes 2359296 | tf_op jit(solution)/shard_map/all_gather | solution.py:318
  11.0 23.1 %collective-permute-start = (f32[8,2048]{1,0:T(8,128)}, f32[8,2048]{1,0:T(8,128)S(1)}, u32[]{:S(2)}, u32[]{:S(2)}) collective-permute-start(f32[8,2048]{1,0:T(8,128)} %get-tuple-element.21), channel_id=1, source_target_pairs={{0,2},{1,3},{2,0},{3,1},{4,6},{5,7},{6,4},{7,5},{8,10},{9,11},{10,... | collective-permute-start | bytes 196616 | tf_op jit(solution)/shard_map/ppermute | solution.py:319
  26.5 58.6 %all-to-all-start = ((f32[32,65,1,128]{3,2,1,0:T(1,128)}), f32[32,65,1,128]{3,2,1,0:T(1,128)S(1)}, u32[]{:S(2)}, u32[]{:S(2)}) async-start(f32[32,65,1,128]{3,2,1,0:T(1,128)} %bitcast.41), calls=%async_computation | async-start | bytes 2129920 | tf_op jit(solution)/shard_map/all_to_all | solution.py:58
  34.1 110.7 %reduce-scatter.2.cloned.1.call-start = ((), (), s32[]{:S(2)}) async-start(), calls=%async_computation.8 | async-start | bytes 4718592 | tf_op jit(solution)/shard_map/reduce_scatter | solution.py:367
  34.1 0.6 copy-start.5
  36.2 36.7 %copy-start.6 = (s32[1,32]{1,0:T(1,128)S(1)}, s32[1,32]{1,0:T(1,128)}, u32[]{:S(2)}) copy-start(s32[1,32]{1,0:T(1,128)} %param.11) | copy-start | bytes 388
  36.2 36.9 %copy-start.4 = (f32[8]{0:T(128)S(1)}, f32[8]{0:T(128)}, u32[]{:S(2)}) copy-start(f32[8]{0:T(128)} %param.16) | copy-start | bytes 100
  36.2 37.1 %copy-start.3 = (f32[512]{0:T(512)S(1)}, f32[512]{0:T(512)}, u32[]{:S(2)}) copy-start(f32[512]{0:T(512)} %param.13) | copy-start | bytes 6148
  36.2 10.7 %collective-permute-start.1 = (f32[8,2048]{1,0:T(8,128)}, f32[8,2048]{1,0:T(8,128)S(1)}, u32[]{:S(2)}, u32[]{:S(2)}) collective-permute-start(f32[8,2048]{1,0:T(8,128)} %swapped.1), channel_id=1, source_target_pairs={{0,128},{16,144},{32,160},{48,176},{64,192},{80,208},{96,224},{112... | collective-permute-start | bytes 196616 | tf_op jit(solution)/shard_map/ppermute | solution.py:297
  39.5 7.4 %collective-permute-start.2 = (f32[8,2048]{1,0:T(8,128)}, f32[8,2048]{1,0:T(8,128)S(1)}, u32[]{:S(2)}, u32[]{:S(2)}) collective-permute-start(f32[8,2048]{1,0:T(8,128)} %swapped.1), channel_id=1, source_target_pairs={{0,256},{16,272},{32,288},{48,304},{64,320},{80,336},{96,352},{112... | collective-permute-start | bytes 196616 | tf_op jit(solution)/shard_map/ppermute | solution.py:297
  43.9 5.6 %collective-permute-start.3 = (f32[8,2048]{1,0:T(8,128)}, f32[8,2048]{1,0:T(8,128)S(1)}, u32[]{:S(2)}, u32[]{:S(2)}) collective-permute-start(f32[8,2048]{1,0:T(8,128)} %swapped.1), channel_id=1, source_target_pairs={{0,384},{16,400},{32,416},{48,432},{64,448},{80,464},{96,480},{112... | collective-permute-start | bytes 196616 | tf_op jit(solution)/shard_map/ppermute | solution.py:297
  50.4 8.0 %collective-permute-start.4 = (f32[4,8,2048]{2,1,0:T(8,128)S(1)}, f32[4,8,2048]{2,1,0:T(8,128)S(1)}, u32[]{:S(2)}, u32[]{:S(2)}) collective-permute-start(f32[4,8,2048]{2,1,0:T(8,128)S(1)} %pad_maximum_fusion), channel_id=1, source_target_pairs={{0,4},{1,5},{2,6},{3,7},{4,8},{5,9},{6,10},{7,11},{8,12},{9,13},{1... | collective-permute-start | bytes 786440 | tf_op jit(solution)/shard_map/ppermute | solution.py:299
  52.3 8.9 %collective-permute-start.5 = (f32[4,8,2048]{2,1,0:T(8,128)S(1)}, f32[4,8,2048]{2,1,0:T(8,128)S(1)}, u32[]{:S(2)}, u32[]{:S(2)}) collective-permute-start(f32[4,8,2048]{2,1,0:T(8,128)S(1)} %pad_maximum_fusion), channel_id=1, source_target_pairs={{0,8},{1,9},{2,10},{3,11},{4,12},{5,13},{6,14},{7,15},{8,0},{9,1},... | collective-permute-start | bytes 786440 | tf_op jit(solution)/shard_map/ppermute | solution.py:299
  56.5 12.1 %collective-permute-start.6 = (f32[4,8,2048]{2,1,0:T(8,128)S(1)}, f32[4,8,2048]{2,1,0:T(8,128)S(1)}, u32[]{:S(2)}, u32[]{:S(2)}) collective-permute-start(f32[4,8,2048]{2,1,0:T(8,128)S(1)} %pad_maximum_fusion), channel_id=1, source_target_pairs={{0,12},{1,13},{2,14},{3,15},{4,0},{5,1},{6,2},{7,3},{8,4},{9,5},{1... | collective-permute-start | bytes 786440 | tf_op jit(solution)/shard_map/ppermute | solution.py:299
  68.6 6.7 %copy-start.1 = (f32[16,8,2048]{2,1,0:T(8,128)}, f32[16,8,2048]{2,1,0:T(8,128)S(1)}, u32[]{:S(2)}) copy-start(f32[16,8,2048]{2,1,0:T(8,128)S(1)} %constant_dynamic-update-slice_fusion.far_mine) | copy-start | bytes 3145732
  68.6 6.7 %collective-permute-start.7 = (f32[16,8,2048]{2,1,0:T(8,128)S(1)}, f32[16,8,2048]{2,1,0:T(8,128)S(1)}, u32[]{:S(2)}, u32[]{:S(2)}) collective-permute-start(f32[16,8,2048]{2,1,0:T(8,128)S(1)} %constant_dynamic-update-slice_fusion.far_mine), channel_id=1, source_target_pairs={{0,1},{1,0},{2,3},{3,2},{4,5},{5,4},{6,7},{7,6},{8,9},{9,8},{10,11... | collective-permute-start | bytes 3145736 | tf_op jit(solution)/shard_map/ppermute | solution.py:300
  75.2 1.1 copy-start.2
  99.1 37.4 %all-to-all-start.1 = ((f32[32,4,8,128]{3,2,1,0:T(8,128)}), f32[32,4,8,128]{3,2,1,0:T(8,128)S(1)}, u32[]{:S(2)}, u32[]{:S(2)}) async-start(f32[32,4,8,128]{3,2,1,0:T(8,128)} %bitcast.19), calls=%async_computation.2 | async-start | bytes 1048576 | tf_op jit(solution)/shard_map/all_to_all | solution.py:58
  107.1 3.6 %collective-permute-start.8 = (f32[4,9,8,128]{3,2,1,0:T(8,128)S(1)}, f32[4,9,8,128]{3,2,1,0:T(8,128)S(1)}, u32[]{:S(2)}, u32[]{:S(2)}) collective-permute-start(f32[4,9,8,128]{3,2,1,0:T(8,128)S(1)} %dynamic-slice_bitcast_fusion), channel_id=1, source_target_pairs={{0,1},{1,0},{2,3},{3,2},{4,5},{5,4},{6,7},{7,6},{8,9},{9,8},{10,11... | collective-permute-start | bytes 442376 | tf_op jit(solution)/shard_map/ppermute | solution.py:370
  110.7 8.4 %collective-permute-start.9 = (f32[4,9,8,128]{3,2,1,0:T(8,128)S(1)}, f32[4,9,8,128]{3,2,1,0:T(8,128)S(1)}, u32[]{:S(2)}, u32[]{:S(2)}) collective-permute-start(f32[4,9,8,128]{3,2,1,0:T(8,128)S(1)} %bitcast_add_fusion), channel_id=1, source_target_pairs={{0,4},{1,5},{2,6},{3,7},{4,0},{5,1},{6,2},{7,3},{8,12},{9,13},{10,... | collective-permute-start | bytes 442376 | tf_op jit(solution)/shard_map/ppermute | solution.py:374
  119.2 9.7 %collective-permute-start.10 = (f32[4,9,8,128]{3,2,1,0:T(8,128)S(1)}, f32[4,9,8,128]{3,2,1,0:T(8,128)S(1)}, u32[]{:S(2)}, u32[]{:S(2)}) collective-permute-start(f32[4,9,8,128]{3,2,1,0:T(8,128)S(1)} %add.38), channel_id=1, source_target_pairs={{0,8},{1,9},{2,10},{3,11},{4,12},{5,13},{6,14},{7,15},{8,0},{9,1},... | collective-permute-start | bytes 442376 | tf_op jit(solution)/shard_map/ppermute | solution.py:374
  136.5 3.3 %copy-start = (f32[32,4,8,128]{3,2,1,0:T(8,128)}, f32[32,4,8,128]{3,2,1,0:T(8,128)S(1)}, u32[]{:S(2)}) copy-start(f32[32,4,8,128]{3,2,1,0:T(8,128)S(1)} %all-to-all-done.1.tiles) | copy-start | bytes 1572868
  136.5 8.2 %all-to-all-start.2 = ((f32[4,9,8,128]{3,2,1,0:T(8,128)}), f32[4,9,8,128]{3,2,1,0:T(8,128)S(1)}, u32[]{:S(2)}, u32[]{:S(2)}) async-start(f32[4,9,8,128]{3,2,1,0:T(8,128)} %add.39), calls=%async_computation.3 | async-start | bytes 294912 | tf_op jit(solution)/shard_map/all_to_all | solution.py:58
  144.7 10.4 %all-to-all-start.3 = ((f32[4,32,8,128]{3,2,1,0:T(8,128)}), f32[4,32,8,128]{3,2,1,0:T(8,128)S(1)}, u32[]{:S(2)}, u32[]{:S(2)}) async-start(f32[4,32,8,128]{3,2,1,0:T(8,128)} %bitcast.46), calls=%async_computation.4 | async-start | bytes 1048576 | tf_op jit(solution)/shard_map/all_to_all | solution.py:58
  207.5 7.2 %collective-permute-start.11 = (f32[128,256]{1,0:T(8,128)S(1)}, f32[128,256]{1,0:T(8,128)S(1)}, u32[]{:S(2)}, u32[]{:S(2)}) collective-permute-start(f32[128,256]{1,0:T(8,128)S(1)} %bitcast.44), channel_id=1, source_target_pairs={{0,1},{1,0},{2,3},{3,2},{4,5},{5,4},{6,7},{7,6},{8,9},{9,8},{10,11... | collective-permute-start | bytes 393224 | tf_op jit(solution)/shard_map/ppermute | solution.py:398
Sparse Core Ops, SparseCore 0:
  11.1 36.4 all-gather.2
  99.2 43.3 reduce-scatter.1

commit v7 on v6

--- a/solution.py
+++ b/solution.py
@@ -131,14 +131,17 @@
     grads_out, tokens_out, tables,
     grads, tokens_new, sems, extras, high, low, emb_ref, og, qkv_h, qkv_l, gm_h, gm_l, mixed, gr_h, gr_l,
 ):
-    arrivals = [
-        pltpu.make_async_copy(source, target, sems.at[17 + i])
-        for i, (source, target) in enumerate(
-            ((extras_in, extras), (high_in, high), (low_in, low))
-        )
-    ]
-    for copy in arrivals:
-        copy.start()
+    extras_copy = pltpu.make_async_copy(extras_in, extras, sems.at[17])
+    extras_copy.start()
+    arrivals = []
+    for chunk in range(4):
+        cols = pl.ds(chunk * 512, 512)
+        arrivals.append([
+            pltpu.make_async_copy(source.at[:, cols], target.at[:, cols], sems.at[18 + chunk * 2 + i])
+            for i, (source, target) in enumerate(((high_in, high), (low_in, low)))
+        ])
+        for copy in arrivals[-1]:
+            copy.start()
     take_rows(tiles, emb_ref, 0)
     take_rows(tiles, og, 4)
 
@@ -148,20 +151,23 @@
 
     emb = emb_ref[...]
     scale = lax.rsqrt(jnp.mean(emb * emb, axis=1, keepdims=True) + 1e-06)
-    arrivals[0].wait()
+    extras_copy.wait()
     spacing = extras[:HALF, :]
     gain = jnp.concatenate([extras[HALF + HEADS + i:HALF + HEADS + i + 1, :] for i in range(4)], axis=1)
     normed = emb * gain * scale
     parts = split(normed)
-    for copy in arrivals[1:]:
-        copy.wait()
     for block in range(QKV // 256):
+        if block % 2 == 0:
+            for copy in arrivals[block // 2]:
+                copy.wait()
         cols = slice(block * 256, block * 256 + 256)
         value = dot3(parts, (high[:, cols], low[:, cols]))
         if block < D // 256:
             value = value * 0.125
         qkv_h[:, cols], qkv_l[:, cols] = split(value)
     og_parts = split(og[...])
+    for copy in arrivals[3]:
+        copy.wait()
     gm_h[...], gm_l[...] = split(dot3(og_parts, (high[:, QKV:], low[:, QKV:]), NT))
 
     lane = lax.broadcasted_iota(jnp.int32, (ROWS, PAIR), 1) < HEAD
@@ -350,7 +356,7 @@
         ],
         [
             pltpu.VMEM((NY * NC, NX, TILES, 8, 128), f32), pltpu.VMEM((ROWS * 4, 128), f32),
-            pltpu.SemaphoreType.DMA((20,)), pltpu.VMEM((HALF + 16, 128), f32),
+            pltpu.SemaphoreType.DMA((26,)), pltpu.VMEM((HALF + 16, 128), f32),
             pltpu.VMEM((D, QKV + D), bf16), pltpu.VMEM((D, QKV + D), bf16),
             pltpu.VMEM((ROWS, D), f32), pltpu.VMEM((ROWS, D), f32),
             pltpu.VMEM((ROWS, QKV), bf16), pltpu.VMEM((ROWS, QKV), bf16),

time: 223 us -> 223 us (level)
  no operation moved by 1% of the time
where the time goes in v7:
time: 223 us; the launch traced here: 222 us
  starting transfers between devices  73.7 us (33%)
  blocking collectives  51.8 us (23%)
  waiting for transfers between devices  49.3 us (22%)
  Pallas kernels  24.3 us (11%)
  between operations  15.2 us (7%)
  local copies, waits for them, and re-layouts  4.08 us (2%)
  other arithmetic  3.49 us (2%)
    all_to_all x3, blocking collectives, exchange(): lax.all_to_all(value, axis, 0, 0, axis_index_groups=groups, tiled=True)  51.8 us
    pallas_call x5, Pallas kernels, call(): pl.pallas_call(kernel, out_shape=outs, in_specs=[smem] * len(scalars) + [...  24.3 us
    all_to_all x4, starting transfers between devices, exchange(): lax.all_to_all(value, axis, 0, 0, axis_index_groups=groups, tiled=True)  22.5 us
    all_to_all x4, waiting for transfers between devices, exchange(): lax.all_to_all(value, axis, 0, 0, axis_index_groups=groups, tiled=True)  20.6 us
    ppermute x1, starting transfers between devices, shards(): quarter = lax.ppermute(quarter, 'dp', SWAP_ZH)  15.4 us
    ppermute x2, waiting for transfers between devices, shards(): part = part + lax.ppermute(part, 'dp', swap_y(bit))  13.2 us
    ppermute x3, starting transfers between devices, far_weights(): lax.ppermute(quarter, 'tm', turn_x(i))  10.7 us
    ppermute x3, waiting for transfers between devices, far_weights(): lax.ppermute(row, 'dp', turn_y(i))  10.1 us
  transfers between devices with their start and end apart: 18, of which 11 were waited for; matrix products, arithmetic and copies ran while one was open for 2% of the time, Pallas kernels for 4%

profile of v7, /device:TPU:25, one launch (start us, length us, event | category | flops | bytes accessed | tf_op | source)
XLA Modules:
  0.0 221.9 jit_solution(10409218137350536783)
XLA Ops:
  8.5 2.5 %front.1 = (f32[2080,128]{1,0:T(8,128)}, f32[32,2048]{1,0:T(8,128)}, f32[8,2048]{1,0:T(8,128)}) custom-call(s32[4]{0:T(128)} %pad_add_fusion.place, s32[1]{0:T(128)} %bitcast.38.action, f32[128,512]{1,0:T(8,128)} %act_table.1, f32[256,512]{1,0:T(8,128)} %bitcast.49, f32[256,512]{1,0:T(8,128)} %bitcast.50, f32[32,1536]{1,0:T(8,128)} %w_qkv.1, f32[32,512]{1,0:T(8,128)} %w_out.1), custom_call_target="tpu_custom_call" | custom-call | tf_op jit(solution)/shard_map/front/pallas_call | solution.py:285
  11.0 15.4 %collective-permute-start = (f32[8,2048]{1,0:T(8,128)}, f32[8,2048]{1,0:T(8,128)S(1)}, u32[]{:S(2)}, u32[]{:S(2)}) collective-permute-start(f32[8,2048]{1,0:T(8,128)} %get-tuple-element.21), channel_id=1, source_target_pairs={{0,2},{1,3},{2,0},{3,1},{4,6},{5,7},{6,4},{7,5},{8,10},{9,11},{10,... | collective-permute-start | bytes 196616 | tf_op jit(solution)/shard_map/ppermute | solution.py:325
  26.5 7.6 %all-to-all-start = ((f32[32,65,1,128]{3,2,1,0:T(1,128)}), f32[32,65,1,128]{3,2,1,0:T(1,128)S(1)}, u32[]{:S(2)}, u32[]{:S(2)}) async-start(f32[32,65,1,128]{3,2,1,0:T(1,128)} %bitcast.41), calls=%async_computation | async-start | bytes 2129920 | tf_op jit(solution)/shard_map/all_to_all | solution.py:58
  36.2 3.3 %collective-permute-start.1 = (f32[8,2048]{1,0:T(8,128)}, f32[8,2048]{1,0:T(8,128)S(1)}, u32[]{:S(2)}, u32[]{:S(2)}) collective-permute-start(f32[8,2048]{1,0:T(8,128)} %swapped.1), channel_id=1, source_target_pairs={{0,128},{16,144},{32,160},{48,176},{64,192},{80,208},{96,224},{112... | collective-permute-start | bytes 196616 | tf_op jit(solution)/shard_map/ppermute | solution.py:303
  39.5 4.3 %collective-permute-start.2 = (f32[8,2048]{1,0:T(8,128)}, f32[8,2048]{1,0:T(8,128)S(1)}, u32[]{:S(2)}, u32[]{:S(2)}) collective-permute-start(f32[8,2048]{1,0:T(8,128)} %swapped.1), channel_id=1, source_target_pairs={{0,256},{16,272},{32,288},{48,304},{64,320},{80,336},{96,352},{112... | collective-permute-start | bytes 196616 | tf_op jit(solution)/shard_map/ppermute | solution.py:303
  43.9 3.1 %collective-permute-start.3 = (f32[8,2048]{1,0:T(8,128)}, f32[8,2048]{1,0:T(8,128)S(1)}, u32[]{:S(2)}, u32[]{:S(2)}) collective-permute-start(f32[8,2048]{1,0:T(8,128)} %swapped.1), channel_id=1, source_target_pairs={{0,384},{16,400},{32,416},{48,432},{64,448},{80,464},{96,480},{112... | collective-permute-start | bytes 196616 | tf_op jit(solution)/shard_map/ppermute | solution.py:303
  46.9 2.5 %collective-permute-done.3 = f32[8,2048]{1,0:T(8,128)S(1)} collective-permute-done((f32[8,2048]{1,0:T(8,128)}, f32[8,2048]{1,0:T(8,128)S(1)}, u32[]{:S(2)}, u32[]{:S(2)}) %collective-permute-start.3) | collective-permute-done | bytes 65568 | tf_op jit(solution)/shard_map/ppermute | solution.py:303
  50.4 1.9 collective-permute-start.4
  52.3 4.1 %collective-permute-start.5 = (f32[4,8,2048]{2,1,0:T(8,128)S(1)}, f32[4,8,2048]{2,1,0:T(8,128)S(1)}, u32[]{:S(2)}, u32[]{:S(2)}) collective-permute-start(f32[4,8,2048]{2,1,0:T(8,128)S(1)} %pad_maximum_fusion), channel_id=1, source_target_pairs={{0,8},{1,9},{2,10},{3,11},{4,12},{5,13},{6,14},{7,15},{8,0},{9,1},... | collective-permute-start | bytes 786440 | tf_op jit(solution)/shard_map/ppermute | solution.py:305
  56.5 1.9 collective-permute-start.6
  58.5 2.8 %collective-permute-done.5 = f32[4,8,2048]{2,1,0:T(8,128)S(1)} collective-permute-done((f32[4,8,2048]{2,1,0:T(8,128)S(1)}, f32[4,8,2048]{2,1,0:T(8,128)S(1)}, u32[]{:S(2)}, u32[]{:S(2)}) %collective-permute-start.5) | collective-permute-done | bytes 262176 | tf_op jit(solution)/shard_map/ppermute | solution.py:305
  61.2 7.3 %collective-permute-done.6 = f32[4,8,2048]{2,1,0:T(8,128)S(1)} collective-permute-done((f32[4,8,2048]{2,1,0:T(8,128)S(1)}, f32[4,8,2048]{2,1,0:T(8,128)S(1)}, u32[]{:S(2)}, u32[]{:S(2)}) %collective-permute-start.6) | collective-permute-done | bytes 262176 | tf_op jit(solution)/shard_map/ppermute | solution.py:305
  68.6 4.4 %collective-permute-start.7 = (f32[16,8,2048]{2,1,0:T(8,128)S(1)}, f32[16,8,2048]{2,1,0:T(8,128)S(1)}, u32[]{:S(2)}, u32[]{:S(2)}) collective-permute-start(f32[16,8,2048]{2,1,0:T(8,128)S(1)} %constant_dynamic-update-slice_fusion.far_mine), channel_id=1, source_target_pairs={{0,1},{1,0},{2,3},{3,2},{4,5},{5,4},{6,7},{7,6},{8,9},{9,8},{10,11... | collective-permute-start | bytes 3145736 | tf_op jit(solution)/shard_map/ppermute | solution.py:306
  76.3 5.0 %weights.1 = (bf16[512,2048]{1,0:T(8,128)(2,1)}, bf16[512,2048]{1,0:T(8,128)(2,1)}) custom-call(s32[4]{0:T(128)} %pad_add_fusion.place, f32[8,32,2048]{2,1,0:T(8,128)} %bitcast.40, f32[16,8,2048]{2,1,0:T(8,128)} %copy-done.1, f32[16,8,2048]{2,1,0:T(8,128)} %copy-done.2), custom_call_target="tpu_custom_call" | custom-call | tf_op jit(solution)/shard_map/weights/pallas_call | solution.py:285
  81.3 3.8 %all-to-all-done = f32[32,65,1,128]{3,2,1,0:T(1,128)S(1)} async-done(((f32[32,65,1,128]{3,2,1,0:T(1,128)}), f32[32,65,1,128]{3,2,1,0:T(1,128)S(1)}, u32[]{:S(2)}, u32[]{:S(2)}) %all-to-all-start) | async-done | bytes 1064992 | tf_op jit(solution)/shard_map/all_to_all | solution.py:58
  85.1 13.5 %sublayer.1 = (f32[8,4,32,8,128]{4,3,2,1,0:T(8,128)}, f32[1024,128]{1,0:T(8,128)}, f32[2,4,9,8,128]{4,3,2,1,0:T(8,128)S(1)}) custom-call(f32[2080,128]{1,0:T(8,128)S(1)} %bitcast.39, f32[144,128]{1,0:T(8,128)S(1)} %maximum_maximum_fusion.extras_in, bf16[512,2048]{1,0:T(8,128)(2,1)} %get-tuple-element.25.high_in, bf16[512,2048]{1,0:T(8,128)(2,1)} %get-tuple-element.26.low_in), custom_call_target="tpu_custom_call" | custom-call | tf_op jit(solution)/shard_map/sublayer/pallas_call | solution.py:285
  98.7 8.0 %all-to-all-start.1 = ((f32[32,4,8,128]{3,2,1,0:T(8,128)}), f32[32,4,8,128]{3,2,1,0:T(8,128)S(1)}, u32[]{:S(2)}, u32[]{:S(2)}) async-start(f32[32,4,8,128]{3,2,1,0:T(8,128)} %bitcast.19), calls=%async_computation.2 | async-start | bytes 1048576 | tf_op jit(solution)/shard_map/all_to_all | solution.py:58
  106.8 2.6 %collective-permute-start.8 = (f32[4,9,8,128]{3,2,1,0:T(8,128)S(1)}, f32[4,9,8,128]{3,2,1,0:T(8,128)S(1)}, u32[]{:S(2)}, u32[]{:S(2)}) collective-permute-start(f32[4,9,8,128]{3,2,1,0:T(8,128)S(1)} %dynamic-slice_bitcast_fusion), channel_id=1, source_target_pairs={{0,1},{1,0},{2,3},{3,2},{4,5},{5,4},{6,7},{7,6},{8,9},{9,8},{10,11... | collective-permute-start | bytes 442376 | tf_op jit(solution)/shard_map/ppermute | solution.py:376
  110.3 1.9 collective-permute-start.9
  112.3 6.5 %collective-permute-done.9 = f32[4,9,8,128]{3,2,1,0:T(8,128)S(1)} collective-permute-done((f32[4,9,8,128]{3,2,1,0:T(8,128)S(1)}, f32[4,9,8,128]{3,2,1,0:T(8,128)S(1)}, u32[]{:S(2)}, u32[]{:S(2)}) %collective-permute-start.9) | collective-permute-done | bytes 147488 | tf_op jit(solution)/shard_map/ppermute | solution.py:380
  118.8 3.0 %collective-permute-start.10 = (f32[4,9,8,128]{3,2,1,0:T(8,128)S(1)}, f32[4,9,8,128]{3,2,1,0:T(8,128)S(1)}, u32[]{:S(2)}, u32[]{:S(2)}) collective-permute-start(f32[4,9,8,128]{3,2,1,0:T(8,128)S(1)} %add.38), channel_id=1, source_target_pairs={{0,8},{1,9},{2,10},{3,11},{4,12},{5,13},{6,14},{7,15},{8,0},{9,1},... | collective-permute-start | bytes 442376 | tf_op jit(solution)/shard_map/ppermute | solution.py:380
  121.8 6.7 %collective-permute-done.10 = f32[4,9,8,128]{3,2,1,0:T(8,128)S(1)} collective-permute-done((f32[4,9,8,128]{3,2,1,0:T(8,128)S(1)}, f32[4,9,8,128]{3,2,1,0:T(8,128)S(1)}, u32[]{:S(2)}, u32[]{:S(2)}) %collective-permute-start.10) | collective-permute-done | bytes 147488 | tf_op jit(solution)/shard_map/ppermute | solution.py:380
  129.2 6.9 %all-to-all-done.1.tiles = f32[32,4,8,128]{3,2,1,0:T(8,128)S(1)} async-done(((f32[32,4,8,128]{3,2,1,0:T(8,128)}), f32[32,4,8,128]{3,2,1,0:T(8,128)S(1)}, u32[]{:S(2)}, u32[]{:S(2)}) %all-to-all-start.1) | async-done | bytes 524320 | tf_op jit(solution)/shard_map/all_to_all | solution.py:58
  136.1 3.3 %all-to-all-start.2 = ((f32[4,9,8,128]{3,2,1,0:T(8,128)}), f32[4,9,8,128]{3,2,1,0:T(8,128)S(1)}, u32[]{:S(2)}, u32[]{:S(2)}) async-start(f32[4,9,8,128]{3,2,1,0:T(8,128)} %add.39), calls=%async_computation.3 | async-start | bytes 294912 | tf_op jit(solution)/shard_map/all_to_all | solution.py:58
  139.4 1.9 unpack.1
  141.3 3.0 %all-to-all-done.2 = f32[4,9,8,128]{3,2,1,0:T(8,128)S(1)} async-done(((f32[4,9,8,128]{3,2,1,0:T(8,128)}), f32[4,9,8,128]{3,2,1,0:T(8,128)S(1)}, u32[]{:S(2)}, u32[]{:S(2)}) %all-to-all-start.2) | async-done | bytes 147488 | tf_op jit(solution)/shard_map/all_to_all | solution.py:58
  144.4 3.5 %all-to-all-start.3 = ((f32[4,32,8,128]{3,2,1,0:T(8,128)}), f32[4,32,8,128]{3,2,1,0:T(8,128)S(1)}, u32[]{:S(2)}, u32[]{:S(2)}) async-start(f32[4,32,8,128]{3,2,1,0:T(8,128)} %bitcast.46), calls=%async_computation.4 | async-start | bytes 1048576 | tf_op jit(solution)/shard_map/all_to_all | solution.py:58
  147.9 6.9 %all-to-all-done.3 = f32[4,32,8,128]{3,2,1,0:T(8,128)S(1)} async-done(((f32[4,32,8,128]{3,2,1,0:T(8,128)}), f32[4,32,8,128]{3,2,1,0:T(8,128)S(1)}, u32[]{:S(2)}, u32[]{:S(2)}) %all-to-all-start.3) | async-done | bytes 524320 | tf_op jit(solution)/shard_map/all_to_all | solution.py:58
  155.0 24.9 %all_to_all.35 = f32[16,25,1,128]{3,2,1,0:T(1,128)S(1)} all-to-all(f32[16,25,1,128]{3,2,1,0:T(1,128)S(1)} %pad_maximum_fusion.1), channel_id=1, replica_groups={{0,16,32,48,64,80,96,112,2,18,34,50,66,82,98,114},{1,17,33,49,65,81,97,..., dimensions={0} | all-to-all | bytes 409600 | tf_op jit(solution)/shard_map/all_to_all | solution.py:58
  180.1 18.3 %all_to_all.36 = f32[8,25,1,128]{3,2,1,0:T(1,128)S(1)} all-to-all(f32[8,25,1,128]{3,2,1,0:T(1,128)S(1)} %broadcast_in_dim.22), channel_id=1, replica_groups={{0,16,32,48,64,80,96,112},{128,144,160,176,192,208,224,240},{256,272,28..., dimensions={0} | all-to-all | bytes 204800 | tf_op jit(solution)/shard_map/all_to_all | solution.py:58
  198.4 8.6 %all_to_all.37 = f32[4,8,3,8,128]{4,3,2,1,0:T(8,128)S(1)} all-to-all(f32[4,8,3,8,128]{4,3,2,1,0:T(8,128)S(1)} %broadcast_in_dim.23), channel_id=1, replica_groups={{0,128,256,384},{16,144,272,400},{32,160,288,416},{48,176,304,432},{64,..., dimensions={0} | all-to-all | bytes 786432 | tf_op jit(solution)/shard_map/all_to_all | solution.py:58
  207.1 5.2 %collective-permute-start.11 = (f32[128,256]{1,0:T(8,128)S(1)}, f32[128,256]{1,0:T(8,128)S(1)}, u32[]{:S(2)}, u32[]{:S(2)}) collective-permute-start(f32[128,256]{1,0:T(8,128)S(1)} %bitcast.44), channel_id=1, source_target_pairs={{0,1},{1,0},{2,3},{3,2},{4,5},{5,4},{6,7},{7,6},{8,9},{9,8},{10,11... | collective-permute-start | bytes 393224 | tf_op jit(solution)/shard_map/ppermute | solution.py:404
  (66 shorter events, 12.0 us)
Async XLA Ops:
  7.2 43.2 %all-gather.3.cloned.1.call-start = ((), (), s32[]{:S(2)}) async-start(), calls=%async_computation.9 | async-start | bytes 2359296 | tf_op jit(solution)/shard_map/all_gather | solution.py:324
  11.0 23.1 %collective-permute-start = (f32[8,2048]{1,0:T(8,128)}, f32[8,2048]{1,0:T(8,128)S(1)}, u32[]{:S(2)}, u32[]{:S(2)}) collective-permute-start(f32[8,2048]{1,0:T(8,128)} %get-tuple-element.21), channel_id=1, source_target_pairs={{0,2},{1,3},{2,0},{3,1},{4,6},{5,7},{6,4},{7,5},{8,10},{9,11},{10,... | collective-permute-start | bytes 196616 | tf_op jit(solution)/shard_map/ppermute | solution.py:325
  26.5 58.6 %all-to-all-start = ((f32[32,65,1,128]{3,2,1,0:T(1,128)}), f32[32,65,1,128]{3,2,1,0:T(1,128)S(1)}, u32[]{:S(2)}, u32[]{:S(2)}) async-start(f32[32,65,1,128]{3,2,1,0:T(1,128)} %bitcast.41), calls=%async_computation | async-start | bytes 2129920 | tf_op jit(solution)/shard_map/all_to_all | solution.py:58
  34.1 110.3 %reduce-scatter.2.cloned.1.call-start = ((), (), s32[]{:S(2)}) async-start(), calls=%async_computation.8 | async-start | bytes 4718592 | tf_op jit(solution)/shard_map/reduce_scatter | solution.py:373
  34.1 0.6 copy-start.5
  36.2 36.7 %copy-start.6 = (s32[1,32]{1,0:T(1,128)S(1)}, s32[1,32]{1,0:T(1,128)}, u32[]{:S(2)}) copy-start(s32[1,32]{1,0:T(1,128)} %param.11) | copy-start | bytes 388
  36.2 36.9 %copy-start.4 = (f32[8]{0:T(128)S(1)}, f32[8]{0:T(128)}, u32[]{:S(2)}) copy-start(f32[8]{0:T(128)} %param.16) | copy-start | bytes 100
  36.2 37.1 %copy-start.3 = (f32[512]{0:T(512)S(1)}, f32[512]{0:T(512)}, u32[]{:S(2)}) copy-start(f32[512]{0:T(512)} %param.13) | copy-start | bytes 6148
  36.2 10.7 %collective-permute-start.1 = (f32[8,2048]{1,0:T(8,128)}, f32[8,2048]{1,0:T(8,128)S(1)}, u32[]{:S(2)}, u32[]{:S(2)}) collective-permute-start(f32[8,2048]{1,0:T(8,128)} %swapped.1), channel_id=1, source_target_pairs={{0,128},{16,144},{32,160},{48,176},{64,192},{80,208},{96,224},{112... | collective-permute-start | bytes 196616 | tf_op jit(solution)/shard_map/ppermute | solution.py:303
  39.5 7.4 %collective-permute-start.2 = (f32[8,2048]{1,0:T(8,128)}, f32[8,2048]{1,0:T(8,128)S(1)}, u32[]{:S(2)}, u32[]{:S(2)}) collective-permute-start(f32[8,2048]{1,0:T(8,128)} %swapped.1), channel_id=1, source_target_pairs={{0,256},{16,272},{32,288},{48,304},{64,320},{80,336},{96,352},{112... | collective-permute-start | bytes 196616 | tf_op jit(solution)/shard_map/ppermute | solution.py:303
  43.9 5.6 %collective-permute-start.3 = (f32[8,2048]{1,0:T(8,128)}, f32[8,2048]{1,0:T(8,128)S(1)}, u32[]{:S(2)}, u32[]{:S(2)}) collective-permute-start(f32[8,2048]{1,0:T(8,128)} %swapped.1), channel_id=1, source_target_pairs={{0,384},{16,400},{32,416},{48,432},{64,448},{80,464},{96,480},{112... | collective-permute-start | bytes 196616 | tf_op jit(solution)/shard_map/ppermute | solution.py:303
  50.4 8.0 %collective-permute-start.4 = (f32[4,8,2048]{2,1,0:T(8,128)S(1)}, f32[4,8,2048]{2,1,0:T(8,128)S(1)}, u32[]{:S(2)}, u32[]{:S(2)}) collective-permute-start(f32[4,8,2048]{2,1,0:T(8,128)S(1)} %pad_maximum_fusion), channel_id=1, source_target_pairs={{0,4},{1,5},{2,6},{3,7},{4,8},{5,9},{6,10},{7,11},{8,12},{9,13},{1... | collective-permute-start | bytes 786440 | tf_op jit(solution)/shard_map/ppermute | solution.py:305
  52.3 8.9 %collective-permute-start.5 = (f32[4,8,2048]{2,1,0:T(8,128)S(1)}, f32[4,8,2048]{2,1,0:T(8,128)S(1)}, u32[]{:S(2)}, u32[]{:S(2)}) collective-permute-start(f32[4,8,2048]{2,1,0:T(8,128)S(1)} %pad_maximum_fusion), channel_id=1, source_target_pairs={{0,8},{1,9},{2,10},{3,11},{4,12},{5,13},{6,14},{7,15},{8,0},{9,1},... | collective-permute-start | bytes 786440 | tf_op jit(solution)/shard_map/ppermute | solution.py:305
  56.5 12.1 %collective-permute-start.6 = (f32[4,8,2048]{2,1,0:T(8,128)S(1)}, f32[4,8,2048]{2,1,0:T(8,128)S(1)}, u32[]{:S(2)}, u32[]{:S(2)}) collective-permute-start(f32[4,8,2048]{2,1,0:T(8,128)S(1)} %pad_maximum_fusion), channel_id=1, source_target_pairs={{0,12},{1,13},{2,14},{3,15},{4,0},{5,1},{6,2},{7,3},{8,4},{9,5},{1... | collective-permute-start | bytes 786440 | tf_op jit(solution)/shard_map/ppermute | solution.py:305
  68.6 6.7 %copy-start.1 = (f32[16,8,2048]{2,1,0:T(8,128)}, f32[16,8,2048]{2,1,0:T(8,128)S(1)}, u32[]{:S(2)}) copy-start(f32[16,8,2048]{2,1,0:T(8,128)S(1)} %constant_dynamic-update-slice_fusion.far_mine) | copy-start | bytes 3145732
  68.6 6.7 %collective-permute-start.7 = (f32[16,8,2048]{2,1,0:T(8,128)S(1)}, f32[16,8,2048]{2,1,0:T(8,128)S(1)}, u32[]{:S(2)}, u32[]{:S(2)}) collective-permute-start(f32[16,8,2048]{2,1,0:T(8,128)S(1)} %constant_dynamic-update-slice_fusion.far_mine), channel_id=1, source_target_pairs={{0,1},{1,0},{2,3},{3,2},{4,5},{5,4},{6,7},{7,6},{8,9},{9,8},{10,11... | collective-permute-start | bytes 3145736 | tf_op jit(solution)/shard_map/ppermute | solution.py:306
  75.2 1.1 copy-start.2
  98.7 37.4 %all-to-all-start.1 = ((f32[32,4,8,128]{3,2,1,0:T(8,128)}), f32[32,4,8,128]{3,2,1,0:T(8,128)S(1)}, u32[]{:S(2)}, u32[]{:S(2)}) async-start(f32[32,4,8,128]{3,2,1,0:T(8,128)} %bitcast.19), calls=%async_computation.2 | async-start | bytes 1048576 | tf_op jit(solution)/shard_map/all_to_all | solution.py:58
  106.8 3.6 %collective-permute-start.8 = (f32[4,9,8,128]{3,2,1,0:T(8,128)S(1)}, f32[4,9,8,128]{3,2,1,0:T(8,128)S(1)}, u32[]{:S(2)}, u32[]{:S(2)}) collective-permute-start(f32[4,9,8,128]{3,2,1,0:T(8,128)S(1)} %dynamic-slice_bitcast_fusion), channel_id=1, source_target_pairs={{0,1},{1,0},{2,3},{3,2},{4,5},{5,4},{6,7},{7,6},{8,9},{9,8},{10,11... | collective-permute-start | bytes 442376 | tf_op jit(solution)/shard_map/ppermute | solution.py:376
  110.3 8.4 %collective-permute-start.9 = (f32[4,9,8,128]{3,2,1,0:T(8,128)S(1)}, f32[4,9,8,128]{3,2,1,0:T(8,128)S(1)}, u32[]{:S(2)}, u32[]{:S(2)}) collective-permute-start(f32[4,9,8,128]{3,2,1,0:T(8,128)S(1)} %bitcast_add_fusion), channel_id=1, source_target_pairs={{0,4},{1,5},{2,6},{3,7},{4,0},{5,1},{6,2},{7,3},{8,12},{9,13},{10,... | collective-permute-start | bytes 442376 | tf_op jit(solution)/shard_map/ppermute | solution.py:380
  118.8 9.7 %collective-permute-start.10 = (f32[4,9,8,128]{3,2,1,0:T(8,128)S(1)}, f32[4,9,8,128]{3,2,1,0:T(8,128)S(1)}, u32[]{:S(2)}, u32[]{:S(2)}) collective-permute-start(f32[4,9,8,128]{3,2,1,0:T(8,128)S(1)} %add.38), channel_id=1, source_target_pairs={{0,8},{1,9},{2,10},{3,11},{4,12},{5,13},{6,14},{7,15},{8,0},{9,1},... | collective-permute-start | bytes 442376 | tf_op jit(solution)/shard_map/ppermute | solution.py:380
  136.1 3.3 %copy-start = (f32[32,4,8,128]{3,2,1,0:T(8,128)}, f32[32,4,8,128]{3,2,1,0:T(8,128)S(1)}, u32[]{:S(2)}) copy-start(f32[32,4,8,128]{3,2,1,0:T(8,128)S(1)} %all-to-all-done.1.tiles) | copy-start | bytes 1572868
  136.1 8.2 %all-to-all-start.2 = ((f32[4,9,8,128]{3,2,1,0:T(8,128)}), f32[4,9,8,128]{3,2,1,0:T(8,128)S(1)}, u32[]{:S(2)}, u32[]{:S(2)}) async-start(f32[4,9,8,128]{3,2,1,0:T(8,128)} %add.39), calls=%async_computation.3 | async-start | bytes 294912 | tf_op jit(solution)/shard_map/all_to_all | solution.py:58
  144.4 10.4 %all-to-all-start.3 = ((f32[4,32,8,128]{3,2,1,0:T(8,128)}), f32[4,32,8,128]{3,2,1,0:T(8,128)S(1)}, u32[]{:S(2)}, u32[]{:S(2)}) async-start(f32[4,32,8,128]{3,2,1,0:T(8,128)} %bitcast.46), calls=%async_computation.4 | async-start | bytes 1048576 | tf_op jit(solution)/shard_map/all_to_all | solution.py:58
  207.1 7.2 %collective-permute-start.11 = (f32[128,256]{1,0:T(8,128)S(1)}, f32[128,256]{1,0:T(8,128)S(1)}, u32[]{:S(2)}, u32[]{:S(2)}) collective-permute-start(f32[128,256]{1,0:T(8,128)S(1)} %bitcast.44), channel_id=1, source_target_pairs={{0,1},{1,0},{2,3},{3,2},{4,5},{5,4},{6,7},{7,6},{8,9},{9,8},{10,11... | collective-permute-start | bytes 393224 | tf_op jit(solution)/shard_map/ppermute | solution.py:404
Sparse Core Ops, SparseCore 0:
  11.1 36.4 all-gather.2
  98.8 43.3 reduce-scatter.1

commit v8 on v6

--- a/solution.py
+++ b/solution.py
@@ -370,7 +370,7 @@
     part = lax.dynamic_index_in_dim(tables, c, 0, False) + lax.ppermute(
         lax.dynamic_index_in_dim(tables, 1 - c, 0, False), "dp", SWAP_CORE
     )
-    for bit in (1, 2):
+    for bit in (2, 1):
         part = part + lax.ppermute(part, "dp", swap_y(bit))
     part, tokens_there = lax.optimization_barrier((part, tokens_there))
     part = jnp.sum(exchange(part, "tm", X_GROUPS), axis=0)

time: 223 us -> 222 us (level)
  no operation moved by 1% of the time
where the time goes in v8:
time: 222 us; the launch traced here: 221 us
  starting transfers between devices  73.7 us (33%)
  blocking collectives  50.7 us (23%)
  waiting for transfers between devices  49.3 us (22%)
  Pallas kernels  24.7 us (11%)
  between operations  15.2 us (7%)
  local copies, waits for them, and re-layouts  4.08 us (2%)
  other arithmetic  3.49 us (2%)
    all_to_all x3, blocking collectives, exchange(): lax.all_to_all(value, axis, 0, 0, axis_index_groups=groups, tiled=True)  50.7 us
    pallas_call x5, Pallas kernels, call(): pl.pallas_call(kernel, out_shape=outs, in_specs=[smem] * len(scalars) + [...  24.7 us
    all_to_all x4, starting transfers between devices, exchange(): lax.all_to_all(value, axis, 0, 0, axis_index_groups=groups, tiled=True)  22.5 us
    all_to_all x4, waiting for transfers between devices, exchange(): lax.all_to_all(value, axis, 0, 0, axis_index_groups=groups, tiled=True)  19.7 us
    ppermute x1, starting transfers between devices, shards(): quarter = lax.ppermute(quarter, 'dp', SWAP_ZH)  15.4 us
    ppermute x2, waiting for transfers between devices, shards(): part = part + lax.ppermute(part, 'dp', swap_y(bit))  14.2 us
    ppermute x3, starting transfers between devices, far_weights(): lax.ppermute(quarter, 'tm', turn_x(i))  10.7 us
    ppermute x3, waiting for transfers between devices, far_weights(): lax.ppermute(row, 'dp', turn_y(i))  10.1 us
  transfers between devices with their start and end apart: 18, of which 11 were waited for; matrix products, arithmetic and copies ran while one was open for 2% of the time, Pallas kernels for 4%

profile of v8, /device:TPU:25, one launch (start us, length us, event | category | flops | bytes accessed | tf_op | source)
XLA Modules:
  0.0 221.2 jit_solution(3503713962533158099)
XLA Ops:
  8.5 2.5 %front.1 = (f32[2080,128]{1,0:T(8,128)}, f32[32,2048]{1,0:T(8,128)}, f32[8,2048]{1,0:T(8,128)}) custom-call(s32[4]{0:T(128)} %pad_add_fusion.place, s32[1]{0:T(128)} %bitcast.38.action, f32[128,512]{1,0:T(8,128)} %act_table.1, f32[256,512]{1,0:T(8,128)} %bitcast.49, f32[256,512]{1,0:T(8,128)} %bitcast.50, f32[32,1536]{1,0:T(8,128)} %w_qkv.1, f32[32,512]{1,0:T(8,128)} %w_out.1), custom_call_target="tpu_custom_call" | custom-call | tf_op jit(solution)/shard_map/front/pallas_call | solution.py:279
  11.0 15.4 %collective-permute-start = (f32[8,2048]{1,0:T(8,128)}, f32[8,2048]{1,0:T(8,128)S(1)}, u32[]{:S(2)}, u32[]{:S(2)}) collective-permute-start(f32[8,2048]{1,0:T(8,128)} %get-tuple-element.21), channel_id=1, source_target_pairs={{0,2},{1,3},{2,0},{3,1},{4,6},{5,7},{6,4},{7,5},{8,10},{9,11},{10,... | collective-permute-start | bytes 196616 | tf_op jit(solution)/shard_map/ppermute | solution.py:319
  26.5 7.6 %all-to-all-start = ((f32[32,65,1,128]{3,2,1,0:T(1,128)}), f32[32,65,1,128]{3,2,1,0:T(1,128)S(1)}, u32[]{:S(2)}, u32[]{:S(2)}) async-start(f32[32,65,1,128]{3,2,1,0:T(1,128)} %bitcast.41), calls=%async_computation | async-start | bytes 2129920 | tf_op jit(solution)/shard_map/all_to_all | solution.py:58
  36.2 3.3 %collective-permute-start.1 = (f32[8,2048]{1,0:T(8,128)}, f32[8,2048]{1,0:T(8,128)S(1)}, u32[]{:S(2)}, u32[]{:S(2)}) collective-permute-start(f32[8,2048]{1,0:T(8,128)} %swapped.1), channel_id=1, source_target_pairs={{0,128},{16,144},{32,160},{48,176},{64,192},{80,208},{96,224},{112... | collective-permute-start | bytes 196616 | tf_op jit(solution)/shard_map/ppermute | solution.py:297
  39.5 4.3 %collective-permute-start.2 = (f32[8,2048]{1,0:T(8,128)}, f32[8,2048]{1,0:T(8,128)S(1)}, u32[]{:S(2)}, u32[]{:S(2)}) collective-permute-start(f32[8,2048]{1,0:T(8,128)} %swapped.1), channel_id=1, source_target_pairs={{0,256},{16,272},{32,288},{48,304},{64,320},{80,336},{96,352},{112... | collective-permute-start | bytes 196616 | tf_op jit(solution)/shard_map/ppermute | solution.py:297
  43.9 3.1 %collective-permute-start.3 = (f32[8,2048]{1,0:T(8,128)}, f32[8,2048]{1,0:T(8,128)S(1)}, u32[]{:S(2)}, u32[]{:S(2)}) collective-permute-start(f32[8,2048]{1,0:T(8,128)} %swapped.1), channel_id=1, source_target_pairs={{0,384},{16,400},{32,416},{48,432},{64,448},{80,464},{96,480},{112... | collective-permute-start | bytes 196616 | tf_op jit(solution)/shard_map/ppermute | solution.py:297
  46.9 2.5 %collective-permute-done.3 = f32[8,2048]{1,0:T(8,128)S(1)} collective-permute-done((f32[8,2048]{1,0:T(8,128)}, f32[8,2048]{1,0:T(8,128)S(1)}, u32[]{:S(2)}, u32[]{:S(2)}) %collective-permute-start.3) | collective-permute-done | bytes 65568 | tf_op jit(solution)/shard_map/ppermute | solution.py:297
  50.4 1.9 collective-permute-start.4
  52.3 4.1 %collective-permute-start.5 = (f32[4,8,2048]{2,1,0:T(8,128)S(1)}, f32[4,8,2048]{2,1,0:T(8,128)S(1)}, u32[]{:S(2)}, u32[]{:S(2)}) collective-permute-start(f32[4,8,2048]{2,1,0:T(8,128)S(1)} %pad_maximum_fusion), channel_id=1, source_target_pairs={{0,8},{1,9},{2,10},{3,11},{4,12},{5,13},{6,14},{7,15},{8,0},{9,1},... | collective-permute-start | bytes 786440 | tf_op jit(solution)/shard_map/ppermute | solution.py:299
  56.5 1.9 collective-permute-start.6
  58.5 2.8 %collective-permute-done.5 = f32[4,8,2048]{2,1,0:T(8,128)S(1)} collective-permute-done((f32[4,8,2048]{2,1,0:T(8,128)S(1)}, f32[4,8,2048]{2,1,0:T(8,128)S(1)}, u32[]{:S(2)}, u32[]{:S(2)}) %collective-permute-start.5) | collective-permute-done | bytes 262176 | tf_op jit(solution)/shard_map/ppermute | solution.py:299
  61.2 7.3 %collective-permute-done.6 = f32[4,8,2048]{2,1,0:T(8,128)S(1)} collective-permute-done((f32[4,8,2048]{2,1,0:T(8,128)S(1)}, f32[4,8,2048]{2,1,0:T(8,128)S(1)}, u32[]{:S(2)}, u32[]{:S(2)}) %collective-permute-start.6) | collective-permute-done | bytes 262176 | tf_op jit(solution)/shard_map/ppermute | solution.py:299
  68.6 4.4 %collective-permute-start.7 = (f32[16,8,2048]{2,1,0:T(8,128)S(1)}, f32[16,8,2048]{2,1,0:T(8,128)S(1)}, u32[]{:S(2)}, u32[]{:S(2)}) collective-permute-start(f32[16,8,2048]{2,1,0:T(8,128)S(1)} %constant_dynamic-update-slice_fusion.far_mine), channel_id=1, source_target_pairs={{0,1},{1,0},{2,3},{3,2},{4,5},{5,4},{6,7},{7,6},{8,9},{9,8},{10,11... | collective-permute-start | bytes 3145736 | tf_op jit(solution)/shard_map/ppermute | solution.py:300
  76.3 5.0 %weights.1 = (bf16[512,2048]{1,0:T(8,128)(2,1)}, bf16[512,2048]{1,0:T(8,128)(2,1)}) custom-call(s32[4]{0:T(128)} %pad_add_fusion.place, f32[8,32,2048]{2,1,0:T(8,128)} %bitcast.40, f32[16,8,2048]{2,1,0:T(8,128)} %copy-done.1, f32[16,8,2048]{2,1,0:T(8,128)} %copy-done.2), custom_call_target="tpu_custom_call" | custom-call | tf_op jit(solution)/shard_map/weights/pallas_call | solution.py:279
  81.3 3.8 %all-to-all-done = f32[32,65,1,128]{3,2,1,0:T(1,128)S(1)} async-done(((f32[32,65,1,128]{3,2,1,0:T(1,128)}), f32[32,65,1,128]{3,2,1,0:T(1,128)S(1)}, u32[]{:S(2)}, u32[]{:S(2)}) %all-to-all-start) | async-done | bytes 1064992 | tf_op jit(solution)/shard_map/all_to_all | solution.py:58
  85.1 13.9 %sublayer.1 = (f32[8,4,32,8,128]{4,3,2,1,0:T(8,128)}, f32[1024,128]{1,0:T(8,128)}, f32[2,4,9,8,128]{4,3,2,1,0:T(8,128)S(1)}) custom-call(f32[2080,128]{1,0:T(8,128)S(1)} %bitcast.39, f32[144,128]{1,0:T(8,128)S(1)} %maximum_maximum_fusion.extras_in, bf16[512,2048]{1,0:T(8,128)(2,1)} %get-tuple-element.25.high_in, bf16[512,2048]{1,0:T(8,128)(2,1)} %get-tuple-element.26.low_in), custom_call_target="tpu_custom_call" | custom-call | tf_op jit(solution)/shard_map/sublayer/pallas_call | solution.py:279
  99.1 8.0 %all-to-all-start.1 = ((f32[32,4,8,128]{3,2,1,0:T(8,128)}), f32[32,4,8,128]{3,2,1,0:T(8,128)S(1)}, u32[]{:S(2)}, u32[]{:S(2)}) async-start(f32[32,4,8,128]{3,2,1,0:T(8,128)} %bitcast.19), calls=%async_computation.2 | async-start | bytes 1048576 | tf_op jit(solution)/shard_map/all_to_all | solution.py:58
  107.1 2.6 %collective-permute-start.8 = (f32[4,9,8,128]{3,2,1,0:T(8,128)S(1)}, f32[4,9,8,128]{3,2,1,0:T(8,128)S(1)}, u32[]{:S(2)}, u32[]{:S(2)}) collective-permute-start(f32[4,9,8,128]{3,2,1,0:T(8,128)S(1)} %dynamic-slice_bitcast_fusion), channel_id=1, source_target_pairs={{0,1},{1,0},{2,3},{3,2},{4,5},{5,4},{6,7},{7,6},{8,9},{9,8},{10,11... | collective-permute-start | bytes 442376 | tf_op jit(solution)/shard_map/ppermute | solution.py:370
  110.7 3.0 %collective-permute-start.9 = (f32[4,9,8,128]{3,2,1,0:T(8,128)S(1)}, f32[4,9,8,128]{3,2,1,0:T(8,128)S(1)}, u32[]{:S(2)}, u32[]{:S(2)}) collective-permute-start(f32[4,9,8,128]{3,2,1,0:T(8,128)S(1)} %bitcast_add_fusion), channel_id=1, source_target_pairs={{0,8},{1,9},{2,10},{3,11},{4,12},{5,13},{6,14},{7,15},{8,0},{9,1},... | collective-permute-start | bytes 442376 | tf_op jit(solution)/shard_map/ppermute | solution.py:374
  113.7 7.6 %collective-permute-done.9 = f32[4,9,8,128]{3,2,1,0:T(8,128)S(1)} collective-permute-done((f32[4,9,8,128]{3,2,1,0:T(8,128)S(1)}, f32[4,9,8,128]{3,2,1,0:T(8,128)S(1)}, u32[]{:S(2)}, u32[]{:S(2)}) %collective-permute-start.9) | collective-permute-done | bytes 147488 | tf_op jit(solution)/shard_map/ppermute | solution.py:374
  121.3 1.9 collective-permute-start.10
  123.3 6.6 %collective-permute-done.10 = f32[4,9,8,128]{3,2,1,0:T(8,128)S(1)} collective-permute-done((f32[4,9,8,128]{3,2,1,0:T(8,128)S(1)}, f32[4,9,8,128]{3,2,1,0:T(8,128)S(1)}, u32[]{:S(2)}, u32[]{:S(2)}) %collective-permute-start.10) | collective-permute-done | bytes 147488 | tf_op jit(solution)/shard_map/ppermute | solution.py:374
  130.5 5.9 %all-to-all-done.1.tiles = f32[32,4,8,128]{3,2,1,0:T(8,128)S(1)} async-done(((f32[32,4,8,128]{3,2,1,0:T(8,128)}), f32[32,4,8,128]{3,2,1,0:T(8,128)S(1)}, u32[]{:S(2)}, u32[]{:S(2)}) %all-to-all-start.1) | async-done | bytes 524320 | tf_op jit(solution)/shard_map/all_to_all | solution.py:58
  136.5 3.3 %all-to-all-start.2 = ((f32[4,9,8,128]{3,2,1,0:T(8,128)}), f32[4,9,8,128]{3,2,1,0:T(8,128)S(1)}, u32[]{:S(2)}, u32[]{:S(2)}) async-start(f32[4,9,8,128]{3,2,1,0:T(8,128)} %add.39), calls=%async_computation.3 | async-start | bytes 294912 | tf_op jit(solution)/shard_map/all_to_all | solution.py:58
  139.8 1.9 unpack.1
  141.7 3.0 %all-to-all-done.2 = f32[4,9,8,128]{3,2,1,0:T(8,128)S(1)} async-done(((f32[4,9,8,128]{3,2,1,0:T(8,128)}), f32[4,9,8,128]{3,2,1,0:T(8,128)S(1)}, u32[]{:S(2)}, u32[]{:S(2)}) %all-to-all-start.2) | async-done | bytes 147488 | tf_op jit(solution)/shard_map/all_to_all | solution.py:58
  144.7 3.5 %all-to-all-start.3 = ((f32[4,32,8,128]{3,2,1,0:T(8,128)}), f32[4,32,8,128]{3,2,1,0:T(8,128)S(1)}, u32[]{:S(2)}, u32[]{:S(2)}) async-start(f32[4,32,8,128]{3,2,1,0:T(8,128)} %bitcast.46), calls=%async_computation.4 | async-start | bytes 1048576 | tf_op jit(solution)/shard_map/all_to_all | solution.py:58
  148.2 6.9 %all-to-all-done.3 = f32[4,32,8,128]{3,2,1,0:T(8,128)S(1)} async-done(((f32[4,32,8,128]{3,2,1,0:T(8,128)}), f32[4,32,8,128]{3,2,1,0:T(8,128)S(1)}, u32[]{:S(2)}, u32[]{:S(2)}) %all-to-all-start.3) | async-done | bytes 524320 | tf_op jit(solution)/shard_map/all_to_all | solution.py:58
  155.4 23.0 %all_to_all.35 = f32[16,25,1,128]{3,2,1,0:T(1,128)S(1)} all-to-all(f32[16,25,1,128]{3,2,1,0:T(1,128)S(1)} %pad_maximum_fusion.1), channel_id=1, replica_groups={{0,16,32,48,64,80,96,112,2,18,34,50,66,82,98,114},{1,17,33,49,65,81,97,..., dimensions={0} | all-to-all | bytes 409600 | tf_op jit(solution)/shard_map/all_to_all | solution.py:58
  178.6 19.1 %all_to_all.36 = f32[8,25,1,128]{3,2,1,0:T(1,128)S(1)} all-to-all(f32[8,25,1,128]{3,2,1,0:T(1,128)S(1)} %broadcast_in_dim.22), channel_id=1, replica_groups={{0,16,32,48,64,80,96,112},{128,144,160,176,192,208,224,240},{256,272,28..., dimensions={0} | all-to-all | bytes 204800 | tf_op jit(solution)/shard_map/all_to_all | solution.py:58
  197.7 8.6 %all_to_all.37 = f32[4,8,3,8,128]{4,3,2,1,0:T(8,128)S(1)} all-to-all(f32[4,8,3,8,128]{4,3,2,1,0:T(8,128)S(1)} %broadcast_in_dim.23), channel_id=1, replica_groups={{0,128,256,384},{16,144,272,400},{32,160,288,416},{48,176,304,432},{64,..., dimensions={0} | all-to-all | bytes 786432 | tf_op jit(solution)/shard_map/all_to_all | solution.py:58
  206.3 5.2 %collective-permute-start.11 = (f32[128,256]{1,0:T(8,128)S(1)}, f32[128,256]{1,0:T(8,128)S(1)}, u32[]{:S(2)}, u32[]{:S(2)}) collective-permute-start(f32[128,256]{1,0:T(8,128)S(1)} %bitcast.44), channel_id=1, source_target_pairs={{0,1},{1,0},{2,3},{3,2},{4,5},{5,4},{6,7},{7,6},{8,9},{9,8},{10,11... | collective-permute-start | bytes 393224 | tf_op jit(solution)/shard_map/ppermute | solution.py:398
  (66 shorter events, 12.0 us)
Async XLA Ops:
  7.2 43.2 %all-gather.3.cloned.1.call-start = ((), (), s32[]{:S(2)}) async-start(), calls=%async_computation.9 | async-start | bytes 2359296 | tf_op jit(solution)/shard_map/all_gather | solution.py:318
  11.0 23.1 %collective-permute-start = (f32[8,2048]{1,0:T(8,128)}, f32[8,2048]{1,0:T(8,128)S(1)}, u32[]{:S(2)}, u32[]{:S(2)}) collective-permute-start(f32[8,2048]{1,0:T(8,128)} %get-tuple-element.21), channel_id=1, source_target_pairs={{0,2},{1,3},{2,0},{3,1},{4,6},{5,7},{6,4},{7,5},{8,10},{9,11},{10,... | collective-permute-start | bytes 196616 | tf_op jit(solution)/shard_map/ppermute | solution.py:319
  26.5 58.6 %all-to-all-start = ((f32[32,65,1,128]{3,2,1,0:T(1,128)}), f32[32,65,1,128]{3,2,1,0:T(1,128)S(1)}, u32[]{:S(2)}, u32[]{:S(2)}) async-start(f32[32,65,1,128]{3,2,1,0:T(1,128)} %bitcast.41), calls=%async_computation | async-start | bytes 2129920 | tf_op jit(solution)/shard_map/all_to_all | solution.py:58
  34.1 110.7 %reduce-scatter.2.cloned.1.call-start = ((), (), s32[]{:S(2)}) async-start(), calls=%async_computation.8 | async-start | bytes 4718592 | tf_op jit(solution)/shard_map/reduce_scatter | solution.py:367
  34.1 0.6 copy-start.5
  36.2 36.7 %copy-start.6 = (s32[1,32]{1,0:T(1,128)S(1)}, s32[1,32]{1,0:T(1,128)}, u32[]{:S(2)}) copy-start(s32[1,32]{1,0:T(1,128)} %param.11) | copy-start | bytes 388
  36.2 36.9 %copy-start.4 = (f32[8]{0:T(128)S(1)}, f32[8]{0:T(128)}, u32[]{:S(2)}) copy-start(f32[8]{0:T(128)} %param.16) | copy-start | bytes 100
  36.2 37.1 %copy-start.3 = (f32[512]{0:T(512)S(1)}, f32[512]{0:T(512)}, u32[]{:S(2)}) copy-start(f32[512]{0:T(512)} %param.13) | copy-start | bytes 6148
  36.2 10.7 %collective-permute-start.1 = (f32[8,2048]{1,0:T(8,128)}, f32[8,2048]{1,0:T(8,128)S(1)}, u32[]{:S(2)}, u32[]{:S(2)}) collective-permute-start(f32[8,2048]{1,0:T(8,128)} %swapped.1), channel_id=1, source_target_pairs={{0,128},{16,144},{32,160},{48,176},{64,192},{80,208},{96,224},{112... | collective-permute-start | bytes 196616 | tf_op jit(solution)/shard_map/ppermute | solution.py:297
  39.5 7.4 %collective-permute-start.2 = (f32[8,2048]{1,0:T(8,128)}, f32[8,2048]{1,0:T(8,128)S(1)}, u32[]{:S(2)}, u32[]{:S(2)}) collective-permute-start(f32[8,2048]{1,0:T(8,128)} %swapped.1), channel_id=1, source_target_pairs={{0,256},{16,272},{32,288},{48,304},{64,320},{80,336},{96,352},{112... | collective-permute-start | bytes 196616 | tf_op jit(solution)/shard_map/ppermute | solution.py:297
  43.9 5.6 %collective-permute-start.3 = (f32[8,2048]{1,0:T(8,128)}, f32[8,2048]{1,0:T(8,128)S(1)}, u32[]{:S(2)}, u32[]{:S(2)}) collective-permute-start(f32[8,2048]{1,0:T(8,128)} %swapped.1), channel_id=1, source_target_pairs={{0,384},{16,400},{32,416},{48,432},{64,448},{80,464},{96,480},{112... | collective-permute-start | bytes 196616 | tf_op jit(solution)/shard_map/ppermute | solution.py:297
  50.4 8.0 %collective-permute-start.4 = (f32[4,8,2048]{2,1,0:T(8,128)S(1)}, f32[4,8,2048]{2,1,0:T(8,128)S(1)}, u32[]{:S(2)}, u32[]{:S(2)}) collective-permute-start(f32[4,8,2048]{2,1,0:T(8,128)S(1)} %pad_maximum_fusion), channel_id=1, source_target_pairs={{0,4},{1,5},{2,6},{3,7},{4,8},{5,9},{6,10},{7,11},{8,12},{9,13},{1... | collective-permute-start | bytes 786440 | tf_op jit(solution)/shard_map/ppermute | solution.py:299
  52.3 8.9 %collective-permute-start.5 = (f32[4,8,2048]{2,1,0:T(8,128)S(1)}, f32[4,8,2048]{2,1,0:T(8,128)S(1)}, u32[]{:S(2)}, u32[]{:S(2)}) collective-permute-start(f32[4,8,2048]{2,1,0:T(8,128)S(1)} %pad_maximum_fusion), channel_id=1, source_target_pairs={{0,8},{1,9},{2,10},{3,11},{4,12},{5,13},{6,14},{7,15},{8,0},{9,1},... | collective-permute-start | bytes 786440 | tf_op jit(solution)/shard_map/ppermute | solution.py:299
  56.5 12.1 %collective-permute-start.6 = (f32[4,8,2048]{2,1,0:T(8,128)S(1)}, f32[4,8,2048]{2,1,0:T(8,128)S(1)}, u32[]{:S(2)}, u32[]{:S(2)}) collective-permute-start(f32[4,8,2048]{2,1,0:T(8,128)S(1)} %pad_maximum_fusion), channel_id=1, source_target_pairs={{0,12},{1,13},{2,14},{3,15},{4,0},{5,1},{6,2},{7,3},{8,4},{9,5},{1... | collective-permute-start | bytes 786440 | tf_op jit(solution)/shard_map/ppermute | solution.py:299
  68.6 6.7 %copy-start.1 = (f32[16,8,2048]{2,1,0:T(8,128)}, f32[16,8,2048]{2,1,0:T(8,128)S(1)}, u32[]{:S(2)}) copy-start(f32[16,8,2048]{2,1,0:T(8,128)S(1)} %constant_dynamic-update-slice_fusion.far_mine) | copy-start | bytes 3145732
  68.6 6.7 %collective-permute-start.7 = (f32[16,8,2048]{2,1,0:T(8,128)S(1)}, f32[16,8,2048]{2,1,0:T(8,128)S(1)}, u32[]{:S(2)}, u32[]{:S(2)}) collective-permute-start(f32[16,8,2048]{2,1,0:T(8,128)S(1)} %constant_dynamic-update-slice_fusion.far_mine), channel_id=1, source_target_pairs={{0,1},{1,0},{2,3},{3,2},{4,5},{5,4},{6,7},{7,6},{8,9},{9,8},{10,11... | collective-permute-start | bytes 3145736 | tf_op jit(solution)/shard_map/ppermute | solution.py:300
  75.2 1.1 copy-start.2
  99.1 37.4 %all-to-all-start.1 = ((f32[32,4,8,128]{3,2,1,0:T(8,128)}), f32[32,4,8,128]{3,2,1,0:T(8,128)S(1)}, u32[]{:S(2)}, u32[]{:S(2)}) async-start(f32[32,4,8,128]{3,2,1,0:T(8,128)} %bitcast.19), calls=%async_computation.2 | async-start | bytes 1048576 | tf_op jit(solution)/shard_map/all_to_all | solution.py:58
  107.1 3.6 %collective-permute-start.8 = (f32[4,9,8,128]{3,2,1,0:T(8,128)S(1)}, f32[4,9,8,128]{3,2,1,0:T(8,128)S(1)}, u32[]{:S(2)}, u32[]{:S(2)}) collective-permute-start(f32[4,9,8,128]{3,2,1,0:T(8,128)S(1)} %dynamic-slice_bitcast_fusion), channel_id=1, source_target_pairs={{0,1},{1,0},{2,3},{3,2},{4,5},{5,4},{6,7},{7,6},{8,9},{9,8},{10,11... | collective-permute-start | bytes 442376 | tf_op jit(solution)/shard_map/ppermute | solution.py:370
  110.7 10.6 %collective-permute-start.9 = (f32[4,9,8,128]{3,2,1,0:T(8,128)S(1)}, f32[4,9,8,128]{3,2,1,0:T(8,128)S(1)}, u32[]{:S(2)}, u32[]{:S(2)}) collective-permute-start(f32[4,9,8,128]{3,2,1,0:T(8,128)S(1)} %bitcast_add_fusion), channel_id=1, source_target_pairs={{0,8},{1,9},{2,10},{3,11},{4,12},{5,13},{6,14},{7,15},{8,0},{9,1},... | collective-permute-start | bytes 442376 | tf_op jit(solution)/shard_map/ppermute | solution.py:374
  121.3 8.5 %collective-permute-start.10 = (f32[4,9,8,128]{3,2,1,0:T(8,128)S(1)}, f32[4,9,8,128]{3,2,1,0:T(8,128)S(1)}, u32[]{:S(2)}, u32[]{:S(2)}) collective-permute-start(f32[4,9,8,128]{3,2,1,0:T(8,128)S(1)} %add.38), channel_id=1, source_target_pairs={{0,4},{1,5},{2,6},{3,7},{4,0},{5,1},{6,2},{7,3},{8,12},{9,13},{10,... | collective-permute-start | bytes 442376 | tf_op jit(solution)/shard_map/ppermute | solution.py:374
  136.5 3.3 %copy-start = (f32[32,4,8,128]{3,2,1,0:T(8,128)}, f32[32,4,8,128]{3,2,1,0:T(8,128)S(1)}, u32[]{:S(2)}) copy-start(f32[32,4,8,128]{3,2,1,0:T(8,128)S(1)} %all-to-all-done.1.tiles) | copy-start | bytes 1572868
  136.5 8.2 %all-to-all-start.2 = ((f32[4,9,8,128]{3,2,1,0:T(8,128)}), f32[4,9,8,128]{3,2,1,0:T(8,128)S(1)}, u32[]{:S(2)}, u32[]{:S(2)}) async-start(f32[4,9,8,128]{3,2,1,0:T(8,128)} %add.39), calls=%async_computation.3 | async-start | bytes 294912 | tf_op jit(solution)/shard_map/all_to_all | solution.py:58
  144.7 10.4 %all-to-all-start.3 = ((f32[4,32,8,128]{3,2,1,0:T(8,128)}), f32[4,32,8,128]{3,2,1,0:T(8,128)S(1)}, u32[]{:S(2)}, u32[]{:S(2)}) async-start(f32[4,32,8,128]{3,2,1,0:T(8,128)} %bitcast.46), calls=%async_computation.4 | async-start | bytes 1048576 | tf_op jit(solution)/shard_map/all_to_all | solution.py:58
  206.3 7.3 %collective-permute-start.11 = (f32[128,256]{1,0:T(8,128)S(1)}, f32[128,256]{1,0:T(8,128)S(1)}, u32[]{:S(2)}, u32[]{:S(2)}) collective-permute-start(f32[128,256]{1,0:T(8,128)S(1)} %bitcast.44), channel_id=1, source_target_pairs={{0,1},{1,0},{2,3},{3,2},{4,5},{5,4},{6,7},{7,6},{8,9},{9,8},{10,11... | collective-permute-start | bytes 393224 | tf_op jit(solution)/shard_map/ppermute | solution.py:398
Sparse Core Ops, SparseCore 0:
  11.1 36.4 all-gather.2
  99.2 43.1 reduce-scatter.1
